TPU v7x, 128 devices: a whole 4x4x4 slice. The times are simulated.
128 devices in a mesh: tm: 2 (over x_lo), rows: 64 (over z, y, x_hi, core), roll: 1.
Axes of the slice: x: 4 (x_hi: 2, x_lo: 2; x = x_hi * 2 + x_lo), y: 4, z: 4, core: 2. Of those that a mesh axis runs over, the one named last changes fastest.
Arguments:
- frames_in: bfloat16 [8, 256, 160, 192], P('tm', 'rows', 'roll'), may hold values from -6 to 6
- gain_one: float32 [192], replicated, may hold values from 0.25 to 1.75
- conv_one: bfloat16 [3, 3, 3, 192, 192], replicated, may hold values from -0.078125 to 0.078125
- bias_one: float32 [192], replicated, may hold values from -3 to 3
- gain_two: float32 [192], replicated, may hold values from 0.25 to 1.75
- conv_two: bfloat16 [3, 3, 3, 192, 192], replicated, may hold values from -0.078125 to 0.078125
- bias_two: float32 [192], replicated, may hold values from -3 to 3
Outputs:
- frames_out: bfloat16 [8, 256, 160, 192], P('tm', 'rows', 'roll')
All inputs are finite; a program needn't handle non-finite values.
Results may differ from a plain program's by a relative error of at most 0.0034.
Values may be sent and summed in bfloat16 or wider, within the bound.
No kernel may reach another device: no remote copies, remote signals or barrier semaphores. Data moves between devices by JAX's collectives and lax.ppermute only.
A program may use at most 256 MiB of HBM per device.

v0:
```python
import jax
import jax.numpy as jnp
from jax import lax
from jax.experimental import pallas as pl
from jax.experimental.pallas import tpu as pltpu
from jax.sharding import PartitionSpec as P

BF = jnp.bfloat16
F32 = jnp.float32
C = 192
W = 160
S = 16
J = W // S
E = W + 2 * S
D = 240
MB = 2**20


def spread(rows, shift):
    n = lax.broadcasted_iota(jnp.int32, (rows, W), 0)
    c = lax.broadcasted_iota(jnp.int32, (rows, W), 1)
    return jnp.where((n & (S - 1)) * J + (n >> 4) - shift == c, 1.0, 0.0).astype(BF)


def gather():
    c = lax.broadcasted_iota(jnp.int32, (W, W), 0)
    n = lax.broadcasted_iota(jnp.int32, (W, W), 1)
    return jnp.where((n & (S - 1)) * J + (n >> 4) == c, 1.0, 0.0).astype(BF)


def flip(n, par):
    return n + par * (3 - 2 * n)


def act(v, gain):
    power = jnp.mean(v * v, axis=-1, keepdims=True)
    h = v * lax.rsqrt(power + 1e-06) * (gain * 0.5)
    return h + h * jnp.tanh(h)


def pack(v):
    hi = v[:, 128:]
    return jnp.concatenate([v[:, :128], jnp.concatenate([hi[:80], hi[80:]], axis=1)], axis=0)


def unpack(d):
    hi = d[W:]
    return jnp.concatenate([d[:W], jnp.concatenate([hi[:, :64], hi[:, 64:]], axis=0)], axis=1)


def put(ref, at, v):
    ref[at + (slice(S, S + W), slice(0, C))] = v
    spot = lax.broadcasted_iota(jnp.int32, (S, C), 0)
    last = pltpu.roll(v[W - S :].astype(F32), 1, 0)
    head = pltpu.roll(v[:S].astype(F32), S - 1, 0)
    ref[at + (slice(0, S), slice(0, C))] = jnp.where(spot == 0, 0.0, last).astype(BF)
    ref[at + (slice(S + W, E), slice(0, C))] = jnp.where(spot == S - 1, 0.0, head).astype(BF)


def taps(src, todo, w, par):
    acc = jnp.zeros((W, C), F32)
    for t, v, a, p in todo:
        for q in range(3):
            wt = w[a, p + par * (2 - 2 * p), q]
            acc = acc + jnp.dot(src[t, v, S * q : S * q + W, :], wt, preferred_element_type=F32)
    return acc


def here():
    r = lax.axis_index("rows")
    keep = jnp.where((r == 0) | (r == lax.axis_size("rows") - 1), 0.0, 1.0).astype(F32)
    return r % 2, keep


def prep_kernel(x_hbm, g_hbm, own_ref, b_ref, a_ref, t_ref, d_ref, x_ref, g_ref, sem):
    par, _ = here()
    cg = pltpu.make_async_copy(g_hbm, g_ref, sem.at[4])
    cg.start()
    copies = [pltpu.make_async_copy(x_hbm.at[t], x_ref.at[t], sem.at[t]) for t in range(4)]
    for c in copies:
        c.start()
    m = spread(E, 1)
    cg.wait()
    g = g_ref[...]
    for t in range(4):
        copies[t].wait()
        for u in range(4):
            xp = jnp.dot(m, x_ref[t, flip(u, par)], preferred_element_type=F32)
            f = act(xp, g).astype(BF)
            own_ref[t, u] = f
            d = pack(f[S : S + W])
            if u < 2:
                b_ref[t, u] = d
                if t >= 2:
                    d_ref[t - 2, u] = d
            else:
                a_ref[t, 3 - u] = d
            if t >= 2:
                t_ref[t - 2, u] = d


def early_kernel(own_ref, a_ref, w1_ref, w2_ref, b_ref, g_ref, s_ref, o_ref, i_ref, pe_ref, pf_ref, x_ref):
    par, _ = here()
    for t in range(4):
        for u in range(4):
            x_ref[t, u] = own_ref[t, u]
        for k in range(2):
            put(x_ref, (t, 4 + k), unpack(a_ref[t, k]))
    bias = b_ref[...]
    g = g_ref[...]

    def row(k, _):
        for tau in range(2):
            acc = taps(x_ref, [(tau + a, k + p, a, p) for a in range(3) for p in range(3)], w1_ref, par)
            put(s_ref, (tau, k), act(acc + bias, g).astype(BF))
        o_ref[0, k] = taps(x_ref, [(0, k + p, 2, p) for p in range(3)], w1_ref, par)
        o_ref[1, k] = taps(x_ref, [(a - 1, k + p, a, p) for a in (1, 2) for p in range(3)], w1_ref, par)
        return 0

    lax.fori_loop(0, 4, row, 0)
    for tau in range(4):
        ok = [a for a in range(3) if tau + a >= 2]
        i_ref[tau, 0] = taps(x_ref, [(tau + a - 2, 0, a, 2) for a in ok], w1_ref, par)
        i_ref[tau, 1] = taps(x_ref, [(tau + a - 2, p - 1, a, p) for a in ok for p in (1, 2)], w1_ref, par)
    for tau in range(2):
        ok = range(2 - tau)
        pf_ref[tau, 0] = taps(s_ref, [(tau + a, 0, a, 2) for a in ok], w2_ref, par)
        pf_ref[tau, 1] = taps(s_ref, [(tau + a, p - 1, a, p) for a in ok for p in (1, 2)], w2_ref, par)
        for u in range(2):
            acc = taps(s_ref, [(tau + a, u + p, a, p) for a in ok for p in range(3)], w2_ref, par)
            pe_ref[tau, u] = pack(acc.astype(BF))


def mid_kernel(bx_ref, i_ref, pe_ref, pf_ref, w1_ref, w2_ref, b_ref, g_ref, s_ref, p_ref, x_ref):
    par, keep = here()
    for t in range(4):
        for k in range(2):
            put(x_ref, (t, 1 - k), unpack(bx_ref[t, k]))
    bias = b_ref[...]
    g = g_ref[...]
    for tau in range(2):
        acc = taps(x_ref, [(tau + a, p, a, p) for a in range(3) for p in range(2)], w1_ref, par)
        put(s_ref, (tau, 0), (act(acc + i_ref[tau + 2, 0] + bias, g) * keep).astype(BF))
        acc = taps(x_ref, [(tau + a, 1, a, 0) for a in range(3)], w1_ref, par)
        put(s_ref, (tau, 1), act(acc + i_ref[tau + 2, 1] + bias, g).astype(BF))
    for tau in range(2):
        for u in range(2):
            p_ref[tau, u + 2] = pe_ref[tau, u]
        ok = range(2 - tau)
        acc = taps(s_ref, [(tau + a, p, a, p) for a in ok for p in range(2)], w2_ref, par)
        p_ref[tau, 0] = pack((acc + pf_ref[tau, 0]).astype(BF))
        acc = taps(s_ref, [(tau + a, 1, a, 0) for a in ok], w2_ref, par)
        p_ref[tau, 1] = pack((acc + pf_ref[tau, 1]).astype(BF))


def wait_kernel(bx_ref, i_ref, se_ref, sm_ref, w1_ref, w2_ref, j_ref, z_ref, x_ref, s_ref):
    par, _ = here()
    for t in range(2):
        for k in range(2):
            put(x_ref, (t, 1 - k), unpack(bx_ref[t, k]))
            s_ref[t, k] = sm_ref[t, k]
        for k in range(4):
            s_ref[t, k + 2] = se_ref[t, k]
    for tau in range(2):
        ok = [a for a in range(3) if tau + a >= 2]
        acc = taps(x_ref, [(tau + a - 2, p, a, p) for a in ok for p in range(2)], w1_ref, par)
        j_ref[tau, 0] = acc + i_ref[tau, 0]
        acc = taps(x_ref, [(tau + a - 2, 1, a, 0) for a in ok], w1_ref, par)
        j_ref[tau, 1] = acc + i_ref[tau, 1]

    def row(u, _):
        z_ref[0, u] = taps(s_ref, [(0, u + p, 2, p) for p in range(3)], w2_ref, par)
        z_ref[1, u] = taps(s_ref, [(a - 1, u + p, a, p) for a in (1, 2) for p in range(3)], w2_ref, par)
        return 0

    lax.fori_loop(0, 4, row, 0)


def late_kernel(
    t_ref, d_ref, c_ref, o_ref, j_ref, z_ref, w1_ref, w2_ref, b_ref, g_ref, b2_ref, in_ref,
    out_ref, acc_ref, x_ref, s_ref, i_ref, y_ref,
):
    par, keep = here()
    for t in range(2):
        for u in range(4):
            put(x_ref, (t, u + 2), unpack(t_ref[t, u]))
        for k in range(2):
            put(x_ref, (t, 1 - k), unpack(d_ref[t, k]))
            put(x_ref, (t, 6 + k), unpack(c_ref[t, k]))
            i_ref[t, k] = j_ref[t, k]
        for k in range(4):
            i_ref[t, k + 2] = o_ref[t, k]
    bias = b_ref[...]
    g = g_ref[...]

    def row(v, _):
        hold = jnp.where(v == 0, keep, 1.0)
        for tau in range(2):
            acc = taps(x_ref, [(tau + a, v + p, a, p) for a in range(2 - tau) for p in range(3)], w1_ref, par)
            put(s_ref, (tau, v), (act(acc + i_ref[tau, v] + bias, g) * hold).astype(BF))
        return 0

    lax.fori_loop(0, 6, row, 0)
    bias2 = b2_ref[...]
    m = spread(W, 0)

    def last(u, _):
        at = flip(u, par)
        for tau in range(4):
            start = jnp.dot(m, in_ref[tau, at], preferred_element_type=F32) + bias2
            frames = [f for f in range(2) if 0 <= f - tau + 2 <= 2]
            acc = taps(s_ref, [(f, u + p, f - tau + 2, p) for f in frames for p in range(3)], w2_ref, par)
            if tau < 2:
                acc_ref[tau, u] = acc + start
            else:
                y_ref[tau - 2, u] = (acc + z_ref[tau - 2, u] + start).astype(BF)
        return 0

    lax.fori_loop(0, 4, last, 0)
    back = gather()
    for tau in range(2):
        for u in range(4):
            y = jnp.dot(back, y_ref[tau, u], preferred_element_type=F32)
            out_ref[tau + 2, flip(u, par)] = y.astype(BF)


def add_kernel(acc_ref, p_ref, full_ref, out_ref):
    par, _ = here()
    back = gather()
    for u in range(4):
        y = (acc_ref[0, u] + unpack(p_ref[0, u]).astype(F32)).astype(BF)
        z = jnp.dot(back, y, preferred_element_type=F32)
        out_ref[0, flip(u, par)] = z.astype(BF)


VMEM = pl.BlockSpec(memory_space=pltpu.VMEM)
HBM = pl.BlockSpec(memory_space=pltpu.HBM)


def call(kernel, name, ins, outs, scratch, units, limit=32, in_specs=None):
    return pl.pallas_call(
        kernel,
        in_specs=in_specs or [VMEM] * len(ins),
        out_specs=[VMEM] * len(outs),
        out_shape=[jax.ShapeDtypeStruct(s, d) for s, d in outs],
        scratch_shapes=scratch,
        compiler_params=pltpu.CompilerParams(vmem_limit_bytes=limit * MB),
        cost_estimate=pl.CostEstimate(
            flops=int(units * 6e8), bytes_accessed=3_000_000, transcendentals=500_000
        ),
        name=name,
    )(*ins)


def local(frames_in, gain_one, conv_one, bias_one, gain_two, conv_two, bias_two):
    n = lax.axis_size("rows")
    near = [(i, i ^ 1) for i in range(n)]
    far = [(i, i + 1) for i in range(1, n - 1, 2)] + [(i + 1, i) for i in range(1, n - 1, 2)]
    diag = [(i, n + j) for i, j in far]
    g1, g2 = gain_one.reshape(1, C), gain_two.reshape(1, C)
    b1, b2 = bias_one.reshape(1, C), bias_two.reshape(1, C)

    own, bs, as_, ts, ds = call(
        prep_kernel, "prep", [frames_in, g1],
        [((4, 4, E, C), BF), ((4, 2, D, 128), BF), ((4, 2, D, 128), BF), ((2, 4, D, 128), BF), ((2, 2, D, 128), BF)],
        [pltpu.VMEM((4, 4, W, C), BF), pltpu.VMEM((1, C), F32), pltpu.SemaphoreType.DMA((5,))],
        1, in_specs=[HBM, HBM],
    )
    ar = lax.ppermute(as_, "rows", near)
    br = lax.ppermute(bs, "rows", far)
    ts, ds, ar = lax.optimization_barrier((ts, ds, ar))
    tr = lax.ppermute(ts, "tm", [(0, 1)])
    dr = lax.ppermute(ds, ("tm", "rows"), diag)

    se, oacc, iacc, pe, pf = call(
        early_kernel, "early", [own, ar, conv_one, conv_two, b1, g2],
        [((2, 4, E, C), BF), ((2, 4, W, C), F32), ((4, 2, W, C), F32), ((2, 2, D, 128), BF), ((2, 2, W, C), F32)],
        [pltpu.VMEM((4, 6, E, C), BF)], 18,
    )
    sm, ps = call(
        mid_kernel, "mid", [br, iacc, pe, pf, conv_one, conv_two, b1, g2],
        [((2, 2, E, C), BF), ((2, 4, D, 128), BF)],
        [pltpu.VMEM((4, 2, E, C), BF)], 3,
    )
    pr = lax.ppermute(ps, "tm", [(0, 1)])
    jacc, zacc = call(
        wait_kernel, "wait", [br, iacc, se, sm, conv_one, conv_two],
        [((2, 2, W, C), F32), ((2, 4, W, C), F32)],
        [pltpu.VMEM((2, 2, E, C), BF), pltpu.VMEM((2, 6, E, C), BF)], 5,
    )
    tr, dr, ps = lax.optimization_barrier((tr, dr, ps))
    cr = lax.ppermute(jnp.stack([tr[:, 3], tr[:, 2]], axis=1), "rows", near)
    out, acc = call(
        late_kernel, "late", [tr, dr, cr, oacc, jacc, zacc, conv_one, conv_two, b1, g2, b2, frames_in],
        [((4, 4, W, C), BF), ((2, 4, W, C), F32)],
        [pltpu.VMEM((2, 8, E, C), BF), pltpu.VMEM((2, 6, E, C), BF), pltpu.VMEM((2, 6, W, C), F32), pltpu.VMEM((2, 4, W, C), BF)],
        14,
    )
    return pl.pallas_call(
        add_kernel,
        grid=(2,),
        in_specs=[
            pl.BlockSpec((1, 4, W, C), lambda t: (t, 0, 0, 0)),
            pl.BlockSpec((1, 4, D, 128), lambda t: (t, 0, 0, 0)),
            pl.BlockSpec(memory_space=pl.ANY),
        ],
        out_specs=pl.BlockSpec((1, 4, W, C), lambda t: (t, 0, 0, 0)),
        out_shape=jax.ShapeDtypeStruct((4, 4, W, C), BF),
        input_output_aliases={2: 0},
        compiler_params=pltpu.CompilerParams(vmem_limit_bytes=24 * MB),
        cost_estimate=pl.CostEstimate(flops=600_000_000, bytes_accessed=3_000_000, transcendentals=0),
        name="add",
    )(acc, pr, out)


def solution(mesh):
    in_specs = (P("tm", "rows", "roll", None), P(), P(), P(), P(), P(), P())
    out_specs = P("tm", "rows", "roll", None)
    return jax.shard_map(local, mesh=mesh, in_specs=in_specs, out_specs=out_specs, check_vma=False)
```

profile of v0, /device:TPU:65, one launch (start us, length us, event | category | flops | bytes accessed | tf_op | source)
XLA Modules:
  0.0 53.8 jit_solution(13853547839959339747)
XLA Ops:
  0.0 0.0 copy-start.5
  0.0 0.0 copy-start.6
  0.0 1.3 %copy-done.6 = bf16[4,4,160,192]{3,2,1,0:T(8,128)(2,1)S(1)} copy-done((bf16[4,4,160,192]{3,2,1,0:T(8,128)(2,1)S(1)}, bf16[4,4,160,192]{3,2,1,0:T(8,128)(2,1)}, u32[]{:S(2)}) %copy-start.6) | copy-done | bytes 983064
  1.3 0.0 copy-start.8
  1.4 0.7 %copy-done.8 = f32[192]{0:T(256)S(1)} copy-done((f32[192]{0:T(256)S(1)}, f32[192]{0:T(256)}, u32[]{:S(2)}) %copy-start.8) | copy-done | bytes 792
  2.0 2.4 %prep.1 = (bf16[4,4,192,192]{3,2,1,0:T(8,128)(2,1)S(1)}, bf16[4,2,240,128]{3,2,1,0:T(8,128)(2,1)S(1)}, bf16[4,2,240,128]{3,2,1,0:T(8,128)(2,1)S(1)}, bf16[2,4,24...) custom-call(bf16[4,4,160,192]{3,2,1,0:T(8,128)(2,1)S(1)} %copy-done.6, f32[1,192]{1,0:T(1,128)S(1)} %bitcast.10), custom_call_target="tpu_custom_call" | custom-call | flops 600000000 | bytes 3000000 | tf_op jit(solution)/shard_map/prep/pallas_call | solution.py:241
  4.4 0.8 %collective-permute-start = (bf16[4,2,240,128]{3,2,1,0:T(8,128)(2,1)S(1)}, bf16[4,2,240,128]{3,2,1,0:T(8,128)(2,1)S(1)}, u32[]{:S(2)}, u32[]{:S(2)}) collective-permute-start(bf16[4,2,240,128]{3,2,1,0:T(8,128)(2,1)S(1)} %get-tuple-element.28), channel_id=1, source_target_pairs={{0,1},{1,0},{2,3},{3,2},{4,5},{5,4},{6,7},{7,6},{8,9},{9,8},{10,11... | collective-permute-start | bytes 1474568 | tf_op jit(solution)/shard_map/ppermute | solution.py:269
  5.2 4.5 %collective-permute-start.3 = (bf16[4,2,240,128]{3,2,1,0:T(8,128)(2,1)S(1)}, bf16[4,2,240,128]{3,2,1,0:T(8,128)(2,1)S(1)}, u32[]{:S(2)}, u32[]{:S(2)}) collective-permute-start(bf16[4,2,240,128]{3,2,1,0:T(8,128)(2,1)S(1)} %get-tuple-element.31), channel_id=1, source_target_pairs={{1,2},{3,4},{5,6},{7,8},{9,10},{11,12},{13,14},{15,16},{17,18},{19... | collective-permute-start | bytes 1474568 | tf_op jit(solution)/shard_map/ppermute | solution.py:270
  9.7 0.0 collective-permute-done.a_ref
  9.7 3.1 %collective-permute-start.2 = (bf16[2,2,240,128]{3,2,1,0:T(8,128)(2,1)S(1)}, bf16[2,2,240,128]{3,2,1,0:T(8,128)(2,1)S(1)}, u32[]{:S(2)}, u32[]{:S(2)}) collective-permute-start(bf16[2,2,240,128]{3,2,1,0:T(8,128)(2,1)S(1)} %get-tuple-element.30), channel_id=1, source_target_pairs={{1,66},{3,68},{5,70},{7,72},{9,74},{11,76},{13,78},{15,80},{17,82}... | collective-permute-start | bytes 737288 | tf_op jit(solution)/shard_map/ppermute | solution.py:273
  12.9 1.3 %collective-permute-start.1 = (bf16[2,4,240,128]{3,2,1,0:T(8,128)(2,1)S(1)}, bf16[2,4,240,128]{3,2,1,0:T(8,128)(2,1)S(1)}, u32[]{:S(2)}, u32[]{:S(2)}) collective-permute-start(bf16[2,4,240,128]{3,2,1,0:T(8,128)(2,1)S(1)} %get-tuple-element.29), channel_id=1, source_target_pairs={{0,64},{1,65},{2,66},{3,67},{4,68},{5,69},{6,70},{7,71},{8,72},{9,... | collective-permute-start | bytes 1474568 | tf_op jit(solution)/shard_map/ppermute | solution.py:272
  14.2 0.0 copy-done.5
  14.2 0.0 copy-done.4
  14.2 0.0 copy-start
  14.3 1.7 %copy-done = bf16[3,3,3,192,192]{4,3,2,1,0:T(8,128)(2,1)S(1)} copy-done((bf16[3,3,3,192,192]{4,3,2,1,0:T(8,128)(2,1)S(1)}, bf16[3,3,3,192,192]{4,3,2,1,0:T(8,128)(2,1)}, u32[]{:S(2)}) %copy-start) | copy-done | bytes 1990680
  16.0 1.7 %copy-done.2 = bf16[3,3,3,192,192]{4,3,2,1,0:T(8,128)(2,1)S(1)} copy-done((bf16[3,3,3,192,192]{4,3,2,1,0:T(8,128)(2,1)S(1)}, bf16[3,3,3,192,192]{4,3,2,1,0:T(8,128)(2,1)}, u32[]{:S(2)}) %copy-start.2) | copy-done | bytes 1990680
  17.7 11.3 %early.1 = (bf16[2,4,192,192]{3,2,1,0:T(8,128)(2,1)S(1)}, f32[2,4,160,192]{3,2,1,0:T(8,128)S(1)}, f32[4,2,160,192]{3,2,1,0:T(8,128)S(1)}, bf16[2,2,240,128]{3,2,1,0:T(8,128)(2,1)S(1)}, f32[2,2,160,192]{3,2,1,0:T(8,128)S(1)}) custom-call(bf16[4,4,192,192]{3,2,1,0:T(8,128)(2,1)S(1)} %get-tuple-element.32.own_ref, ...), custom_call_target="tpu_custom_call" | custom-call | flops 10800000000 | bytes 3000000 | tf_op jit(solution)/shard_map/early/pallas_call | solution.py:241
  29.0 0.0 collective-permute-done.3.bx_ref
  29.1 0.0 copy-done.1
  29.1 0.0 copy-done.3
  29.1 2.1 %mid.1 = (bf16[2,2,192,192]{3,2,1,0:T(8,128)(2,1)S(1)}, bf16[2,4,240,128]{3,2,1,0:T(8,128)(2,1)S(1)}) custom-call(bf16[4,2,240,128]{3,2,1,0:T(8,128)(2,1)S(1)} %collective-permute-done.3.bx_ref, f32[4,2,160,192]{3,2,1,0:T(8,128)S(1)} %get-tuple-element.34.i_ref, bf16[2,2,240,128]{3,2,1,0:T(8,128)(2,1)S(1)} %get-tuple-element.35.pe_ref, ...), custom_call_target="tpu_custom_call" | custom-call | flops 1800000000 | bytes 3000000 | tf_op jit(solution)/shard_map/mid/pallas_call | solution.py:241
  31.2 1.3 %collective-permute-start.5 = (bf16[2,4,240,128]{3,2,1,0:T(8,128)(2,1)S(1)}, bf16[2,4,240,128]{3,2,1,0:T(8,128)(2,1)S(1)}, u32[]{:S(2)}, u32[]{:S(2)}) collective-permute-start(bf16[2,4,240,128]{3,2,1,0:T(8,128)(2,1)S(1)} %get-tuple-element.37), channel_id=1, source_target_pairs={{0,64},{1,65},{2,66},{3,67},{4,68},{5,69},{6,70},{7,71},{8,72},{9,... | collective-permute-start | bytes 1474568 | tf_op jit(solution)/shard_map/ppermute | solution.py:285
  32.5 0.0 collective-permute-done.2.d_ref
  32.5 0.0 collective-permute-done.1.t_ref
  32.6 3.3 %collective-permute-start.4 = (bf16[2,2,240,128]{3,2,1,0:T(8,128)(2,1)S(1)}, bf16[2,2,240,128]{3,2,1,0:T(8,128)(2,1)S(1)}, u32[]{:S(2)}, u32[]{:S(2)}) collective-permute-start(bf16[2,2,240,128]{3,2,1,0:T(8,128)(2,1)S(1)} %pad_maximum_fusion), channel_id=1, source_target_pairs={{0,1},{1,0},{2,3},{3,2},{4,5},{5,4},{6,7},{7,6},{8,9},{9,8},{10,11... | collective-permute-start | bytes 737288 | tf_op jit(solution)/shard_map/ppermute | solution.py:292
  35.9 3.8 %wait.1 = (f32[2,2,160,192]{3,2,1,0:T(8,128)S(1)}, f32[2,4,160,192]{3,2,1,0:T(8,128)S(1)}) custom-call(bf16[4,2,240,128]{3,2,1,0:T(8,128)(2,1)S(1)} %collective-permute-done.3.bx_ref, f32[4,2,160,192]{3,2,1,0:T(8,128)S(1)} %get-tuple-element.34.i_ref, bf16[2,4,192,192]{3,2,1,0:T(8,128)(2,1)S(1)} %get-tuple-element.41.se_ref, ...), custom_call_target="tpu_custom_call" | custom-call | flops 3000000000 | bytes 3000000 | tf_op jit(solution)/shard_map/wait/pallas_call | solution.py:241
  39.8 0.0 collective-permute-done.4.c_ref
  39.8 0.0 copy-done.7
  39.8 0.0 copy-done.9
  39.8 12.6 %late.1 = (bf16[4,4,160,192]{3,2,1,0:T(8,128)(2,1)}, f32[2,4,160,192]{3,2,1,0:T(8,128)S(1)}) custom-call(bf16[2,4,240,128]{3,2,1,0:T(8,128)(2,1)S(1)} %collective-permute-done.1.t_ref, bf16[2,2,240,128]{3,2,1,0:T(8,128)(2,1)S(1)} %collective-permute-done.2.d_ref, bf16[2,2,240,128]{3,2,1,0:T(8,128)(2,1)S(1)} %collective-permute-done.4.c_ref, ...), custom_call_target="tpu_custom_call" | custom-call | flops 8400000000 | bytes 3000000 | tf_op jit(solution)/shard_map/late/pallas_call | solution.py:241
  52.4 0.0 collective-permute-done.5.p_ref
  52.4 1.4 %add.1 = bf16[4,4,160,192]{3,2,1,0:T(8,128)(2,1)} custom-call(f32[2,4,160,192]{3,2,1,0:T(8,128)S(1)} %get-tuple-element.45.acc_ref, bf16[2,4,240,128]{3,2,1,0:T(8,128)(2,1)S(1)} %collective-permute-done.5.p_ref, bf16[4,4,160,192]{3,2,1,0:T(8,128)(2,1)} %get-tuple-element.46.full_ref), custom_call_target="tpu_custom_call", output_to_operand_aliasing={{}: (2, {})} | custom-call | flops 600000000 | bytes 3000000 | tf_op jit(solution)/shard_map/add/pallas_call | solution.py:299
  (8 shorter events, 0.1 us)
Async XLA Ops:
  0.0 14.2 %copy-start.5 = (f32[192]{0:T(256)S(1)}, f32[192]{0:T(256)}, u32[]{:S(2)}) copy-start(f32[192]{0:T(256)} %param.11) | copy-start | bytes 2308
  0.0 14.2 %copy-start.4 = (f32[192]{0:T(256)S(1)}, f32[192]{0:T(256)}, u32[]{:S(2)}) copy-start(f32[192]{0:T(256)} %param.10) | copy-start | bytes 2308
  0.0 1.3 %copy-start.6 = (bf16[4,4,160,192]{3,2,1,0:T(8,128)(2,1)S(1)}, bf16[4,4,160,192]{3,2,1,0:T(8,128)(2,1)}, u32[]{:S(2)}) copy-start(bf16[4,4,160,192]{3,2,1,0:T(8,128)(2,1)} %in_ref.1) | copy-start | bytes 2949124
  1.3 0.7 %copy-start.8 = (f32[192]{0:T(256)S(1)}, f32[192]{0:T(256)}, u32[]{:S(2)}) copy-start(f32[192]{0:T(256)} %param.8) | copy-start | bytes 2308
  4.4 5.3 %collective-permute-start = (bf16[4,2,240,128]{3,2,1,0:T(8,128)(2,1)S(1)}, bf16[4,2,240,128]{3,2,1,0:T(8,128)(2,1)S(1)}, u32[]{:S(2)}, u32[]{:S(2)}) collective-permute-start(bf16[4,2,240,128]{3,2,1,0:T(8,128)(2,1)S(1)} %get-tuple-element.28), channel_id=1, source_target_pairs={{0,1},{1,0},{2,3},{3,2},{4,5},{5,4},{6,7},{7,6},{8,9},{9,8},{10,11... | collective-permute-start | bytes 1474568 | tf_op jit(solution)/shard_map/ppermute | solution.py:269
  5.2 23.9 %collective-permute-start.3 = (bf16[4,2,240,128]{3,2,1,0:T(8,128)(2,1)S(1)}, bf16[4,2,240,128]{3,2,1,0:T(8,128)(2,1)S(1)}, u32[]{:S(2)}, u32[]{:S(2)}) collective-permute-start(bf16[4,2,240,128]{3,2,1,0:T(8,128)(2,1)S(1)} %get-tuple-element.31), channel_id=1, source_target_pairs={{1,2},{3,4},{5,6},{7,8},{9,10},{11,12},{13,14},{15,16},{17,18},{19... | collective-permute-start | bytes 1474568 | tf_op jit(solution)/shard_map/ppermute | solution.py:270
  9.7 22.8 %collective-permute-start.2 = (bf16[2,2,240,128]{3,2,1,0:T(8,128)(2,1)S(1)}, bf16[2,2,240,128]{3,2,1,0:T(8,128)(2,1)S(1)}, u32[]{:S(2)}, u32[]{:S(2)}) collective-permute-start(bf16[2,2,240,128]{3,2,1,0:T(8,128)(2,1)S(1)} %get-tuple-element.30), channel_id=1, source_target_pairs={{1,66},{3,68},{5,70},{7,72},{9,74},{11,76},{13,78},{15,80},{17,82}... | collective-permute-start | bytes 737288 | tf_op jit(solution)/shard_map/ppermute | solution.py:273
  12.9 19.7 %collective-permute-start.1 = (bf16[2,4,240,128]{3,2,1,0:T(8,128)(2,1)S(1)}, bf16[2,4,240,128]{3,2,1,0:T(8,128)(2,1)S(1)}, u32[]{:S(2)}, u32[]{:S(2)}) collective-permute-start(bf16[2,4,240,128]{3,2,1,0:T(8,128)(2,1)S(1)} %get-tuple-element.29), channel_id=1, source_target_pairs={{0,64},{1,65},{2,66},{3,67},{4,68},{5,69},{6,70},{7,71},{8,72},{9,... | collective-permute-start | bytes 1474568 | tf_op jit(solution)/shard_map/ppermute | solution.py:272
  14.2 1.8 %copy-start = (bf16[3,3,3,192,192]{4,3,2,1,0:T(8,128)(2,1)S(1)}, bf16[3,3,3,192,192]{4,3,2,1,0:T(8,128)(2,1)}, u32[]{:S(2)}) copy-start(bf16[3,3,3,192,192]{4,3,2,1,0:T(8,128)(2,1)} %w1_ref.7) | copy-start | bytes 5971972
  16.0 1.7 %copy-start.2 = (bf16[3,3,3,192,192]{4,3,2,1,0:T(8,128)(2,1)S(1)}, bf16[3,3,3,192,192]{4,3,2,1,0:T(8,128)(2,1)}, u32[]{:S(2)}) copy-start(bf16[3,3,3,192,192]{4,3,2,1,0:T(8,128)(2,1)} %w2_ref.7) | copy-start | bytes 5971972
  17.7 11.3 %copy-start.1 = (bf16[3,3,3,192,192]{4,3,2,1,0:T(8,128)(2,1)S(1)}, bf16[3,3,3,192,192]{4,3,2,1,0:T(8,128)(2,1)}, u32[]{:S(2)}) copy-start(bf16[3,3,3,192,192]{4,3,2,1,0:T(8,128)(2,1)} %w1_ref.7) | copy-start | bytes 5971972
  17.7 11.3 %copy-start.3 = (bf16[3,3,3,192,192]{4,3,2,1,0:T(8,128)(2,1)S(1)}, bf16[3,3,3,192,192]{4,3,2,1,0:T(8,128)(2,1)}, u32[]{:S(2)}) copy-start(bf16[3,3,3,192,192]{4,3,2,1,0:T(8,128)(2,1)} %w2_ref.7) | copy-start | bytes 5971972
  31.2 21.2 %collective-permute-start.5 = (bf16[2,4,240,128]{3,2,1,0:T(8,128)(2,1)S(1)}, bf16[2,4,240,128]{3,2,1,0:T(8,128)(2,1)S(1)}, u32[]{:S(2)}, u32[]{:S(2)}) collective-permute-start(bf16[2,4,240,128]{3,2,1,0:T(8,128)(2,1)S(1)} %get-tuple-element.37), channel_id=1, source_target_pairs={{0,64},{1,65},{2,66},{3,67},{4,68},{5,69},{6,70},{7,71},{8,72},{9,... | collective-permute-start | bytes 1474568 | tf_op jit(solution)/shard_map/ppermute | solution.py:285
  32.6 7.2 %collective-permute-start.4 = (bf16[2,2,240,128]{3,2,1,0:T(8,128)(2,1)S(1)}, bf16[2,2,240,128]{3,2,1,0:T(8,128)(2,1)S(1)}, u32[]{:S(2)}, u32[]{:S(2)}) collective-permute-start(bf16[2,2,240,128]{3,2,1,0:T(8,128)(2,1)S(1)} %pad_maximum_fusion), channel_id=1, source_target_pairs={{0,1},{1,0},{2,3},{3,2},{4,5},{5,4},{6,7},{7,6},{8,9},{9,8},{10,11... | collective-permute-start | bytes 737288 | tf_op jit(solution)/shard_map/ppermute | solution.py:292
  35.9 3.9 %copy-start.7 = (bf16[4,4,160,192]{3,2,1,0:T(8,128)(2,1)S(1)}, bf16[4,4,160,192]{3,2,1,0:T(8,128)(2,1)}, u32[]{:S(2)}) copy-start(bf16[4,4,160,192]{3,2,1,0:T(8,128)(2,1)} %in_ref.1) | copy-start | bytes 2949124
  35.9 3.9 %copy-start.9 = (f32[192]{0:T(256)S(1)}, f32[192]{0:T(256)}, u32[]{:S(2)}) copy-start(f32[192]{0:T(256)} %param.13) | copy-start | bytes 2308
where the time goes:
time: 54.1 us; the launch traced here: 53.8 us
  Pallas kernels  33.6 us (62%)
  starting transfers between devices  14.4 us (27%)
  local copies, waits for them, and re-layouts  5.55 us (10%)
    pallas_call x5, Pallas kernels, call(): pl.pallas_call(kernel, in_specs=in_specs or [VMEM] * len(ins), out_specs=...  32.3 us
    unnamed x20, local copies, waits for them, and re-layouts  5.53 us
    ppermute x1, starting transfers between devices, local(): br = lax.ppermute(bs, 'rows', far)  4.55 us
    ppermute x1, starting transfers between devices, local(): cr = lax.ppermute(jnp.stack([tr[:, 3], tr[:, 2]], axis=1), 'rows', near)  3.3 us
    ppermute x1, starting transfers between devices, local(): dr = lax.ppermute(ds, ('tm', 'rows'), diag)  3.15 us
    pallas_call x1, Pallas kernels, local(): pl.pallas_call(add_kernel, grid=(2,), in_specs=[pl.BlockSpec((1, 4, W, C)...  1.37 us
    ppermute x1, starting transfers between devices, local(): tr = lax.ppermute(ts, 'tm', [(0, 1)])  1.32 us
    ppermute x1, starting transfers between devices, local(): pr = lax.ppermute(ps, 'tm', [(0, 1)])  1.32 us
  transfers between devices with their start and end apart: 6, of which 0 were waited for; matrix products, arithmetic and copies ran while one was open for 0% of the time, Pallas kernels for 56%

commit v1 on v0

--- a/solution.py
+++ b/solution.py
@@ -72,18 +72,11 @@
     return r % 2, keep
 
 
-def prep_kernel(x_hbm, g_hbm, own_ref, b_ref, a_ref, t_ref, d_ref, x_ref, g_ref, sem):
+def prep_kernel(x_ref, k_ref, own_ref, b_ref, a_ref, t_ref, d_ref):
     par, _ = here()
-    cg = pltpu.make_async_copy(g_hbm, g_ref, sem.at[4])
-    cg.start()
-    copies = [pltpu.make_async_copy(x_hbm.at[t], x_ref.at[t], sem.at[t]) for t in range(4)]
-    for c in copies:
-        c.start()
     m = spread(E, 1)
-    cg.wait()
-    g = g_ref[...]
+    g = k_ref[0:1, :]
     for t in range(4):
-        copies[t].wait()
         for u in range(4):
             xp = jnp.dot(m, x_ref[t, flip(u, par)], preferred_element_type=F32)
             f = act(xp, g).astype(BF)
@@ -99,15 +92,14 @@
                 t_ref[t - 2, u] = d
 
 
-def early_kernel(own_ref, a_ref, w1_ref, w2_ref, b_ref, g_ref, s_ref, o_ref, i_ref, pe_ref, pf_ref, x_ref):
+def early_kernel(own_ref, a_ref, w1_ref, w2_ref, k_ref, s_ref, o_ref, i_ref, pe_ref, pf_ref, x_ref):
     par, _ = here()
     for t in range(4):
         for u in range(4):
             x_ref[t, u] = own_ref[t, u]
         for k in range(2):
             put(x_ref, (t, 4 + k), unpack(a_ref[t, k]))
-    bias = b_ref[...]
-    g = g_ref[...]
+    bias, g = k_ref[1:2, :], k_ref[2:3, :]
 
     def row(k, _):
         for tau in range(2):
@@ -131,13 +123,12 @@
             pe_ref[tau, u] = pack(acc.astype(BF))
 
 
-def mid_kernel(bx_ref, i_ref, pe_ref, pf_ref, w1_ref, w2_ref, b_ref, g_ref, s_ref, p_ref, x_ref):
+def mid_kernel(bx_ref, i_ref, pe_ref, pf_ref, w1_ref, w2_ref, k_ref, s_ref, p_ref, x_ref):
     par, keep = here()
     for t in range(4):
         for k in range(2):
             put(x_ref, (t, 1 - k), unpack(bx_ref[t, k]))
-    bias = b_ref[...]
-    g = g_ref[...]
+    bias, g = k_ref[1:2, :], k_ref[2:3, :]
     for tau in range(2):
         acc = taps(x_ref, [(tau + a, p, a, p) for a in range(3) for p in range(2)], w1_ref, par)
         put(s_ref, (tau, 0), (act(acc + i_ref[tau + 2, 0] + bias, g) * keep).astype(BF))
@@ -177,34 +168,37 @@
 
 
 def late_kernel(
-    t_ref, d_ref, c_ref, o_ref, j_ref, z_ref, w1_ref, w2_ref, b_ref, g_ref, b2_ref, in_ref,
-    out_ref, acc_ref, x_ref, s_ref, i_ref, y_ref,
+    t_ref, d_ref, c_ref, o_ref, j_ref, z_ref, w1_ref, w2_ref, k_ref, in_ref,
+    out_ref, acc_ref, x_ref, s_ref, y_ref, n_ref, sem,
 ):
     par, keep = here()
-    for t in range(2):
-        for u in range(4):
-            put(x_ref, (t, u + 2), unpack(t_ref[t, u]))
-        for k in range(2):
-            put(x_ref, (t, 1 - k), unpack(d_ref[t, k]))
-            put(x_ref, (t, 6 + k), unpack(c_ref[t, k]))
-            i_ref[t, k] = j_ref[t, k]
-        for k in range(4):
-            i_ref[t, k + 2] = o_ref[t, k]
-    bias = b_ref[...]
-    g = g_ref[...]
-
-    def row(v, _):
-        hold = jnp.where(v == 0, keep, 1.0)
+
+    def fetch(v):
+        for t in range(2):
+            d = d_ref[t, 1 - v] if v < 2 else t_ref[t, v - 2] if v < 6 else c_ref[t, v - 6]
+            put(x_ref, (t, v), unpack(d))
+
+    for v in range(3):
+        fetch(v)
+    bias, g, bias2 = k_ref[1:2, :], k_ref[2:3, :], k_ref[3:4, :]
+    for v in range(6):
+        if v:
+            fetch(v + 2)
         for tau in range(2):
             acc = taps(x_ref, [(tau + a, v + p, a, p) for a in range(2 - tau) for p in range(3)], w1_ref, par)
-            put(s_ref, (tau, v), (act(acc + i_ref[tau, v] + bias, g) * hold).astype(BF))
-        return 0
-
-    lax.fori_loop(0, 6, row, 0)
-    bias2 = b2_ref[...]
-    m = spread(W, 0)
-
-    def last(u, _):
+            f = act(acc + (j_ref[tau, v] if v < 2 else o_ref[tau, v - 2]) + bias, g)
+            put(s_ref, (tau, v), (f if v else f * keep).astype(BF))
+    m, back = spread(W, 0), gather()
+
+    def leave(tau, u):
+        return pltpu.make_async_copy(n_ref.at[tau, u], out_ref.at[tau + 2, flip(u, par)], sem.at[tau, u])
+
+    def finish(u):
+        for tau in range(2):
+            n_ref[tau, u] = jnp.dot(back, y_ref[tau, u], preferred_element_type=F32).astype(BF)
+            leave(tau, u).start()
+
+    for u in range(4):
         at = flip(u, par)
         for tau in range(4):
             start = jnp.dot(m, in_ref[tau, at], preferred_element_type=F32) + bias2
@@ -214,40 +208,45 @@
                 acc_ref[tau, u] = acc + start
             else:
                 y_ref[tau - 2, u] = (acc + z_ref[tau - 2, u] + start).astype(BF)
-        return 0
-
-    lax.fori_loop(0, 4, last, 0)
-    back = gather()
-    for tau in range(2):
-        for u in range(4):
-            y = jnp.dot(back, y_ref[tau, u], preferred_element_type=F32)
-            out_ref[tau + 2, flip(u, par)] = y.astype(BF)
-
-
-def add_kernel(acc_ref, p_ref, full_ref, out_ref):
+        if u:
+            finish(u - 1)
+    finish(3)
+    for u in range(4):
+        for tau in range(2):
+            leave(tau, u).wait()
+
+
+def add_kernel(acc_ref, p_ref, full_ref, out_ref, n_ref, sem):
     par, _ = here()
     back = gather()
-    for u in range(4):
-        y = (acc_ref[0, u] + unpack(p_ref[0, u]).astype(F32)).astype(BF)
-        z = jnp.dot(back, y, preferred_element_type=F32)
-        out_ref[0, flip(u, par)] = z.astype(BF)
+    sent = []
+    for t in range(2):
+        for u in range(4):
+            y = (acc_ref[t, u] + unpack(p_ref[t, u]).astype(F32)).astype(BF)
+            n_ref[t, u] = jnp.dot(back, y, preferred_element_type=F32).astype(BF)
+            copy = pltpu.make_async_copy(n_ref.at[t, u], out_ref.at[t, flip(u, par)], sem.at[t, u])
+            copy.start()
+            sent.append(copy)
+    for copy in sent:
+        copy.wait()
 
 
 VMEM = pl.BlockSpec(memory_space=pltpu.VMEM)
-HBM = pl.BlockSpec(memory_space=pltpu.HBM)
-
-
-def call(kernel, name, ins, outs, scratch, units, limit=32, in_specs=None):
+ANY = pl.BlockSpec(memory_space=pl.ANY)
+
+
+def call(kernel, name, ins, outs, scratch, units, limit=32, in_specs=None, out_specs=None, alias={}):
     return pl.pallas_call(
         kernel,
         in_specs=in_specs or [VMEM] * len(ins),
-        out_specs=[VMEM] * len(outs),
+        out_specs=out_specs or [VMEM] * len(outs),
         out_shape=[jax.ShapeDtypeStruct(s, d) for s, d in outs],
         scratch_shapes=scratch,
         compiler_params=pltpu.CompilerParams(vmem_limit_bytes=limit * MB),
         cost_estimate=pl.CostEstimate(
             flops=int(units * 6e8), bytes_accessed=3_000_000, transcendentals=500_000
         ),
+        input_output_aliases=alias,
         name=name,
     )(*ins)
 
@@ -257,14 +256,12 @@
     near = [(i, i ^ 1) for i in range(n)]
     far = [(i, i + 1) for i in range(1, n - 1, 2)] + [(i + 1, i) for i in range(1, n - 1, 2)]
     diag = [(i, n + j) for i, j in far]
-    g1, g2 = gain_one.reshape(1, C), gain_two.reshape(1, C)
-    b1, b2 = bias_one.reshape(1, C), bias_two.reshape(1, C)
+    kv = jnp.stack([gain_one, bias_one, gain_two, bias_two])
 
     own, bs, as_, ts, ds = call(
-        prep_kernel, "prep", [frames_in, g1],
+        prep_kernel, "prep", [frames_in, kv],
         [((4, 4, E, C), BF), ((4, 2, D, 128), BF), ((4, 2, D, 128), BF), ((2, 4, D, 128), BF), ((2, 2, D, 128), BF)],
-        [pltpu.VMEM((4, 4, W, C), BF), pltpu.VMEM((1, C), F32), pltpu.SemaphoreType.DMA((5,))],
-        1, in_specs=[HBM, HBM],
+        [], 40,
     )
     ar = lax.ppermute(as_, "rows", near)
     br = lax.ppermute(bs, "rows", far)
@@ -273,12 +270,12 @@
     dr = lax.ppermute(ds, ("tm", "rows"), diag)
 
     se, oacc, iacc, pe, pf = call(
-        early_kernel, "early", [own, ar, conv_one, conv_two, b1, g2],
+        early_kernel, "early", [own, ar, conv_one, conv_two, kv],
         [((2, 4, E, C), BF), ((2, 4, W, C), F32), ((4, 2, W, C), F32), ((2, 2, D, 128), BF), ((2, 2, W, C), F32)],
         [pltpu.VMEM((4, 6, E, C), BF)], 18,
     )
     sm, ps = call(
-        mid_kernel, "mid", [br, iacc, pe, pf, conv_one, conv_two, b1, g2],
+        mid_kernel, "mid", [br, iacc, pe, pf, conv_one, conv_two, kv],
         [((2, 2, E, C), BF), ((2, 4, D, 128), BF)],
         [pltpu.VMEM((4, 2, E, C), BF)], 3,
     )
@@ -286,31 +283,25 @@
     jacc, zacc = call(
         wait_kernel, "wait", [br, iacc, se, sm, conv_one, conv_two],
         [((2, 2, W, C), F32), ((2, 4, W, C), F32)],
-        [pltpu.VMEM((2, 2, E, C), BF), pltpu.VMEM((2, 6, E, C), BF)], 5,
-    )
-    tr, dr, ps = lax.optimization_barrier((tr, dr, ps))
+        [pltpu.VMEM((2, 2, E, C), BF), pltpu.VMEM((2, 6, E, C), BF)], 20,
+    )
+    tr, dr, zacc = lax.optimization_barrier((tr, dr, zacc))
     cr = lax.ppermute(jnp.stack([tr[:, 3], tr[:, 2]], axis=1), "rows", near)
     out, acc = call(
-        late_kernel, "late", [tr, dr, cr, oacc, jacc, zacc, conv_one, conv_two, b1, g2, b2, frames_in],
+        late_kernel, "late", [tr, dr, cr, oacc, jacc, zacc, conv_one, conv_two, kv, frames_in],
         [((4, 4, W, C), BF), ((2, 4, W, C), F32)],
-        [pltpu.VMEM((2, 8, E, C), BF), pltpu.VMEM((2, 6, E, C), BF), pltpu.VMEM((2, 6, W, C), F32), pltpu.VMEM((2, 4, W, C), BF)],
-        14,
-    )
-    return pl.pallas_call(
-        add_kernel,
-        grid=(2,),
-        in_specs=[
-            pl.BlockSpec((1, 4, W, C), lambda t: (t, 0, 0, 0)),
-            pl.BlockSpec((1, 4, D, 128), lambda t: (t, 0, 0, 0)),
-            pl.BlockSpec(memory_space=pl.ANY),
+        [
+            pltpu.VMEM((2, 8, E, C), BF), pltpu.VMEM((2, 6, E, C), BF), pltpu.VMEM((2, 4, W, C), BF),
+            pltpu.VMEM((2, 4, W, C), BF), pltpu.SemaphoreType.DMA((2, 4)),
         ],
-        out_specs=pl.BlockSpec((1, 4, W, C), lambda t: (t, 0, 0, 0)),
-        out_shape=jax.ShapeDtypeStruct((4, 4, W, C), BF),
-        input_output_aliases={2: 0},
-        compiler_params=pltpu.CompilerParams(vmem_limit_bytes=24 * MB),
-        cost_estimate=pl.CostEstimate(flops=600_000_000, bytes_accessed=3_000_000, transcendentals=0),
-        name="add",
-    )(acc, pr, out)
+        1, out_specs=[ANY, VMEM],
+    )
+    (out,) = call(
+        add_kernel, "add", [acc, pr, out], [((4, 4, W, C), BF)],
+        [pltpu.VMEM((2, 4, W, C), BF), pltpu.SemaphoreType.DMA((2, 4))],
+        1, in_specs=[VMEM, VMEM, ANY], out_specs=[ANY], alias={2: 0},
+    )
+    return out
 
 
 def solution(mesh):

time: 54.1 us -> 48.7 us (0.900)
  local copies, waits for them, and re-layouts: 5.55 us -> 1.34 us
  Pallas kernels: 33.6 us -> 30.5 us
  waiting for transfers between devices: 0.02 us -> 1.15 us
  other arithmetic: 0.03 us -> 0.76 us
    unnamed x20 -> x8, local copies, waits for them, and re-layouts: 5.53 us -> 1.33 us
    pallas_call x5 -> x6, Pallas kernels: 32.3 us -> 30.5 us  [call(): pl.pallas_call(kernel, in_specs=in_specs or [VMEM] * len(ins), out_specs=...]
    pallas_call x1 -> x0, Pallas kernels: 1.37 us -> none  [local(): pl.pallas_call(add_kernel, grid=(2,), in_specs=[pl.BlockSpec((1, 4, W, C)...]
    ppermute x1, waiting for transfers between devices: 0.01 us -> 1.14 us  [local(): cr = lax.ppermute(jnp.stack([tr[:, 3], tr[:, 2]], axis=1), 'rows', near)]
    another operation x0 -> x1, other arithmetic: none -> 0.74 us  [local(): kv = jnp.stack([gain_one, bias_one, gain_two, bias_two])]
  transfers between devices with their start and end apart: 6 -> 6, of which waited for: 0 -> 1; matrix products, arithmetic and copies ran while one was open for 0% -> 0% of each run, Pallas kernels for 56% -> 57%
where the time goes in v1:
time: 48.7 us; the launch traced here: 48.5 us
  Pallas kernels  30.5 us (63%)
  starting transfers between devices  14.4 us (30%)
  local copies, waits for them, and re-layouts  1.34 us (3%)
  waiting for transfers between devices  1.15 us (2%)
  other arithmetic  0.76 us (2%)
    pallas_call x6, Pallas kernels, call(): pl.pallas_call(kernel, in_specs=in_specs or [VMEM] * len(ins), out_specs=...  30.5 us
    ppermute x1, starting transfers between devices, local(): br = lax.ppermute(bs, 'rows', far)  4.55 us
    ppermute x1, starting transfers between devices, local(): cr = lax.ppermute(jnp.stack([tr[:, 3], tr[:, 2]], axis=1), 'rows', near)  3.28 us
    ppermute x1, starting transfers between devices, local(): dr = lax.ppermute(ds, ('tm', 'rows'), diag)  3.15 us
    unnamed x8, local copies, waits for them, and re-layouts  1.33 us
    ppermute x1, starting transfers between devices, local(): tr = lax.ppermute(ts, 'tm', [(0, 1)])  1.32 us
    ppermute x1, starting transfers between devices, local(): pr = lax.ppermute(ps, 'tm', [(0, 1)])  1.32 us
    ppermute x1, waiting for transfers between devices, local(): cr = lax.ppermute(jnp.stack([tr[:, 3], tr[:, 2]], axis=1), 'rows', near)  1.14 us
  transfers between devices with their start and end apart: 6, of which 1 were waited for; matrix products, arithmetic and copies ran while one was open for 0% of the time, Pallas kernels for 57%

profile of v1, /device:TPU:65, one launch (start us, length us, event | category | flops | bytes accessed | tf_op | source)
XLA Modules:
  0.0 48.5 jit_solution(9928247288373392036)
XLA Ops:
  0.0 0.7 %pad_maximum_fusion.1.k_ref = f32[4,192]{1,0:T(4,128)S(1)} fusion(f32[1,192]{1,0:T(1,128)} %bitcast.4, f32[1,192]{1,0:T(1,128)} %bitcast.5, f32[1,192]{1,0:T(1,128)} %bitcast.6, f32[1,192]{1,0:T(1,128)} %bitcast.7), kind=kLoop, calls=%fused_computation.1 | loop fusion | flops 2304 | bytes 6144 | tf_op jit(solution)/shard_map/stack | solution.py:259
  0.7 0.0 copy-start.2
  0.8 1.3 %copy-done.2 = bf16[4,4,160,192]{3,2,1,0:T(8,128)(2,1)S(1)} copy-done((bf16[4,4,160,192]{3,2,1,0:T(8,128)(2,1)S(1)}, bf16[4,4,160,192]{3,2,1,0:T(8,128)(2,1)}, u32[]{:S(2)}) %copy-start.2) | copy-done | bytes 983064
  2.1 0.0 copy-start
  2.1 0.0 copy-start.1
  2.1 1.9 %prep.1 = (bf16[4,4,192,192]{3,2,1,0:T(8,128)(2,1)S(1)}, bf16[4,2,240,128]{3,2,1,0:T(8,128)(2,1)S(1)}, bf16[4,2,240,128]{3,2,1,0:T(8,128)(2,1)S(1)}, bf16[2,4,24...) custom-call(bf16[4,4,160,192]{3,2,1,0:T(8,128)(2,1)S(1)} %copy-done.2, f32[4,192]{1,0:T(4,128)S(1)} %pad_maximum_fusion.1.k_ref), custom_call_target="tpu_custom_call" | custom-call | flops 24000000000 | bytes 3000000 | tf_op jit(solution)/shard_map/prep/pallas_call | solution.py:239
  4.0 0.8 %collective-permute-start = (bf16[4,2,240,128]{3,2,1,0:T(8,128)(2,1)S(1)}, bf16[4,2,240,128]{3,2,1,0:T(8,128)(2,1)S(1)}, u32[]{:S(2)}, u32[]{:S(2)}) collective-permute-start(bf16[4,2,240,128]{3,2,1,0:T(8,128)(2,1)S(1)} %get-tuple-element.29), channel_id=1, source_target_pairs={{0,1},{1,0},{2,3},{3,2},{4,5},{5,4},{6,7},{7,6},{8,9},{9,8},{10,11... | collective-permute-start | bytes 1474568 | tf_op jit(solution)/shard_map/ppermute | solution.py:266
  4.7 4.6 %collective-permute-start.3 = (bf16[4,2,240,128]{3,2,1,0:T(8,128)(2,1)S(1)}, bf16[4,2,240,128]{3,2,1,0:T(8,128)(2,1)S(1)}, u32[]{:S(2)}, u32[]{:S(2)}) collective-permute-start(bf16[4,2,240,128]{3,2,1,0:T(8,128)(2,1)S(1)} %get-tuple-element.32), channel_id=1, source_target_pairs={{1,2},{3,4},{5,6},{7,8},{9,10},{11,12},{13,14},{15,16},{17,18},{19... | collective-permute-start | bytes 1474568 | tf_op jit(solution)/shard_map/ppermute | solution.py:267
  9.3 0.0 collective-permute-done.a_ref
  9.3 3.2 %collective-permute-start.2 = (bf16[2,2,240,128]{3,2,1,0:T(8,128)(2,1)S(1)}, bf16[2,2,240,128]{3,2,1,0:T(8,128)(2,1)S(1)}, u32[]{:S(2)}, u32[]{:S(2)}) collective-permute-start(bf16[2,2,240,128]{3,2,1,0:T(8,128)(2,1)S(1)} %get-tuple-element.31), channel_id=1, source_target_pairs={{1,66},{3,68},{5,70},{7,72},{9,74},{11,76},{13,78},{15,80},{17,82}... | collective-permute-start | bytes 737288 | tf_op jit(solution)/shard_map/ppermute | solution.py:270
  12.5 1.3 %collective-permute-start.1 = (bf16[2,4,240,128]{3,2,1,0:T(8,128)(2,1)S(1)}, bf16[2,4,240,128]{3,2,1,0:T(8,128)(2,1)S(1)}, u32[]{:S(2)}, u32[]{:S(2)}) collective-permute-start(bf16[2,4,240,128]{3,2,1,0:T(8,128)(2,1)S(1)} %get-tuple-element.30), channel_id=1, source_target_pairs={{0,64},{1,65},{2,66},{3,67},{4,68},{5,69},{6,70},{7,71},{8,72},{9,... | collective-permute-start | bytes 1474568 | tf_op jit(solution)/shard_map/ppermute | solution.py:269
  13.8 0.0 copy-done
  13.8 0.0 copy-done.1
  13.8 11.5 %early.1 = (bf16[2,4,192,192]{3,2,1,0:T(8,128)(2,1)S(1)}, f32[2,4,160,192]{3,2,1,0:T(8,128)S(1)}, f32[4,2,160,192]{3,2,1,0:T(8,128)S(1)}, bf16[2,2,240,128]{3,2,1,0:T(8,128)(2,1)S(1)}, f32[2,2,160,192]{3,2,1,0:T(8,128)S(1)}) custom-call(bf16[4,4,192,192]{3,2,1,0:T(8,128)(2,1)S(1)} %get-tuple-element.33.own_ref, ...), custom_call_target="tpu_custom_call" | custom-call | flops 10800000000 | bytes 3000000 | tf_op jit(solution)/shard_map/early/pallas_call | solution.py:239
  25.3 0.0 collective-permute-done.3.bx_ref
  25.3 2.1 %mid.1 = (bf16[2,2,192,192]{3,2,1,0:T(8,128)(2,1)S(1)}, bf16[2,4,240,128]{3,2,1,0:T(8,128)(2,1)S(1)}) custom-call(bf16[4,2,240,128]{3,2,1,0:T(8,128)(2,1)S(1)} %collective-permute-done.3.bx_ref, f32[4,2,160,192]{3,2,1,0:T(8,128)S(1)} %get-tuple-element.35.i_ref, bf16[2,2,240,128]{3,2,1,0:T(8,128)(2,1)S(1)} %get-tuple-element.37.pe_ref, ...), custom_call_target="tpu_custom_call" | custom-call | flops 1800000000 | bytes 3000000 | tf_op jit(solution)/shard_map/mid/pallas_call | solution.py:239
  27.4 1.3 %collective-permute-start.5 = (bf16[2,4,240,128]{3,2,1,0:T(8,128)(2,1)S(1)}, bf16[2,4,240,128]{3,2,1,0:T(8,128)(2,1)S(1)}, u32[]{:S(2)}, u32[]{:S(2)}) collective-permute-start(bf16[2,4,240,128]{3,2,1,0:T(8,128)(2,1)S(1)} %get-tuple-element.47), channel_id=1, source_target_pairs={{0,64},{1,65},{2,66},{3,67},{4,68},{5,69},{6,70},{7,71},{8,72},{9,... | collective-permute-start | bytes 1474568 | tf_op jit(solution)/shard_map/ppermute | solution.py:282
  28.8 0.0 copy-start.3
  28.8 3.8 %wait.1 = (f32[2,2,160,192]{3,2,1,0:T(8,128)S(1)}, f32[2,4,160,192]{3,2,1,0:T(8,128)S(1)}) custom-call(bf16[4,2,240,128]{3,2,1,0:T(8,128)(2,1)S(1)} %collective-permute-done.3.bx_ref, f32[4,2,160,192]{3,2,1,0:T(8,128)S(1)} %get-tuple-element.35.i_ref, bf16[2,4,192,192]{3,2,1,0:T(8,128)(2,1)S(1)} %get-tuple-element.36.se_ref, ...), custom_call_target="tpu_custom_call" | custom-call | flops 12000000000 | bytes 3000000 | tf_op jit(solution)/shard_map/wait/pallas_call | solution.py:239
  32.6 0.0 collective-permute-done.2.d_ref
  32.6 0.0 collective-permute-done.1.t_ref
  32.7 3.3 %collective-permute-start.4 = (bf16[2,2,240,128]{3,2,1,0:T(8,128)(2,1)S(1)}, bf16[2,2,240,128]{3,2,1,0:T(8,128)(2,1)S(1)}, u32[]{:S(2)}, u32[]{:S(2)}) collective-permute-start(bf16[2,2,240,128]{3,2,1,0:T(8,128)(2,1)S(1)} %pad_maximum_fusion), channel_id=1, source_target_pairs={{0,1},{1,0},{2,3},{3,2},{4,5},{5,4},{6,7},{7,6},{8,9},{9,8},{10,11... | collective-permute-start | bytes 737288 | tf_op jit(solution)/shard_map/ppermute | solution.py:289
  36.0 1.1 %collective-permute-done.4.c_ref = bf16[2,2,240,128]{3,2,1,0:T(8,128)(2,1)S(1)} collective-permute-done((bf16[2,2,240,128]{3,2,1,0:T(8,128)(2,1)S(1)}, bf16[2,2,240,128]{3,2,1,0:T(8,128)(2,1)S(1)}, u32[]{:S(2)}, u32[]{:S(2)}) %collective-permute-start.4) | collective-permute-done | bytes 245792 | tf_op jit(solution)/shard_map/ppermute | solution.py:289
  37.1 0.0 copy-done.3
  37.1 10.0 %late.1 = (bf16[4,4,160,192]{3,2,1,0:T(8,128)(2,1)}, f32[2,4,160,192]{3,2,1,0:T(8,128)S(1)}) custom-call(bf16[2,4,240,128]{3,2,1,0:T(8,128)(2,1)S(1)} %collective-permute-done.1.t_ref, bf16[2,2,240,128]{3,2,1,0:T(8,128)(2,1)S(1)} %collective-permute-done.2.d_ref, bf16[2,2,240,128]{3,2,1,0:T(8,128)(2,1)S(1)} %collective-permute-done.4.c_ref, ...), custom_call_target="tpu_custom_call" | custom-call | flops 600000000 | bytes 3000000 | tf_op jit(solution)/shard_map/late/pallas_call | solution.py:239
  47.1 0.0 collective-permute-done.5.p_ref
  47.1 1.2 %add.1 = bf16[4,4,160,192]{3,2,1,0:T(8,128)(2,1)} custom-call(f32[2,4,160,192]{3,2,1,0:T(8,128)S(1)} %get-tuple-element.46.acc_ref, bf16[2,4,240,128]{3,2,1,0:T(8,128)(2,1)S(1)} %collective-permute-done.5.p_ref, bf16[4,4,160,192]{3,2,1,0:T(8,128)(2,1)} %get-tuple-element.48.full_ref), custom_call_target="tpu_custom_call", output_to_operand_aliasing={{}: (2, {})} | custom-call | flops 600000000 | bytes 3000000 | tf_op jit(solution)/shard_map/add/pallas_call | solution.py:239
  (2 shorter events, 0.0 us)
Async XLA Ops:
  0.7 1.3 %copy-start.2 = (bf16[4,4,160,192]{3,2,1,0:T(8,128)(2,1)S(1)}, bf16[4,4,160,192]{3,2,1,0:T(8,128)(2,1)}, u32[]{:S(2)}) copy-start(bf16[4,4,160,192]{3,2,1,0:T(8,128)(2,1)} %in_ref.1) | copy-start | bytes 2949124
  2.1 11.7 %copy-start = (bf16[3,3,3,192,192]{4,3,2,1,0:T(8,128)(2,1)S(1)}, bf16[3,3,3,192,192]{4,3,2,1,0:T(8,128)(2,1)}, u32[]{:S(2)}) copy-start(bf16[3,3,3,192,192]{4,3,2,1,0:T(8,128)(2,1)} %w1_ref.7) | copy-start | bytes 5971972
  2.1 11.7 %copy-start.1 = (bf16[3,3,3,192,192]{4,3,2,1,0:T(8,128)(2,1)S(1)}, bf16[3,3,3,192,192]{4,3,2,1,0:T(8,128)(2,1)}, u32[]{:S(2)}) copy-start(bf16[3,3,3,192,192]{4,3,2,1,0:T(8,128)(2,1)} %w2_ref.7) | copy-start | bytes 5971972
  4.0 5.3 %collective-permute-start = (bf16[4,2,240,128]{3,2,1,0:T(8,128)(2,1)S(1)}, bf16[4,2,240,128]{3,2,1,0:T(8,128)(2,1)S(1)}, u32[]{:S(2)}, u32[]{:S(2)}) collective-permute-start(bf16[4,2,240,128]{3,2,1,0:T(8,128)(2,1)S(1)} %get-tuple-element.29), channel_id=1, source_target_pairs={{0,1},{1,0},{2,3},{3,2},{4,5},{5,4},{6,7},{7,6},{8,9},{9,8},{10,11... | collective-permute-start | bytes 1474568 | tf_op jit(solution)/shard_map/ppermute | solution.py:266
  4.7 20.6 %collective-permute-start.3 = (bf16[4,2,240,128]{3,2,1,0:T(8,128)(2,1)S(1)}, bf16[4,2,240,128]{3,2,1,0:T(8,128)(2,1)S(1)}, u32[]{:S(2)}, u32[]{:S(2)}) collective-permute-start(bf16[4,2,240,128]{3,2,1,0:T(8,128)(2,1)S(1)} %get-tuple-element.32), channel_id=1, source_target_pairs={{1,2},{3,4},{5,6},{7,8},{9,10},{11,12},{13,14},{15,16},{17,18},{19... | collective-permute-start | bytes 1474568 | tf_op jit(solution)/shard_map/ppermute | solution.py:267
  9.3 23.3 %collective-permute-start.2 = (bf16[2,2,240,128]{3,2,1,0:T(8,128)(2,1)S(1)}, bf16[2,2,240,128]{3,2,1,0:T(8,128)(2,1)S(1)}, u32[]{:S(2)}, u32[]{:S(2)}) collective-permute-start(bf16[2,2,240,128]{3,2,1,0:T(8,128)(2,1)S(1)} %get-tuple-element.31), channel_id=1, source_target_pairs={{1,66},{3,68},{5,70},{7,72},{9,74},{11,76},{13,78},{15,80},{17,82}... | collective-permute-start | bytes 737288 | tf_op jit(solution)/shard_map/ppermute | solution.py:270
  12.5 20.2 %collective-permute-start.1 = (bf16[2,4,240,128]{3,2,1,0:T(8,128)(2,1)S(1)}, bf16[2,4,240,128]{3,2,1,0:T(8,128)(2,1)S(1)}, u32[]{:S(2)}, u32[]{:S(2)}) collective-permute-start(bf16[2,4,240,128]{3,2,1,0:T(8,128)(2,1)S(1)} %get-tuple-element.30), channel_id=1, source_target_pairs={{0,64},{1,65},{2,66},{3,67},{4,68},{5,69},{6,70},{7,71},{8,72},{9,... | collective-permute-start | bytes 1474568 | tf_op jit(solution)/shard_map/ppermute | solution.py:269
  27.4 19.7 %collective-permute-start.5 = (bf16[2,4,240,128]{3,2,1,0:T(8,128)(2,1)S(1)}, bf16[2,4,240,128]{3,2,1,0:T(8,128)(2,1)S(1)}, u32[]{:S(2)}, u32[]{:S(2)}) collective-permute-start(bf16[2,4,240,128]{3,2,1,0:T(8,128)(2,1)S(1)} %get-tuple-element.47), channel_id=1, source_target_pairs={{0,64},{1,65},{2,66},{3,67},{4,68},{5,69},{6,70},{7,71},{8,72},{9,... | collective-permute-start | bytes 1474568 | tf_op jit(solution)/shard_map/ppermute | solution.py:282
  28.8 8.4 %copy-start.3 = (bf16[4,4,160,192]{3,2,1,0:T(8,128)(2,1)S(1)}, bf16[4,4,160,192]{3,2,1,0:T(8,128)(2,1)}, u32[]{:S(2)}) copy-start(bf16[4,4,160,192]{3,2,1,0:T(8,128)(2,1)} %in_ref.1) | copy-start | bytes 2949124
  32.7 4.4 %collective-permute-start.4 = (bf16[2,2,240,128]{3,2,1,0:T(8,128)(2,1)S(1)}, bf16[2,2,240,128]{3,2,1,0:T(8,128)(2,1)S(1)}, u32[]{:S(2)}, u32[]{:S(2)}) collective-permute-start(bf16[2,2,240,128]{3,2,1,0:T(8,128)(2,1)S(1)} %pad_maximum_fusion), channel_id=1, source_target_pairs={{0,1},{1,0},{2,3},{3,2},{4,5},{5,4},{6,7},{7,6},{8,9},{9,8},{10,11... | collective-permute-start | bytes 737288 | tf_op jit(solution)/shard_map/ppermute | solution.py:289

commit v2 on v1

v2 whole, which is shorter than its diff:
```python
import jax
import jax.numpy as jnp
from jax import lax
from jax.experimental import pallas as pl
from jax.experimental.pallas import tpu as pltpu
from jax.sharding import PartitionSpec as P

BF = jnp.bfloat16
F32 = jnp.float32
C = 192
W = 160
S = 16
J = W // S
E = W + 2 * S
D = 240
MB = 2**20


def spread(rows, shift):
    n = lax.broadcasted_iota(jnp.int32, (rows, W), 0)
    c = lax.broadcasted_iota(jnp.int32, (rows, W), 1)
    return jnp.where((n & (S - 1)) * J + (n >> 4) - shift == c, 1.0, 0.0).astype(BF)


def gather():
    c = lax.broadcasted_iota(jnp.int32, (W, W), 0)
    n = lax.broadcasted_iota(jnp.int32, (W, W), 1)
    return jnp.where((n & (S - 1)) * J + (n >> 4) == c, 1.0, 0.0).astype(BF)


def flip(n, par):
    return n + par * (3 - 2 * n)


def act(v, gain):
    power = jnp.mean(v * v, axis=-1, keepdims=True)
    h = v * lax.rsqrt(power + 1e-06) * (gain * 0.5)
    return h + h * jnp.tanh(h)


def pack(v):
    hi = v[:, 128:]
    return jnp.concatenate([v[:, :128], jnp.concatenate([hi[:80], hi[80:]], axis=1)], axis=0)


def unpack(d):
    hi = d[W:]
    return jnp.concatenate([d[:W], jnp.concatenate([hi[:, :64], hi[:, 64:]], axis=0)], axis=1)


def edged(v):
    spot = lax.broadcasted_iota(jnp.int32, (S, C), 0)
    last = pltpu.roll(v[W - S :].astype(F32), 1, 0)
    head = pltpu.roll(v[:S].astype(F32), S - 1, 0)
    last = jnp.where(spot == 0, 0.0, last).astype(BF)
    head = jnp.where(spot == S - 1, 0.0, head).astype(BF)
    return jnp.concatenate([last, v, head], axis=0)


def place(ref, t, v, full, above=True):
    hi = full[:, 128:]
    ref[t, v, 0] = full[:, :128]
    on = jnp.concatenate([hi[S:], jnp.zeros((S, C - 128), BF)], axis=0)
    ref[t, v, 1] = jnp.concatenate([hi, on], axis=1)
    ref[t, v, 2, :, 0:64] = hi
    if above:
        ref[t, v - 1, 2, :, 64:128] = hi


def put(ref, at, v, above=True):
    place(ref, at[0], at[1], edged(v), above)


def taps(src, todo, w, par):
    ins, wts = [], []
    for t, v, a, ps in todo:
        at = {p: p + par * (2 - 2 * p) for p in ps}
        for p in ps:
            for q in range(3):
                ins.append(src[t, v + p, 0, S * q : S * q + W, :])
                wts.append(w[a, at[p], q, 0:128, :])
            ins.append(src[t, v + p, 1, 0:W, :])
            wts.append(jnp.concatenate([w[a, at[p], q, 128:C, :] for q in range(2)], axis=0))
        ps = list(ps)
        while ps:
            p = ps.pop(0)
            if ps:
                more = w[a, at[ps.pop(0)], 2, 128:C, :]
                ins.append(src[t, v + p, 2, 2 * S : E, :])
            else:
                more = jnp.zeros((C - 128, C), BF)
                ins.append(src[t, v + p, 1, 2 * S : E, :])
            wts.append(jnp.concatenate([w[a, at[p], 2, 128:C, :], more], axis=0))
    acc = jnp.zeros((W, C), F32)
    for i in range(0, len(ins), 2):
        left = jnp.concatenate(ins[i : i + 2], axis=1)
        right = jnp.concatenate(wts[i : i + 2], axis=0)
        acc = acc + jnp.dot(left, right, preferred_element_type=F32)
    return acc


def here():
    r = lax.axis_index("rows")
    keep = jnp.where((r == 0) | (r == lax.axis_size("rows") - 1), 0.0, 1.0).astype(F32)
    return r % 2, keep


def prep_kernel(x_ref, k_ref, own_ref, b_ref, a_ref, t_ref, d_ref):
    par, _ = here()
    m = spread(E, 1)
    g = k_ref[0:1, :]
    for t in range(4):
        for u in range(4):
            xp = jnp.dot(m, x_ref[t, flip(u, par)], preferred_element_type=F32)
            f = act(xp, g).astype(BF)
            own_ref[t, u, 0] = f[:, :128]
            hi = f[:, 128:]
            on = jnp.concatenate([hi[S:], jnp.zeros((S, C - 128), BF)], axis=0)
            own_ref[t, u, 1] = jnp.concatenate([hi, on], axis=1)
            own_ref[t, u, 2, :, 0:64] = hi
            if u:
                own_ref[t, u - 1, 2, :, 64:128] = hi
            d = pack(f[S : S + W])
            if u < 2:
                b_ref[t, u] = d
                if t >= 2:
                    d_ref[t - 2, u] = d
            else:
                a_ref[t, 3 - u] = d
            if t >= 2:
                t_ref[t - 2, u] = d


def early_kernel(own_ref, a_ref, w1_ref, w2_ref, k_ref, r_ref, o_ref, i_ref, pe_ref, pf_ref, x_ref, s_ref):
    par, _ = here()
    for t in range(4):
        for u in range(4):
            x_ref[t, u] = own_ref[t, u]
        for k in range(2):
            put(x_ref, (t, 4 + k), unpack(a_ref[t, k]))
    bias, g = k_ref[1:2, :], k_ref[2:3, :]
    all3 = (0, 1, 2)

    def row(k, _):
        for tau in range(2):
            acc = taps(x_ref, [(tau + a, k, a, all3) for a in range(3)], w1_ref, par)
            f = act(acc + bias, g).astype(BF)
            r_ref[tau, k] = f
            put(s_ref, (tau, k + 1), f)
        o_ref[0, k] = taps(x_ref, [(0, k, 2, all3)], w1_ref, par)
        o_ref[1, k] = taps(x_ref, [(a - 1, k, a, all3) for a in (1, 2)], w1_ref, par)
        return 0

    lax.fori_loop(0, 4, row, 0)
    for tau in range(4):
        ok = [a for a in range(3) if tau + a >= 2]
        i_ref[tau, 0] = taps(x_ref, [(tau + a - 2, -2, a, (2,)) for a in ok], w1_ref, par)
        i_ref[tau, 1] = taps(x_ref, [(tau + a - 2, -1, a, (1, 2)) for a in ok], w1_ref, par)
    for tau in range(2):
        ok = range(2 - tau)
        pf_ref[tau, 0] = taps(s_ref, [(tau + a, -1, a, (2,)) for a in ok], w2_ref, par)
        pf_ref[tau, 1] = taps(s_ref, [(tau + a, 0, a, (1, 2)) for a in ok], w2_ref, par)
        for u in range(2):
            acc = taps(s_ref, [(tau + a, u + 1, a, all3) for a in ok], w2_ref, par)
            pe_ref[tau, u] = pack(acc.astype(BF))


def mid_kernel(bx_ref, i_ref, pe_ref, pf_ref, w1_ref, w2_ref, k_ref, r_ref, p_ref, x_ref, s_ref):
    par, keep = here()
    for t in range(4):
        for k in (1, 0):
            put(x_ref, (t, 1 - k), unpack(bx_ref[t, k]), above=k == 0)
    bias, g = k_ref[1:2, :], k_ref[2:3, :]
    for tau in range(2):
        acc = taps(x_ref, [(tau + a, 0, a, (0, 1)) for a in range(3)], w1_ref, par)
        r_ref[tau, 0] = (act(acc + i_ref[tau + 2, 0] + bias, g) * keep).astype(BF)
        acc = taps(x_ref, [(tau + a, 1, a, (0,)) for a in range(3)], w1_ref, par)
        r_ref[tau, 1] = act(acc + i_ref[tau + 2, 1] + bias, g).astype(BF)
        for v in range(2):
            put(s_ref, (tau, v), r_ref[tau, v], above=v > 0)
    for tau in range(2):
        for u in range(2):
            p_ref[tau, u + 2] = pe_ref[tau, u]
        ok = range(2 - tau)
        acc = taps(s_ref, [(tau + a, 0, a, (0, 1)) for a in ok], w2_ref, par)
        p_ref[tau, 0] = pack((acc + pf_ref[tau, 0]).astype(BF))
        acc = taps(s_ref, [(tau + a, 1, a, (0,)) for a in ok], w2_ref, par)
        p_ref[tau, 1] = pack((acc + pf_ref[tau, 1]).astype(BF))


def wait_kernel(bx_ref, i_ref, re_ref, rm_ref, w1_ref, w2_ref, k_ref, in_ref, j_ref, z_ref, x_ref, s_ref):
    par, _ = here()
    for t in range(2):
        for k in (1, 0):
            put(x_ref, (t, 1 - k), unpack(bx_ref[t, k]), above=k == 0)
        for v in range(6):
            put(s_ref, (t, v), rm_ref[t, v] if v < 2 else re_ref[t, v - 2], above=v > 0)
    for tau in range(2):
        ok = [a for a in range(3) if tau + a >= 2]
        acc = taps(x_ref, [(tau + a - 2, 0, a, (0, 1)) for a in ok], w1_ref, par)
        j_ref[tau, 0] = acc + i_ref[tau, 0]
        acc = taps(x_ref, [(tau + a - 2, 1, a, (0,)) for a in ok], w1_ref, par)
        j_ref[tau, 1] = acc + i_ref[tau, 1]
    bias2 = k_ref[3:4, :]
    m = spread(W, 0)

    def row(u, _):
        at = flip(u, par)
        for tau in range(4):
            start = jnp.dot(m, in_ref[tau, at], preferred_element_type=F32) + bias2
            if tau >= 2:
                todo = [(f, u, f - tau + 4, (0, 1, 2)) for f in range(tau - 1)]
                start = start + taps(s_ref, todo, w2_ref, par)
            z_ref[tau, u] = start
        return 0

    lax.fori_loop(0, 4, row, 0)


def late_kernel(
    t_ref, d_ref, c_ref, o_ref, j_ref, z_ref, w1_ref, w2_ref, k_ref,
    out_ref, acc_ref, x_ref, s_ref, y_ref, n_ref, sem,
):
    par, keep = here()

    def fetch(v):
        for t in range(2):
            d = d_ref[t, 1 - v] if v < 2 else t_ref[t, v - 2] if v < 6 else c_ref[t, v - 6]
            put(x_ref, (t, v), unpack(d), above=v > 0)

    for v in range(3):
        fetch(v)
    bias, g = k_ref[1:2, :], k_ref[2:3, :]
    for v in range(6):
        if v:
            fetch(v + 2)
        for tau in range(2):
            acc = taps(x_ref, [(tau + a, v, a, (0, 1, 2)) for a in range(2 - tau)], w1_ref, par)
            f = act(acc + (j_ref[tau, v] if v < 2 else o_ref[tau, v - 2]) + bias, g)
            put(s_ref, (tau, v), (f if v else f * keep).astype(BF), above=v > 0)
    back = gather()

    def leave(tau, u):
        return pltpu.make_async_copy(n_ref.at[tau, u], out_ref.at[tau + 2, flip(u, par)], sem.at[tau, u])

    def finish(u):
        for tau in range(2):
            n_ref[tau, u] = jnp.dot(back, y_ref[tau, u], preferred_element_type=F32).astype(BF)
            leave(tau, u).start()

    for u in range(4):
        for tau in range(4):
            frames = [f for f in range(2) if 0 <= f - tau + 2 <= 2]
            acc = taps(s_ref, [(f, u, f - tau + 2, (0, 1, 2)) for f in frames], w2_ref, par) + z_ref[tau, u]
            if tau < 2:
                acc_ref[tau, u] = acc
            else:
                y_ref[tau - 2, u] = acc.astype(BF)
        if u:
            finish(u - 1)
    finish(3)
    for u in range(4):
        for tau in range(2):
            leave(tau, u).wait()


def add_kernel(acc_ref, p_ref, full_ref, out_ref, n_ref, sem):
    par, _ = here()
    back = gather()
    sent = []
    for t in range(2):
        for u in range(4):
            y = (acc_ref[t, u] + unpack(p_ref[t, u]).astype(F32)).astype(BF)
            n_ref[t, u] = jnp.dot(back, y, preferred_element_type=F32).astype(BF)
            copy = pltpu.make_async_copy(n_ref.at[t, u], out_ref.at[t, flip(u, par)], sem.at[t, u])
            copy.start()
            sent.append(copy)
    for copy in sent:
        copy.wait()


VMEM = pl.BlockSpec(memory_space=pltpu.VMEM)
ANY = pl.BlockSpec(memory_space=pl.ANY)


def call(kernel, name, ins, outs, scratch, units, limit=32, in_specs=None, out_specs=None, alias={}):
    return pl.pallas_call(
        kernel,
        in_specs=in_specs or [VMEM] * len(ins),
        out_specs=out_specs or [VMEM] * len(outs),
        out_shape=[jax.ShapeDtypeStruct(s, d) for s, d in outs],
        scratch_shapes=scratch,
        compiler_params=pltpu.CompilerParams(vmem_limit_bytes=limit * MB),
        cost_estimate=pl.CostEstimate(
            flops=int(units * 6e8), bytes_accessed=3_000_000, transcendentals=500_000
        ),
        input_output_aliases=alias,
        name=name,
    )(*ins)


def local(frames_in, gain_one, conv_one, bias_one, gain_two, conv_two, bias_two):
    n = lax.axis_size("rows")
    near = [(i, i ^ 1) for i in range(n)]
    far = [(i, i + 1) for i in range(1, n - 1, 2)] + [(i + 1, i) for i in range(1, n - 1, 2)]
    diag = [(i, n + j) for i, j in far]
    kv = jnp.stack([gain_one, bias_one, gain_two, bias_two])

    own, bs, as_, ts, ds = call(
        prep_kernel, "prep", [frames_in, kv],
        [((4, 4, 3, E, 128), BF), ((4, 2, D, 128), BF), ((4, 2, D, 128), BF), ((2, 4, D, 128), BF), ((2, 2, D, 128), BF)],
        [], 40,
    )
    ar = lax.ppermute(as_, "rows", near)
    br = lax.ppermute(bs, "rows", far)
    ts, ds, ar = lax.optimization_barrier((ts, ds, ar))
    tr = lax.ppermute(ts, "tm", [(0, 1)])
    dr = lax.ppermute(ds, ("tm", "rows"), diag)

    se, oacc, iacc, pe, pf = call(
        early_kernel, "early", [own, ar, conv_one, conv_two, kv],
        [((2, 4, W, C), BF), ((2, 4, W, C), F32), ((4, 2, W, C), F32), ((2, 2, D, 128), BF), ((2, 2, W, C), F32)],
        [pltpu.VMEM((4, 6, 3, E, 128), BF), pltpu.VMEM((2, 5, 3, E, 128), BF)], 18,
    )
    sm, ps = call(
        mid_kernel, "mid", [br, iacc, pe, pf, conv_one, conv_two, kv],
        [((2, 2, W, C), BF), ((2, 4, D, 128), BF)],
        [pltpu.VMEM((4, 2, 3, E, 128), BF), pltpu.VMEM((2, 2, 3, E, 128), BF)], 3,
    )
    pr = lax.ppermute(ps, "tm", [(0, 1)])
    jacc, zacc = call(
        wait_kernel, "wait", [br, iacc, se, sm, conv_one, conv_two, kv, frames_in],
        [((2, 2, W, C), F32), ((4, 4, W, C), F32)],
        [pltpu.VMEM((2, 2, 3, E, 128), BF), pltpu.VMEM((2, 6, 3, E, 128), BF)], 20,
    )
    tr, dr, zacc = lax.optimization_barrier((tr, dr, zacc))
    cr = lax.ppermute(jnp.stack([tr[:, 3], tr[:, 2]], axis=1), "rows", near)
    out, acc = call(
        late_kernel, "late", [tr, dr, cr, oacc, jacc, zacc, conv_one, conv_two, kv],
        [((4, 4, W, C), BF), ((2, 4, W, C), F32)],
        [
            pltpu.VMEM((2, 8, 3, E, 128), BF), pltpu.VMEM((2, 6, 3, E, 128), BF), pltpu.VMEM((2, 4, W, C), BF),
            pltpu.VMEM((2, 4, W, C), BF), pltpu.SemaphoreType.DMA((2, 4)),
        ],
        1, out_specs=[ANY, VMEM],
    )
    (out,) = call(
        add_kernel, "add", [acc, pr, out], [((4, 4, W, C), BF)],
        [pltpu.VMEM((2, 4, W, C), BF), pltpu.SemaphoreType.DMA((2, 4))],
        1, in_specs=[VMEM, VMEM, ANY], out_specs=[ANY], alias={2: 0},
    )
    return out


def solution(mesh):
    in_specs = (P("tm", "rows", "roll", None), P(), P(), P(), P(), P(), P())
    out_specs = P("tm", "rows", "roll", None)
    return jax.shard_map(local, mesh=mesh, in_specs=in_specs, out_specs=out_specs, check_vma=False)
```

time: 48.7 us -> 47 us (0.965)
  the two profiles are of different devices: /device:TPU:65 before, /device:TPU:99 now
where the time goes in v2:
time: 47 us; the launch traced here: 46.8 us
  Pallas kernels  27.7 us (59%)
  starting transfers between devices  14.9 us (32%)
  waiting for transfers between devices  1.78 us (4%)
  local copies, waits for them, and re-layouts  1.34 us (3%)
  other arithmetic  0.76 us (2%)
    pallas_call x6, Pallas kernels, call(): pl.pallas_call(kernel, in_specs=in_specs or [VMEM] * len(ins), out_specs=...  27.7 us
    ppermute x1, starting transfers between devices, local(): cr = lax.ppermute(jnp.stack([tr[:, 3], tr[:, 2]], axis=1), 'rows', near)  6.64 us
    ppermute x1, starting transfers between devices, local(): br = lax.ppermute(bs, 'rows', far)  3.65 us
    unnamed x8, local copies, waits for them, and re-layouts  1.32 us
    ppermute x1, starting transfers between devices, local(): dr = lax.ppermute(ds, ('tm', 'rows'), diag)  1.29 us
    ppermute x1, starting transfers between devices, local(): tr = lax.ppermute(ts, 'tm', [(0, 1)])  1.29 us
    ppermute x1, starting transfers between devices, local(): pr = lax.ppermute(ps, 'tm', [(0, 1)])  1.29 us
    ppermute x1, waiting for transfers between devices, local(): cr = lax.ppermute(jnp.stack([tr[:, 3], tr[:, 2]], axis=1), 'rows', near)  1.14 us
  transfers between devices with their start and end apart: 6, of which 2 were waited for; matrix products, arithmetic and copies ran while one was open for 0% of the time, Pallas kernels for 51%

profile of v2, /device:TPU:99, one launch (start us, length us, event | category | flops | bytes accessed | tf_op | source)
XLA Modules:
  0.0 46.8 jit_solution(12975787331457540861)
XLA Ops:
  0.0 0.7 %pad_maximum_fusion.1.k_ref = f32[4,192]{1,0:T(4,128)S(1)} fusion(f32[1,192]{1,0:T(1,128)} %bitcast.4, f32[1,192]{1,0:T(1,128)} %bitcast.5, f32[1,192]{1,0:T(1,128)} %bitcast.6, f32[1,192]{1,0:T(1,128)} %bitcast.7), kind=kLoop, calls=%fused_computation.1 | loop fusion | flops 2304 | bytes 6144 | tf_op jit(solution)/shard_map/stack | solution.py:307
  0.7 0.0 copy-start.2
  0.8 1.3 %copy-done.2 = bf16[4,4,160,192]{3,2,1,0:T(8,128)(2,1)S(1)} copy-done((bf16[4,4,160,192]{3,2,1,0:T(8,128)(2,1)S(1)}, bf16[4,4,160,192]{3,2,1,0:T(8,128)(2,1)}, u32[]{:S(2)}) %copy-start.2) | copy-done | bytes 983064
  2.1 0.0 copy-start
  2.1 0.0 copy-start.1
  2.1 2.8 %prep.1 = (bf16[4,4,3,192,128]{4,3,2,1,0:T(8,128)(2,1)S(1)}, bf16[4,2,240,128]{3,2,1,0:T(8,128)(2,1)S(1)}, bf16[4,2,240,128]{3,2,1,0:T(8,128)(2,1)S(1)}, bf16[2,...) custom-call(bf16[4,4,160,192]{3,2,1,0:T(8,128)(2,1)S(1)} %copy-done.2, f32[4,192]{1,0:T(4,128)S(1)} %pad_maximum_fusion.1.k_ref), custom_call_target="tpu_custom_call" | custom-call | flops 24000000000 | bytes 3000000 | tf_op jit(solution)/shard_map/prep/pallas_call | solution.py:287
  4.8 0.8 %collective-permute-start = (bf16[4,2,240,128]{3,2,1,0:T(8,128)(2,1)S(1)}, bf16[4,2,240,128]{3,2,1,0:T(8,128)(2,1)S(1)}, u32[]{:S(2)}, u32[]{:S(2)}) collective-permute-start(bf16[4,2,240,128]{3,2,1,0:T(8,128)(2,1)S(1)} %get-tuple-element.29), channel_id=1, source_target_pairs={{0,1},{1,0},{2,3},{3,2},{4,5},{5,4},{6,7},{7,6},{8,9},{9,8},{10,11... | collective-permute-start | bytes 1474568 | tf_op jit(solution)/shard_map/ppermute | solution.py:314
  5.6 3.7 %collective-permute-start.3 = (bf16[4,2,240,128]{3,2,1,0:T(8,128)(2,1)S(1)}, bf16[4,2,240,128]{3,2,1,0:T(8,128)(2,1)S(1)}, u32[]{:S(2)}, u32[]{:S(2)}) collective-permute-start(bf16[4,2,240,128]{3,2,1,0:T(8,128)(2,1)S(1)} %get-tuple-element.32), channel_id=1, source_target_pairs={{1,2},{3,4},{5,6},{7,8},{9,10},{11,12},{13,14},{15,16},{17,18},{19... | collective-permute-start | bytes 1474568 | tf_op jit(solution)/shard_map/ppermute | solution.py:315
  9.2 0.0 collective-permute-done.a_ref
  9.3 1.3 %collective-permute-start.2 = (bf16[2,2,240,128]{3,2,1,0:T(8,128)(2,1)S(1)}, bf16[2,2,240,128]{3,2,1,0:T(8,128)(2,1)S(1)}, u32[]{:S(2)}, u32[]{:S(2)}) collective-permute-start(bf16[2,2,240,128]{3,2,1,0:T(8,128)(2,1)S(1)} %get-tuple-element.31), channel_id=1, source_target_pairs={{1,66},{3,68},{5,70},{7,72},{9,74},{11,76},{13,78},{15,80},{17,82}... | collective-permute-start | bytes 737288 | tf_op jit(solution)/shard_map/ppermute | solution.py:318
  10.6 1.3 %collective-permute-start.1 = (bf16[2,4,240,128]{3,2,1,0:T(8,128)(2,1)S(1)}, bf16[2,4,240,128]{3,2,1,0:T(8,128)(2,1)S(1)}, u32[]{:S(2)}, u32[]{:S(2)}) collective-permute-start(bf16[2,4,240,128]{3,2,1,0:T(8,128)(2,1)S(1)} %get-tuple-element.30), channel_id=1, source_target_pairs={{0,64},{1,65},{2,66},{3,67},{4,68},{5,69},{6,70},{7,71},{8,72},{9,... | collective-permute-start | bytes 1474568 | tf_op jit(solution)/shard_map/ppermute | solution.py:317
  11.9 0.0 copy-done
  11.9 0.0 copy-done.1
  11.9 10.1 %early.1 = (bf16[2,4,160,192]{3,2,1,0:T(8,128)(2,1)S(1)}, f32[2,4,160,192]{3,2,1,0:T(8,128)S(1)}, f32[4,2,160,192]{3,2,1,0:T(8,128)S(1)}, bf16[2,2,240,128]{3,2,1,0:T(8,128)(2,1)S(1)}, f32[2,2,160,192]{3,2,1,0:T(8,128)S(1)}) custom-call(bf16[4,4,3,192,128]{4,3,2,1,0:T(8,128)(2,1)S(1)} %get-tuple-element.33.own_ref, ...), custom_call_target="tpu_custom_call" | custom-call | flops 10800000000 | bytes 3000000 | tf_op jit(solution)/shard_map/early/pallas_call | solution.py:287
  21.9 0.6 %collective-permute-done.3.bx_ref = bf16[4,2,240,128]{3,2,1,0:T(8,128)(2,1)S(1)} collective-permute-done((bf16[4,2,240,128]{3,2,1,0:T(8,128)(2,1)S(1)}, bf16[4,2,240,128]{3,2,1,0:T(8,128)(2,1)S(1)}, u32[]{:S(2)}, u32[]{:S(2)}) %collective-permute-start.3) | collective-permute-done | bytes 491552 | tf_op jit(solution)/shard_map/ppermute | solution.py:315
  22.6 0.0 copy-start.3
  22.6 2.1 %mid.1 = (bf16[2,2,160,192]{3,2,1,0:T(8,128)(2,1)S(1)}, bf16[2,4,240,128]{3,2,1,0:T(8,128)(2,1)S(1)}) custom-call(bf16[4,2,240,128]{3,2,1,0:T(8,128)(2,1)S(1)} %collective-permute-done.3.bx_ref, f32[4,2,160,192]{3,2,1,0:T(8,128)S(1)} %get-tuple-element.35.i_ref, bf16[2,2,240,128]{3,2,1,0:T(8,128)(2,1)S(1)} %get-tuple-element.37.pe_ref, ...), custom_call_target="tpu_custom_call" | custom-call | flops 1800000000 | bytes 3000000 | tf_op jit(solution)/shard_map/mid/pallas_call | solution.py:287
  24.6 1.3 %collective-permute-start.5 = (bf16[2,4,240,128]{3,2,1,0:T(8,128)(2,1)S(1)}, bf16[2,4,240,128]{3,2,1,0:T(8,128)(2,1)S(1)}, u32[]{:S(2)}, u32[]{:S(2)}) collective-permute-start(bf16[2,4,240,128]{3,2,1,0:T(8,128)(2,1)S(1)} %get-tuple-element.47), channel_id=1, source_target_pairs={{0,64},{1,65},{2,66},{3,67},{4,68},{5,69},{6,70},{7,71},{8,72},{9,... | collective-permute-start | bytes 1474568 | tf_op jit(solution)/shard_map/ppermute | solution.py:330
  25.9 0.0 copy-done.3
  26.0 3.7 %wait.1 = (f32[2,2,160,192]{3,2,1,0:T(8,128)S(1)}, f32[4,4,160,192]{3,2,1,0:T(8,128)S(1)}) custom-call(bf16[4,2,240,128]{3,2,1,0:T(8,128)(2,1)S(1)} %collective-permute-done.3.bx_ref, f32[4,2,160,192]{3,2,1,0:T(8,128)S(1)} %get-tuple-element.35.i_ref, bf16[2,4,160,192]{3,2,1,0:T(8,128)(2,1)S(1)} %get-tuple-element.36.re_ref, ...), custom_call_target="tpu_custom_call" | custom-call | flops 12000000000 | bytes 3000000 | tf_op jit(solution)/shard_map/wait/pallas_call | solution.py:287
  29.7 0.0 collective-permute-done.2.d_ref
  29.7 0.0 collective-permute-done.1.t_ref
  29.8 6.6 %collective-permute-start.4 = (bf16[2,2,240,128]{3,2,1,0:T(8,128)(2,1)S(1)}, bf16[2,2,240,128]{3,2,1,0:T(8,128)(2,1)S(1)}, u32[]{:S(2)}, u32[]{:S(2)}) collective-permute-start(bf16[2,2,240,128]{3,2,1,0:T(8,128)(2,1)S(1)} %pad_maximum_fusion), channel_id=1, source_target_pairs={{0,1},{1,0},{2,3},{3,2},{4,5},{5,4},{6,7},{7,6},{8,9},{9,8},{10,11... | collective-permute-start | bytes 737288 | tf_op jit(solution)/shard_map/ppermute | solution.py:337
  36.4 1.1 %collective-permute-done.4.c_ref = bf16[2,2,240,128]{3,2,1,0:T(8,128)(2,1)S(1)} collective-permute-done((bf16[2,2,240,128]{3,2,1,0:T(8,128)(2,1)S(1)}, bf16[2,2,240,128]{3,2,1,0:T(8,128)(2,1)S(1)}, u32[]{:S(2)}, u32[]{:S(2)}) %collective-permute-start.4) | collective-permute-done | bytes 245792 | tf_op jit(solution)/shard_map/ppermute | solution.py:337
  37.5 7.9 %late.1 = (bf16[4,4,160,192]{3,2,1,0:T(8,128)(2,1)}, f32[2,4,160,192]{3,2,1,0:T(8,128)S(1)}) custom-call(bf16[2,4,240,128]{3,2,1,0:T(8,128)(2,1)S(1)} %collective-permute-done.1.t_ref, bf16[2,2,240,128]{3,2,1,0:T(8,128)(2,1)S(1)} %collective-permute-done.2.d_ref, bf16[2,2,240,128]{3,2,1,0:T(8,128)(2,1)S(1)} %collective-permute-done.4.c_ref, ...), custom_call_target="tpu_custom_call" | custom-call | flops 600000000 | bytes 3000000 | tf_op jit(solution)/shard_map/late/pallas_call | solution.py:287
  45.5 0.0 collective-permute-done.5.p_ref
  45.5 1.2 %add.1 = bf16[4,4,160,192]{3,2,1,0:T(8,128)(2,1)} custom-call(f32[2,4,160,192]{3,2,1,0:T(8,128)S(1)} %get-tuple-element.46.acc_ref, bf16[2,4,240,128]{3,2,1,0:T(8,128)(2,1)S(1)} %collective-permute-done.5.p_ref, bf16[4,4,160,192]{3,2,1,0:T(8,128)(2,1)} %get-tuple-element.48.full_ref), custom_call_target="tpu_custom_call", output_to_operand_aliasing={{}: (2, {})} | custom-call | flops 600000000 | bytes 3000000 | tf_op jit(solution)/shard_map/add/pallas_call | solution.py:287
  (2 shorter events, 0.0 us)
Async XLA Ops:
  0.7 1.3 %copy-start.2 = (bf16[4,4,160,192]{3,2,1,0:T(8,128)(2,1)S(1)}, bf16[4,4,160,192]{3,2,1,0:T(8,128)(2,1)}, u32[]{:S(2)}) copy-start(bf16[4,4,160,192]{3,2,1,0:T(8,128)(2,1)} %in_ref.1) | copy-start | bytes 2949124
  2.1 9.8 %copy-start = (bf16[3,3,3,192,192]{4,3,2,1,0:T(8,128)(2,1)S(1)}, bf16[3,3,3,192,192]{4,3,2,1,0:T(8,128)(2,1)}, u32[]{:S(2)}) copy-start(bf16[3,3,3,192,192]{4,3,2,1,0:T(8,128)(2,1)} %w1_ref.7) | copy-start | bytes 5971972
  2.1 9.8 %copy-start.1 = (bf16[3,3,3,192,192]{4,3,2,1,0:T(8,128)(2,1)S(1)}, bf16[3,3,3,192,192]{4,3,2,1,0:T(8,128)(2,1)}, u32[]{:S(2)}) copy-start(bf16[3,3,3,192,192]{4,3,2,1,0:T(8,128)(2,1)} %w2_ref.7) | copy-start | bytes 5971972
  4.8 4.4 %collective-permute-start = (bf16[4,2,240,128]{3,2,1,0:T(8,128)(2,1)S(1)}, bf16[4,2,240,128]{3,2,1,0:T(8,128)(2,1)S(1)}, u32[]{:S(2)}, u32[]{:S(2)}) collective-permute-start(bf16[4,2,240,128]{3,2,1,0:T(8,128)(2,1)S(1)} %get-tuple-element.29), channel_id=1, source_target_pairs={{0,1},{1,0},{2,3},{3,2},{4,5},{5,4},{6,7},{7,6},{8,9},{9,8},{10,11... | collective-permute-start | bytes 1474568 | tf_op jit(solution)/shard_map/ppermute | solution.py:314
  5.6 17.0 %collective-permute-start.3 = (bf16[4,2,240,128]{3,2,1,0:T(8,128)(2,1)S(1)}, bf16[4,2,240,128]{3,2,1,0:T(8,128)(2,1)S(1)}, u32[]{:S(2)}, u32[]{:S(2)}) collective-permute-start(bf16[4,2,240,128]{3,2,1,0:T(8,128)(2,1)S(1)} %get-tuple-element.32), channel_id=1, source_target_pairs={{1,2},{3,4},{5,6},{7,8},{9,10},{11,12},{13,14},{15,16},{17,18},{19... | collective-permute-start | bytes 1474568 | tf_op jit(solution)/shard_map/ppermute | solution.py:315
  9.3 20.4 %collective-permute-start.2 = (bf16[2,2,240,128]{3,2,1,0:T(8,128)(2,1)S(1)}, bf16[2,2,240,128]{3,2,1,0:T(8,128)(2,1)S(1)}, u32[]{:S(2)}, u32[]{:S(2)}) collective-permute-start(bf16[2,2,240,128]{3,2,1,0:T(8,128)(2,1)S(1)} %get-tuple-element.31), channel_id=1, source_target_pairs={{1,66},{3,68},{5,70},{7,72},{9,74},{11,76},{13,78},{15,80},{17,82}... | collective-permute-start | bytes 737288 | tf_op jit(solution)/shard_map/ppermute | solution.py:318
  10.6 19.1 %collective-permute-start.1 = (bf16[2,4,240,128]{3,2,1,0:T(8,128)(2,1)S(1)}, bf16[2,4,240,128]{3,2,1,0:T(8,128)(2,1)S(1)}, u32[]{:S(2)}, u32[]{:S(2)}) collective-permute-start(bf16[2,4,240,128]{3,2,1,0:T(8,128)(2,1)S(1)} %get-tuple-element.30), channel_id=1, source_target_pairs={{0,64},{1,65},{2,66},{3,67},{4,68},{5,69},{6,70},{7,71},{8,72},{9,... | collective-permute-start | bytes 1474568 | tf_op jit(solution)/shard_map/ppermute | solution.py:317
  22.6 3.4 %copy-start.3 = (bf16[4,4,160,192]{3,2,1,0:T(8,128)(2,1)S(1)}, bf16[4,4,160,192]{3,2,1,0:T(8,128)(2,1)}, u32[]{:S(2)}) copy-start(bf16[4,4,160,192]{3,2,1,0:T(8,128)(2,1)} %in_ref.1) | copy-start | bytes 2949124
  24.6 20.8 %collective-permute-start.5 = (bf16[2,4,240,128]{3,2,1,0:T(8,128)(2,1)S(1)}, bf16[2,4,240,128]{3,2,1,0:T(8,128)(2,1)S(1)}, u32[]{:S(2)}, u32[]{:S(2)}) collective-permute-start(bf16[2,4,240,128]{3,2,1,0:T(8,128)(2,1)S(1)} %get-tuple-element.47), channel_id=1, source_target_pairs={{0,64},{1,65},{2,66},{3,67},{4,68},{5,69},{6,70},{7,71},{8,72},{9,... | collective-permute-start | bytes 1474568 | tf_op jit(solution)/shard_map/ppermute | solution.py:330
  29.8 7.8 %collective-permute-start.4 = (bf16[2,2,240,128]{3,2,1,0:T(8,128)(2,1)S(1)}, bf16[2,2,240,128]{3,2,1,0:T(8,128)(2,1)S(1)}, u32[]{:S(2)}, u32[]{:S(2)}) collective-permute-start(bf16[2,2,240,128]{3,2,1,0:T(8,128)(2,1)S(1)} %pad_maximum_fusion), channel_id=1, source_target_pairs={{0,1},{1,0},{2,3},{3,2},{4,5},{5,4},{6,7},{7,6},{8,9},{9,8},{10,11... | collective-permute-start | bytes 737288 | tf_op jit(solution)/shard_map/ppermute | solution.py:337

commit v3 on v2

--- a/solution.py
+++ b/solution.py
@@ -105,6 +105,14 @@
     return r % 2, keep
 
 
+def has_next():
+    return lax.axis_index("tm") < lax.axis_size("tm") - 1
+
+
+def has_last():
+    return lax.axis_index("tm") > 0
+
+
 def prep_kernel(x_ref, k_ref, own_ref, b_ref, a_ref, t_ref, d_ref):
     par, _ = here()
     m = spread(E, 1)
@@ -113,13 +121,7 @@
         for u in range(4):
             xp = jnp.dot(m, x_ref[t, flip(u, par)], preferred_element_type=F32)
             f = act(xp, g).astype(BF)
-            own_ref[t, u, 0] = f[:, :128]
-            hi = f[:, 128:]
-            on = jnp.concatenate([hi[S:], jnp.zeros((S, C - 128), BF)], axis=0)
-            own_ref[t, u, 1] = jnp.concatenate([hi, on], axis=1)
-            own_ref[t, u, 2, :, 0:64] = hi
-            if u:
-                own_ref[t, u - 1, 2, :, 64:128] = hi
+            own_ref[t, u] = f
             d = pack(f[S : S + W])
             if u < 2:
                 b_ref[t, u] = d
@@ -135,7 +137,7 @@
     par, _ = here()
     for t in range(4):
         for u in range(4):
-            x_ref[t, u] = own_ref[t, u]
+            place(x_ref, t, u, own_ref[t, u], above=u > 0)
         for k in range(2):
             put(x_ref, (t, 4 + k), unpack(a_ref[t, k]))
     bias, g = k_ref[1:2, :], k_ref[2:3, :]
@@ -156,13 +158,16 @@
         ok = [a for a in range(3) if tau + a >= 2]
         i_ref[tau, 0] = taps(x_ref, [(tau + a - 2, -2, a, (2,)) for a in ok], w1_ref, par)
         i_ref[tau, 1] = taps(x_ref, [(tau + a - 2, -1, a, (1, 2)) for a in ok], w1_ref, par)
-    for tau in range(2):
-        ok = range(2 - tau)
-        pf_ref[tau, 0] = taps(s_ref, [(tau + a, -1, a, (2,)) for a in ok], w2_ref, par)
-        pf_ref[tau, 1] = taps(s_ref, [(tau + a, 0, a, (1, 2)) for a in ok], w2_ref, par)
-        for u in range(2):
-            acc = taps(s_ref, [(tau + a, u + 1, a, all3) for a in ok], w2_ref, par)
-            pe_ref[tau, u] = pack(acc.astype(BF))
+
+    @pl.when(has_next())
+    def _():
+        for tau in range(2):
+            ok = range(2 - tau)
+            pf_ref[tau, 0] = taps(s_ref, [(tau + a, -1, a, (2,)) for a in ok], w2_ref, par)
+            pf_ref[tau, 1] = taps(s_ref, [(tau + a, 0, a, (1, 2)) for a in ok], w2_ref, par)
+            for u in range(2):
+                acc = taps(s_ref, [(tau + a, u + 1, a, all3) for a in ok], w2_ref, par)
+                pe_ref[tau, u] = pack(acc.astype(BF))
 
 
 def mid_kernel(bx_ref, i_ref, pe_ref, pf_ref, w1_ref, w2_ref, k_ref, r_ref, p_ref, x_ref, s_ref):
@@ -176,16 +181,20 @@
         r_ref[tau, 0] = (act(acc + i_ref[tau + 2, 0] + bias, g) * keep).astype(BF)
         acc = taps(x_ref, [(tau + a, 1, a, (0,)) for a in range(3)], w1_ref, par)
         r_ref[tau, 1] = act(acc + i_ref[tau + 2, 1] + bias, g).astype(BF)
-        for v in range(2):
-            put(s_ref, (tau, v), r_ref[tau, v], above=v > 0)
-    for tau in range(2):
-        for u in range(2):
-            p_ref[tau, u + 2] = pe_ref[tau, u]
-        ok = range(2 - tau)
-        acc = taps(s_ref, [(tau + a, 0, a, (0, 1)) for a in ok], w2_ref, par)
-        p_ref[tau, 0] = pack((acc + pf_ref[tau, 0]).astype(BF))
-        acc = taps(s_ref, [(tau + a, 1, a, (0,)) for a in ok], w2_ref, par)
-        p_ref[tau, 1] = pack((acc + pf_ref[tau, 1]).astype(BF))
+
+    @pl.when(has_next())
+    def _():
+        for tau in range(2):
+            for v in range(2):
+                put(s_ref, (tau, v), r_ref[tau, v], above=v > 0)
+        for tau in range(2):
+            for u in range(2):
+                p_ref[tau, u + 2] = pe_ref[tau, u]
+            ok = range(2 - tau)
+            acc = taps(s_ref, [(tau + a, 0, a, (0, 1)) for a in ok], w2_ref, par)
+            p_ref[tau, 0] = pack((acc + pf_ref[tau, 0]).astype(BF))
+            acc = taps(s_ref, [(tau + a, 1, a, (0,)) for a in ok], w2_ref, par)
+            p_ref[tau, 1] = pack((acc + pf_ref[tau, 1]).astype(BF))
 
 
 def wait_kernel(bx_ref, i_ref, re_ref, rm_ref, w1_ref, w2_ref, k_ref, in_ref, j_ref, z_ref, x_ref, s_ref):
@@ -217,27 +226,56 @@
     lax.fori_loop(0, 4, row, 0)
 
 
-def late_kernel(
-    t_ref, d_ref, c_ref, o_ref, j_ref, z_ref, w1_ref, w2_ref, k_ref,
-    out_ref, acc_ref, x_ref, s_ref, y_ref, n_ref, sem,
-):
+def recent(x_ref, r_ref, o_ref, k_ref, w1_ref, par, rows, off, fetch, scale):
+    bias, g = k_ref[1:2, :], k_ref[2:3, :]
+
+    @pl.when(has_last())
+    def _():
+        for v in (rows[0] - off, rows[0] - off + 1):
+            fetch(v)
+        for v in rows:
+            fetch(v - off + 2)
+            for tau in range(2):
+                acc = taps(x_ref, [(tau + a, v - off, a, (0, 1, 2)) for a in range(2 - tau)], w1_ref, par)
+                r_ref[tau, v - off] = scale(v, act(acc + o_ref(tau, v) + bias, g)).astype(BF)
+
+    @pl.when(jnp.logical_not(has_last()))
+    def _():
+        for v in rows:
+            for tau in range(2):
+                r_ref[tau, v - off] = scale(v, act(o_ref(tau, v) + bias, g)).astype(BF)
+
+
+def late_kernel(t_ref, d_ref, o_ref, j_ref, w1_ref, k_ref, r_ref, x_ref):
     par, keep = here()
 
     def fetch(v):
         for t in range(2):
-            d = d_ref[t, 1 - v] if v < 2 else t_ref[t, v - 2] if v < 6 else c_ref[t, v - 6]
-            put(x_ref, (t, v), unpack(d), above=v > 0)
-
-    for v in range(3):
-        fetch(v)
-    bias, g = k_ref[1:2, :], k_ref[2:3, :]
+            put(x_ref, (t, v), unpack(d_ref[t, 1 - v] if v < 2 else t_ref[t, v - 2]), above=v > 0)
+
+    recent(
+        x_ref, r_ref, lambda tau, v: j_ref[tau, v] if v < 2 else o_ref[tau, v - 2], k_ref, w1_ref, par,
+        range(4), 0, fetch, lambda v, f: f if v else f * keep,
+    )
+
+
+def last_kernel(
+    t_ref, c_ref, o_ref, r_ref, z_ref, w1_ref, w2_ref, k_ref,
+    out_ref, acc_ref, x_ref, s_ref, q_ref, y_ref, n_ref, sem,
+):
+    par, _ = here()
+
+    def fetch(v):
+        for t in range(2):
+            put(x_ref, (t, v), unpack(t_ref[t, v + 2] if v < 2 else c_ref[t, v - 2]), above=v > 0)
+
+    recent(
+        x_ref, q_ref, lambda tau, v: o_ref[tau, v - 2], k_ref, w1_ref, par,
+        range(4, 6), 4, fetch, lambda v, f: f,
+    )
     for v in range(6):
-        if v:
-            fetch(v + 2)
-        for tau in range(2):
-            acc = taps(x_ref, [(tau + a, v, a, (0, 1, 2)) for a in range(2 - tau)], w1_ref, par)
-            f = act(acc + (j_ref[tau, v] if v < 2 else o_ref[tau, v - 2]) + bias, g)
-            put(s_ref, (tau, v), (f if v else f * keep).astype(BF), above=v > 0)
+        for tau in range(2):
+            put(s_ref, (tau, v), r_ref[tau, v] if v < 4 else q_ref[tau, v - 4], above=v > 0)
     back = gather()
 
     def leave(tau, u):
@@ -249,16 +287,14 @@
             leave(tau, u).start()
 
     for u in range(4):
-        for tau in range(4):
+        for tau in (2, 3, 0, 1):
             frames = [f for f in range(2) if 0 <= f - tau + 2 <= 2]
             acc = taps(s_ref, [(f, u, f - tau + 2, (0, 1, 2)) for f in frames], w2_ref, par) + z_ref[tau, u]
             if tau < 2:
                 acc_ref[tau, u] = acc
             else:
                 y_ref[tau - 2, u] = acc.astype(BF)
-        if u:
-            finish(u - 1)
-    finish(3)
+        finish(u)
     for u in range(4):
         for tau in range(2):
             leave(tau, u).wait()
@@ -308,20 +344,20 @@
 
     own, bs, as_, ts, ds = call(
         prep_kernel, "prep", [frames_in, kv],
-        [((4, 4, 3, E, 128), BF), ((4, 2, D, 128), BF), ((4, 2, D, 128), BF), ((2, 4, D, 128), BF), ((2, 2, D, 128), BF)],
+        [((4, 4, E, C), BF), ((4, 2, D, 128), BF), ((4, 2, D, 128), BF), ((2, 4, D, 128), BF), ((2, 2, D, 128), BF)],
         [], 40,
     )
     ar = lax.ppermute(as_, "rows", near)
     br = lax.ppermute(bs, "rows", far)
-    ts, ds, ar = lax.optimization_barrier((ts, ds, ar))
+    ts, ar = lax.optimization_barrier((ts, ar))
     tr = lax.ppermute(ts, "tm", [(0, 1)])
-    dr = lax.ppermute(ds, ("tm", "rows"), diag)
-
     se, oacc, iacc, pe, pf = call(
         early_kernel, "early", [own, ar, conv_one, conv_two, kv],
         [((2, 4, W, C), BF), ((2, 4, W, C), F32), ((4, 2, W, C), F32), ((2, 2, D, 128), BF), ((2, 2, W, C), F32)],
         [pltpu.VMEM((4, 6, 3, E, 128), BF), pltpu.VMEM((2, 5, 3, E, 128), BF)], 18,
     )
+    ds, pe = lax.optimization_barrier((ds, pe))
+    dr = lax.ppermute(ds, ("tm", "rows"), diag)
     sm, ps = call(
         mid_kernel, "mid", [br, iacc, pe, pf, conv_one, conv_two, kv],
         [((2, 2, W, C), BF), ((2, 4, D, 128), BF)],
@@ -335,12 +371,17 @@
     )
     tr, dr, zacc = lax.optimization_barrier((tr, dr, zacc))
     cr = lax.ppermute(jnp.stack([tr[:, 3], tr[:, 2]], axis=1), "rows", near)
+    (rs,) = call(
+        late_kernel, "late", [tr, dr, oacc, jacc, conv_one, kv], [((2, 4, W, C), BF)],
+        [pltpu.VMEM((2, 6, 3, E, 128), BF)], 1,
+    )
+    rs, cr = lax.optimization_barrier((rs, cr))
     out, acc = call(
-        late_kernel, "late", [tr, dr, cr, oacc, jacc, zacc, conv_one, conv_two, kv],
+        last_kernel, "last", [tr, cr, oacc, rs, zacc, conv_one, conv_two, kv],
         [((4, 4, W, C), BF), ((2, 4, W, C), F32)],
         [
-            pltpu.VMEM((2, 8, 3, E, 128), BF), pltpu.VMEM((2, 6, 3, E, 128), BF), pltpu.VMEM((2, 4, W, C), BF),
-            pltpu.VMEM((2, 4, W, C), BF), pltpu.SemaphoreType.DMA((2, 4)),
+            pltpu.VMEM((2, 4, 3, E, 128), BF), pltpu.VMEM((2, 6, 3, E, 128), BF), pltpu.VMEM((2, 2, W, C), BF),
+            pltpu.VMEM((2, 4, W, C), BF), pltpu.VMEM((2, 4, W, C), BF), pltpu.SemaphoreType.DMA((2, 4)),
         ],
         1, out_specs=[ANY, VMEM],
     )

time: 47 us -> 45.4 us (0.966)
  waiting for transfers between devices: 1.78 us -> 4.61 us
  starting transfers between devices: 14.9 us -> 12.4 us
  Pallas kernels: 27.7 us -> 25.8 us
    ppermute x1, waiting for transfers between devices: 0.01 us -> 3.12 us  [local(): dr = lax.ppermute(ds, ('tm', 'rows'), diag)]
    ppermute x1, starting transfers between devices: 6.64 us -> 4.09 us  [local(): cr = lax.ppermute(jnp.stack([tr[:, 3], tr[:, 2]], axis=1), 'rows', near)]
    pallas_call x6 -> x7, Pallas kernels: 27.7 us -> 25.8 us  [call(): pl.pallas_call(kernel, in_specs=in_specs or [VMEM] * len(ins), out_specs=...]
    ppermute x1, waiting for transfers between devices: 1.14 us -> 0.01 us  [local(): cr = lax.ppermute(jnp.stack([tr[:, 3], tr[:, 2]], axis=1), 'rows', near)]
    ppermute x1, waiting for transfers between devices: 0.63 us -> 1.48 us  [local(): br = lax.ppermute(bs, 'rows', far)]
  transfers between devices with their start and end apart: 6 -> 6, of which waited for: 2 -> 2; matrix products, arithmetic and copies ran while one was open for 0% -> 0% of each run, Pallas kernels for 51% -> 50%
where the time goes in v3:
time: 45.4 us; the launch traced here: 45.2 us
  Pallas kernels  25.8 us (57%)
  starting transfers between devices  12.4 us (27%)
  waiting for transfers between devices  4.61 us (10%)
  local copies, waits for them, and re-layouts  1.34 us (3%)
  other arithmetic  0.76 us (2%)
    pallas_call x7, Pallas kernels, call(): pl.pallas_call(kernel, in_specs=in_specs or [VMEM] * len(ins), out_specs=...  25.8 us
    ppermute x1, starting transfers between devices, local(): cr = lax.ppermute(jnp.stack([tr[:, 3], tr[:, 2]], axis=1), 'rows', near)  4.09 us
    ppermute x1, starting transfers between devices, local(): br = lax.ppermute(bs, 'rows', far)  3.66 us
    ppermute x1, waiting for transfers between devices, local(): dr = lax.ppermute(ds, ('tm', 'rows'), diag)  3.12 us
    ppermute x1, waiting for transfers between devices, local(): br = lax.ppermute(bs, 'rows', far)  1.48 us
    unnamed x8, local copies, waits for them, and re-layouts  1.32 us
    ppermute x1, starting transfers between devices, local(): tr = lax.ppermute(ts, 'tm', [(0, 1)])  1.29 us
    ppermute x1, starting transfers between devices, local(): dr = lax.ppermute(ds, ('tm', 'rows'), diag)  1.29 us
  transfers between devices with their start and end apart: 6, of which 2 were waited for; matrix products, arithmetic and copies ran while one was open for 0% of the time, Pallas kernels for 50%

profile of v3, /device:TPU:99, one launch (start us, length us, event | category | flops | bytes accessed | tf_op | source)
XLA Modules:
  0.0 45.2 jit_solution(5312678392439561264)
XLA Ops:
  0.0 0.7 %pad_maximum_fusion.1.k_ref = f32[4,192]{1,0:T(4,128)S(1)} fusion(f32[1,192]{1,0:T(1,128)} %bitcast.4, f32[1,192]{1,0:T(1,128)} %bitcast.5, f32[1,192]{1,0:T(1,128)} %bitcast.6, f32[1,192]{1,0:T(1,128)} %bitcast.7), kind=kLoop, calls=%fused_computation.1 | loop fusion | flops 2304 | bytes 6144 | tf_op jit(solution)/shard_map/stack | solution.py:343
  0.7 0.0 copy-start.2
  0.8 1.3 %copy-done.2 = bf16[4,4,160,192]{3,2,1,0:T(8,128)(2,1)S(1)} copy-done((bf16[4,4,160,192]{3,2,1,0:T(8,128)(2,1)S(1)}, bf16[4,4,160,192]{3,2,1,0:T(8,128)(2,1)}, u32[]{:S(2)}) %copy-start.2) | copy-done | bytes 983064
  2.1 0.0 copy-start
  2.1 0.0 copy-start.1
  2.1 1.9 %prep.1 = (bf16[4,4,192,192]{3,2,1,0:T(8,128)(2,1)S(1)}, bf16[4,2,240,128]{3,2,1,0:T(8,128)(2,1)S(1)}, bf16[4,2,240,128]{3,2,1,0:T(8,128)(2,1)S(1)}, bf16[2,4,24...) custom-call(bf16[4,4,160,192]{3,2,1,0:T(8,128)(2,1)S(1)} %copy-done.2, f32[4,192]{1,0:T(4,128)S(1)} %pad_maximum_fusion.1.k_ref), custom_call_target="tpu_custom_call" | custom-call | flops 24000000000 | bytes 3000000 | tf_op jit(solution)/shard_map/prep/pallas_call | solution.py:323
  4.0 0.8 %collective-permute-start = (bf16[4,2,240,128]{3,2,1,0:T(8,128)(2,1)S(1)}, bf16[4,2,240,128]{3,2,1,0:T(8,128)(2,1)S(1)}, u32[]{:S(2)}, u32[]{:S(2)}) collective-permute-start(bf16[4,2,240,128]{3,2,1,0:T(8,128)(2,1)S(1)} %get-tuple-element.31), channel_id=1, source_target_pairs={{0,1},{1,0},{2,3},{3,2},{4,5},{5,4},{6,7},{7,6},{8,9},{9,8},{10,11... | collective-permute-start | bytes 1474568 | tf_op jit(solution)/shard_map/ppermute | solution.py:350
  4.7 3.7 %collective-permute-start.3 = (bf16[4,2,240,128]{3,2,1,0:T(8,128)(2,1)S(1)}, bf16[4,2,240,128]{3,2,1,0:T(8,128)(2,1)S(1)}, u32[]{:S(2)}, u32[]{:S(2)}) collective-permute-start(bf16[4,2,240,128]{3,2,1,0:T(8,128)(2,1)S(1)} %get-tuple-element.38), channel_id=1, source_target_pairs={{1,2},{3,4},{5,6},{7,8},{9,10},{11,12},{13,14},{15,16},{17,18},{19... | collective-permute-start | bytes 1474568 | tf_op jit(solution)/shard_map/ppermute | solution.py:351
  8.4 0.0 collective-permute-done.a_ref
  8.4 1.3 %collective-permute-start.1 = (bf16[2,4,240,128]{3,2,1,0:T(8,128)(2,1)S(1)}, bf16[2,4,240,128]{3,2,1,0:T(8,128)(2,1)S(1)}, u32[]{:S(2)}, u32[]{:S(2)}) collective-permute-start(bf16[2,4,240,128]{3,2,1,0:T(8,128)(2,1)S(1)} %get-tuple-element.32), channel_id=1, source_target_pairs={{0,64},{1,65},{2,66},{3,67},{4,68},{5,69},{6,70},{7,71},{8,72},{9,... | collective-permute-start | bytes 1474568 | tf_op jit(solution)/shard_map/ppermute | solution.py:353
  9.7 0.0 copy-done
  9.7 0.0 copy-done.1
  9.7 9.2 %early.1 = (bf16[2,4,160,192]{3,2,1,0:T(8,128)(2,1)S(1)}, f32[2,4,160,192]{3,2,1,0:T(8,128)S(1)}, f32[4,2,160,192]{3,2,1,0:T(8,128)S(1)}, bf16[2,2,240,128]{3,2,1,0:T(8,128)(2,1)S(1)}, f32[2,2,160,192]{3,2,1,0:T(8,128)S(1)}) custom-call(bf16[4,4,192,192]{3,2,1,0:T(8,128)(2,1)S(1)} %get-tuple-element.34.own_ref, ...), custom_call_target="tpu_custom_call" | custom-call | flops 10800000000 | bytes 3000000 | tf_op jit(solution)/shard_map/early/pallas_call | solution.py:323
  18.9 1.3 %collective-permute-start.2 = (bf16[2,2,240,128]{3,2,1,0:T(8,128)(2,1)S(1)}, bf16[2,2,240,128]{3,2,1,0:T(8,128)(2,1)S(1)}, u32[]{:S(2)}, u32[]{:S(2)}) collective-permute-start(bf16[2,2,240,128]{3,2,1,0:T(8,128)(2,1)S(1)} %get-tuple-element.37), channel_id=1, source_target_pairs={{1,66},{3,68},{5,70},{7,72},{9,74},{11,76},{13,78},{15,80},{17,82}... | collective-permute-start | bytes 737288 | tf_op jit(solution)/shard_map/ppermute | solution.py:360
  20.2 1.5 %collective-permute-done.3.bx_ref = bf16[4,2,240,128]{3,2,1,0:T(8,128)(2,1)S(1)} collective-permute-done((bf16[4,2,240,128]{3,2,1,0:T(8,128)(2,1)S(1)}, bf16[4,2,240,128]{3,2,1,0:T(8,128)(2,1)S(1)}, u32[]{:S(2)}, u32[]{:S(2)}) %collective-permute-start.3) | collective-permute-done | bytes 491552 | tf_op jit(solution)/shard_map/ppermute | solution.py:351
  21.7 0.0 copy-start.3
  21.7 1.4 %mid.1 = (bf16[2,2,160,192]{3,2,1,0:T(8,128)(2,1)S(1)}, bf16[2,4,240,128]{3,2,1,0:T(8,128)(2,1)S(1)}) custom-call(bf16[4,2,240,128]{3,2,1,0:T(8,128)(2,1)S(1)} %collective-permute-done.3.bx_ref, f32[4,2,160,192]{3,2,1,0:T(8,128)S(1)} %get-tuple-element.39.i_ref, bf16[2,2,240,128]{3,2,1,0:T(8,128)(2,1)S(1)} %get-tuple-element.41.pe_ref, ...), custom_call_target="tpu_custom_call" | custom-call | flops 1800000000 | bytes 3000000 | tf_op jit(solution)/shard_map/mid/pallas_call | solution.py:323
  23.1 1.3 %collective-permute-start.5 = (bf16[2,4,240,128]{3,2,1,0:T(8,128)(2,1)S(1)}, bf16[2,4,240,128]{3,2,1,0:T(8,128)(2,1)S(1)}, u32[]{:S(2)}, u32[]{:S(2)}) collective-permute-start(bf16[2,4,240,128]{3,2,1,0:T(8,128)(2,1)S(1)} %get-tuple-element.53), channel_id=1, source_target_pairs={{0,64},{1,65},{2,66},{3,67},{4,68},{5,69},{6,70},{7,71},{8,72},{9,... | collective-permute-start | bytes 1474568 | tf_op jit(solution)/shard_map/ppermute | solution.py:366
  24.4 0.0 copy-done.3
  24.4 3.7 %wait.1 = (f32[2,2,160,192]{3,2,1,0:T(8,128)S(1)}, f32[4,4,160,192]{3,2,1,0:T(8,128)S(1)}) custom-call(bf16[4,2,240,128]{3,2,1,0:T(8,128)(2,1)S(1)} %collective-permute-done.3.bx_ref, f32[4,2,160,192]{3,2,1,0:T(8,128)S(1)} %get-tuple-element.39.i_ref, bf16[2,4,160,192]{3,2,1,0:T(8,128)(2,1)S(1)} %get-tuple-element.40.re_ref, ...), custom_call_target="tpu_custom_call" | custom-call | flops 12000000000 | bytes 3000000 | tf_op jit(solution)/shard_map/wait/pallas_call | solution.py:323
  28.1 3.1 %collective-permute-done.2.d_ref = bf16[2,2,240,128]{3,2,1,0:T(8,128)(2,1)S(1)} collective-permute-done((bf16[2,2,240,128]{3,2,1,0:T(8,128)(2,1)S(1)}, bf16[2,2,240,128]{3,2,1,0:T(8,128)(2,1)S(1)}, u32[]{:S(2)}, u32[]{:S(2)}) %collective-permute-start.2) | collective-permute-done | bytes 245792 | tf_op jit(solution)/shard_map/ppermute | solution.py:360
  31.2 0.0 collective-permute-done.1.t_ref
  31.3 4.1 %collective-permute-start.4 = (bf16[2,2,240,128]{3,2,1,0:T(8,128)(2,1)S(1)}, bf16[2,2,240,128]{3,2,1,0:T(8,128)(2,1)S(1)}, u32[]{:S(2)}, u32[]{:S(2)}) collective-permute-start(bf16[2,2,240,128]{3,2,1,0:T(8,128)(2,1)S(1)} %pad_maximum_fusion), channel_id=1, source_target_pairs={{0,1},{1,0},{2,3},{3,2},{4,5},{5,4},{6,7},{7,6},{8,9},{9,8},{10,11... | collective-permute-start | bytes 737288 | tf_op jit(solution)/shard_map/ppermute | solution.py:373
  35.4 2.3 %late.1.r_ref = bf16[2,4,160,192]{3,2,1,0:T(8,128)(2,1)S(1)} custom-call(bf16[2,4,240,128]{3,2,1,0:T(8,128)(2,1)S(1)} %collective-permute-done.1.t_ref, bf16[2,2,240,128]{3,2,1,0:T(8,128)(2,1)S(1)} %collective-permute-done.2.d_ref, f32[2,4,160,192]{3,2,1,0:T(8,128)S(1)} %get-tuple-element.47.o_ref, f32[2,2,160,192]{3,2,1,0:T(8,128)S(1)} %get-tuple-element.48.j_ref, ...), custom_call_target="tpu_custom_call" | custom-call | flops 600000000 | bytes 3000000 | tf_op jit(solution)/shard_map/late/pallas_call | solution.py:323
  37.7 0.0 collective-permute-done.4.c_ref
  37.7 6.2 %last.1 = (bf16[4,4,160,192]{3,2,1,0:T(8,128)(2,1)}, f32[2,4,160,192]{3,2,1,0:T(8,128)S(1)}) custom-call(bf16[2,4,240,128]{3,2,1,0:T(8,128)(2,1)S(1)} %collective-permute-done.1.t_ref, bf16[2,2,240,128]{3,2,1,0:T(8,128)(2,1)S(1)} %collective-permute-done.4.c_ref, f32[2,4,160,192]{3,2,1,0:T(8,128)S(1)} %get-tuple-element.47.o_ref, ...), custom_call_target="tpu_custom_call" | custom-call | flops 600000000 | bytes 3000000 | tf_op jit(solution)/shard_map/last/pallas_call | solution.py:323
  43.9 0.0 collective-permute-done.5.p_ref
  43.9 1.2 %add.1 = bf16[4,4,160,192]{3,2,1,0:T(8,128)(2,1)} custom-call(f32[2,4,160,192]{3,2,1,0:T(8,128)S(1)} %get-tuple-element.52.acc_ref, bf16[2,4,240,128]{3,2,1,0:T(8,128)(2,1)S(1)} %collective-permute-done.5.p_ref, bf16[4,4,160,192]{3,2,1,0:T(8,128)(2,1)} %get-tuple-element.54.full_ref), custom_call_target="tpu_custom_call", output_to_operand_aliasing={{}: (2, {})} | custom-call | flops 600000000 | bytes 3000000 | tf_op jit(solution)/shard_map/add/pallas_call | solution.py:323
  (2 shorter events, 0.0 us)
Async XLA Ops:
  0.7 1.3 %copy-start.2 = (bf16[4,4,160,192]{3,2,1,0:T(8,128)(2,1)S(1)}, bf16[4,4,160,192]{3,2,1,0:T(8,128)(2,1)}, u32[]{:S(2)}) copy-start(bf16[4,4,160,192]{3,2,1,0:T(8,128)(2,1)} %in_ref.1) | copy-start | bytes 2949124
  2.1 7.6 %copy-start = (bf16[3,3,3,192,192]{4,3,2,1,0:T(8,128)(2,1)S(1)}, bf16[3,3,3,192,192]{4,3,2,1,0:T(8,128)(2,1)}, u32[]{:S(2)}) copy-start(bf16[3,3,3,192,192]{4,3,2,1,0:T(8,128)(2,1)} %w1_ref.9) | copy-start | bytes 5971972
  2.1 7.6 %copy-start.1 = (bf16[3,3,3,192,192]{4,3,2,1,0:T(8,128)(2,1)S(1)}, bf16[3,3,3,192,192]{4,3,2,1,0:T(8,128)(2,1)}, u32[]{:S(2)}) copy-start(bf16[3,3,3,192,192]{4,3,2,1,0:T(8,128)(2,1)} %w2_ref.7) | copy-start | bytes 5971972
  4.0 4.4 %collective-permute-start = (bf16[4,2,240,128]{3,2,1,0:T(8,128)(2,1)S(1)}, bf16[4,2,240,128]{3,2,1,0:T(8,128)(2,1)S(1)}, u32[]{:S(2)}, u32[]{:S(2)}) collective-permute-start(bf16[4,2,240,128]{3,2,1,0:T(8,128)(2,1)S(1)} %get-tuple-element.31), channel_id=1, source_target_pairs={{0,1},{1,0},{2,3},{3,2},{4,5},{5,4},{6,7},{7,6},{8,9},{9,8},{10,11... | collective-permute-start | bytes 1474568 | tf_op jit(solution)/shard_map/ppermute | solution.py:350
  4.7 16.9 %collective-permute-start.3 = (bf16[4,2,240,128]{3,2,1,0:T(8,128)(2,1)S(1)}, bf16[4,2,240,128]{3,2,1,0:T(8,128)(2,1)S(1)}, u32[]{:S(2)}, u32[]{:S(2)}) collective-permute-start(bf16[4,2,240,128]{3,2,1,0:T(8,128)(2,1)S(1)} %get-tuple-element.38), channel_id=1, source_target_pairs={{1,2},{3,4},{5,6},{7,8},{9,10},{11,12},{13,14},{15,16},{17,18},{19... | collective-permute-start | bytes 1474568 | tf_op jit(solution)/shard_map/ppermute | solution.py:351
  8.4 22.8 %collective-permute-start.1 = (bf16[2,4,240,128]{3,2,1,0:T(8,128)(2,1)S(1)}, bf16[2,4,240,128]{3,2,1,0:T(8,128)(2,1)S(1)}, u32[]{:S(2)}, u32[]{:S(2)}) collective-permute-start(bf16[2,4,240,128]{3,2,1,0:T(8,128)(2,1)S(1)} %get-tuple-element.32), channel_id=1, source_target_pairs={{0,64},{1,65},{2,66},{3,67},{4,68},{5,69},{6,70},{7,71},{8,72},{9,... | collective-permute-start | bytes 1474568 | tf_op jit(solution)/shard_map/ppermute | solution.py:353
  18.9 12.3 %collective-permute-start.2 = (bf16[2,2,240,128]{3,2,1,0:T(8,128)(2,1)S(1)}, bf16[2,2,240,128]{3,2,1,0:T(8,128)(2,1)S(1)}, u32[]{:S(2)}, u32[]{:S(2)}) collective-permute-start(bf16[2,2,240,128]{3,2,1,0:T(8,128)(2,1)S(1)} %get-tuple-element.37), channel_id=1, source_target_pairs={{1,66},{3,68},{5,70},{7,72},{9,74},{11,76},{13,78},{15,80},{17,82}... | collective-permute-start | bytes 737288 | tf_op jit(solution)/shard_map/ppermute | solution.py:360
  21.7 2.7 %copy-start.3 = (bf16[4,4,160,192]{3,2,1,0:T(8,128)(2,1)S(1)}, bf16[4,4,160,192]{3,2,1,0:T(8,128)(2,1)}, u32[]{:S(2)}) copy-start(bf16[4,4,160,192]{3,2,1,0:T(8,128)(2,1)} %in_ref.1) | copy-start | bytes 2949124
  23.1 20.8 %collective-permute-start.5 = (bf16[2,4,240,128]{3,2,1,0:T(8,128)(2,1)S(1)}, bf16[2,4,240,128]{3,2,1,0:T(8,128)(2,1)S(1)}, u32[]{:S(2)}, u32[]{:S(2)}) collective-permute-start(bf16[2,4,240,128]{3,2,1,0:T(8,128)(2,1)S(1)} %get-tuple-element.53), channel_id=1, source_target_pairs={{0,64},{1,65},{2,66},{3,67},{4,68},{5,69},{6,70},{7,71},{8,72},{9,... | collective-permute-start | bytes 1474568 | tf_op jit(solution)/shard_map/ppermute | solution.py:366
  31.3 6.4 %collective-permute-start.4 = (bf16[2,2,240,128]{3,2,1,0:T(8,128)(2,1)S(1)}, bf16[2,2,240,128]{3,2,1,0:T(8,128)(2,1)S(1)}, u32[]{:S(2)}, u32[]{:S(2)}) collective-permute-start(bf16[2,2,240,128]{3,2,1,0:T(8,128)(2,1)S(1)} %pad_maximum_fusion), channel_id=1, source_target_pairs={{0,1},{1,0},{2,3},{3,2},{4,5},{5,4},{6,7},{7,6},{8,9},{9,8},{10,11... | collective-permute-start | bytes 737288 | tf_op jit(solution)/shard_map/ppermute | solution.py:373

commit v4 on v3

--- a/solution.py
+++ b/solution.py
@@ -226,7 +226,7 @@
     lax.fori_loop(0, 4, row, 0)
 
 
-def recent(x_ref, r_ref, o_ref, k_ref, w1_ref, par, rows, off, fetch, scale):
+def recent(x_ref, r_ref, o_ref, k_ref, w1_ref, par, rows, off, fetch, scale, also):
     bias, g = k_ref[1:2, :], k_ref[2:3, :]
 
     @pl.when(has_last())
@@ -235,6 +235,7 @@
             fetch(v)
         for v in rows:
             fetch(v - off + 2)
+            also(v)
             for tau in range(2):
                 acc = taps(x_ref, [(tau + a, v - off, a, (0, 1, 2)) for a in range(2 - tau)], w1_ref, par)
                 r_ref[tau, v - off] = scale(v, act(acc + o_ref(tau, v) + bias, g)).astype(BF)
@@ -242,6 +243,7 @@
     @pl.when(jnp.logical_not(has_last()))
     def _():
         for v in rows:
+            also(v)
             for tau in range(2):
                 r_ref[tau, v - off] = scale(v, act(o_ref(tau, v) + bias, g)).astype(BF)
 
@@ -255,7 +257,7 @@
 
     recent(
         x_ref, r_ref, lambda tau, v: j_ref[tau, v] if v < 2 else o_ref[tau, v - 2], k_ref, w1_ref, par,
-        range(4), 0, fetch, lambda v, f: f if v else f * keep,
+        range(4), 0, fetch, lambda v, f: f if v else f * keep, lambda v: None,
     )
 
 
@@ -269,13 +271,18 @@
         for t in range(2):
             put(x_ref, (t, v), unpack(t_ref[t, v + 2] if v < 2 else c_ref[t, v - 2]), above=v > 0)
 
+    def ready(v):
+        for n in (2 * v - 8, 2 * v - 7):
+            for tau in range(2):
+                put(s_ref, (tau, n), r_ref[tau, n], above=n > 0)
+
     recent(
         x_ref, q_ref, lambda tau, v: o_ref[tau, v - 2], k_ref, w1_ref, par,
-        range(4, 6), 4, fetch, lambda v, f: f,
-    )
-    for v in range(6):
-        for tau in range(2):
-            put(s_ref, (tau, v), r_ref[tau, v] if v < 4 else q_ref[tau, v - 4], above=v > 0)
+        range(4, 6), 4, fetch, lambda v, f: f, ready,
+    )
+    for tau in range(2):
+        for v in (4, 5):
+            put(s_ref, (tau, v), q_ref[tau, v - 4])
     back = gather()
 
     def leave(tau, u):
@@ -349,14 +356,13 @@
     )
     ar = lax.ppermute(as_, "rows", near)
     br = lax.ppermute(bs, "rows", far)
-    ts, ar = lax.optimization_barrier((ts, ar))
+    ts, ds, ar = lax.optimization_barrier((ts, ds, ar))
     tr = lax.ppermute(ts, "tm", [(0, 1)])
     se, oacc, iacc, pe, pf = call(
         early_kernel, "early", [own, ar, conv_one, conv_two, kv],
         [((2, 4, W, C), BF), ((2, 4, W, C), F32), ((4, 2, W, C), F32), ((2, 2, D, 128), BF), ((2, 2, W, C), F32)],
         [pltpu.VMEM((4, 6, 3, E, 128), BF), pltpu.VMEM((2, 5, 3, E, 128), BF)], 18,
     )
-    ds, pe = lax.optimization_barrier((ds, pe))
     dr = lax.ppermute(ds, ("tm", "rows"), diag)
     sm, ps = call(
         mid_kernel, "mid", [br, iacc, pe, pf, conv_one, conv_two, kv],
@@ -369,7 +375,7 @@
         [((2, 2, W, C), F32), ((4, 4, W, C), F32)],
         [pltpu.VMEM((2, 2, 3, E, 128), BF), pltpu.VMEM((2, 6, 3, E, 128), BF)], 20,
     )
-    tr, dr, zacc = lax.optimization_barrier((tr, dr, zacc))
+    tr, zacc = lax.optimization_barrier((tr, zacc))
     cr = lax.ppermute(jnp.stack([tr[:, 3], tr[:, 2]], axis=1), "rows", near)
     (rs,) = call(
         late_kernel, "late", [tr, dr, oacc, jacc, conv_one, kv], [((2, 4, W, C), BF)],

time: 45.4 us -> 44.6 us (0.982)
  the two profiles are of different devices: /device:TPU:99 before, /device:TPU:35 now
where the time goes in v4:
time: 44.6 us; the launch traced here: 44.4 us
  Pallas kernels  25.8 us (58%)
  starting transfers between devices  13.7 us (31%)
  waiting for transfers between devices  2.49 us (6%)
  local copies, waits for them, and re-layouts  1.34 us (3%)
  other arithmetic  0.76 us (2%)
    pallas_call x7, Pallas kernels, call(): pl.pallas_call(kernel, in_specs=in_specs or [VMEM] * len(ins), out_specs=...  25.8 us
    ppermute x1, starting transfers between devices, local(): cr = lax.ppermute(jnp.stack([tr[:, 3], tr[:, 2]], axis=1), 'rows', near)  5.4 us
    ppermute x1, starting transfers between devices, local(): br = lax.ppermute(bs, 'rows', far)  3.65 us
    ppermute x1, waiting for transfers between devices, local(): br = lax.ppermute(bs, 'rows', far)  1.52 us
    unnamed x8, local copies, waits for them, and re-layouts  1.32 us
    ppermute x1, starting transfers between devices, local(): pr = lax.ppermute(ps, 'tm', [(0, 1)])  1.29 us
    ppermute x1, starting transfers between devices, local(): dr = lax.ppermute(ds, ('tm', 'rows'), diag)  1.29 us
    ppermute x1, starting transfers between devices, local(): tr = lax.ppermute(ts, 'tm', [(0, 1)])  1.29 us
  transfers between devices with their start and end apart: 6, of which 2 were waited for; matrix products, arithmetic and copies ran while one was open for 0% of the time, Pallas kernels for 51%

profile of v4, /device:TPU:35, one launch (start us, length us, event | category | flops | bytes accessed | tf_op | source)
XLA Modules:
  0.0 44.4 jit_solution(1060124583684236001)
XLA Ops:
  0.0 0.7 %pad_maximum_fusion.1.k_ref = f32[4,192]{1,0:T(4,128)S(1)} fusion(f32[1,192]{1,0:T(1,128)} %bitcast.4, f32[1,192]{1,0:T(1,128)} %bitcast.5, f32[1,192]{1,0:T(1,128)} %bitcast.6, f32[1,192]{1,0:T(1,128)} %bitcast.7), kind=kLoop, calls=%fused_computation.1 | loop fusion | flops 2304 | bytes 6144 | tf_op jit(solution)/shard_map/stack | solution.py:350
  0.7 0.0 copy-start.2
  0.8 1.3 %copy-done.2 = bf16[4,4,160,192]{3,2,1,0:T(8,128)(2,1)S(1)} copy-done((bf16[4,4,160,192]{3,2,1,0:T(8,128)(2,1)S(1)}, bf16[4,4,160,192]{3,2,1,0:T(8,128)(2,1)}, u32[]{:S(2)}) %copy-start.2) | copy-done | bytes 983064
  2.1 0.0 copy-start
  2.1 0.0 copy-start.1
  2.1 1.9 %prep.1 = (bf16[4,4,192,192]{3,2,1,0:T(8,128)(2,1)S(1)}, bf16[4,2,240,128]{3,2,1,0:T(8,128)(2,1)S(1)}, bf16[4,2,240,128]{3,2,1,0:T(8,128)(2,1)S(1)}, bf16[2,4,24...) custom-call(bf16[4,4,160,192]{3,2,1,0:T(8,128)(2,1)S(1)} %copy-done.2, f32[4,192]{1,0:T(4,128)S(1)} %pad_maximum_fusion.1.k_ref), custom_call_target="tpu_custom_call" | custom-call | flops 24000000000 | bytes 3000000 | tf_op jit(solution)/shard_map/prep/pallas_call | solution.py:330
  4.0 0.8 %collective-permute-start = (bf16[4,2,240,128]{3,2,1,0:T(8,128)(2,1)S(1)}, bf16[4,2,240,128]{3,2,1,0:T(8,128)(2,1)S(1)}, u32[]{:S(2)}, u32[]{:S(2)}) collective-permute-start(bf16[4,2,240,128]{3,2,1,0:T(8,128)(2,1)S(1)} %get-tuple-element.30), channel_id=1, source_target_pairs={{0,1},{1,0},{2,3},{3,2},{4,5},{5,4},{6,7},{7,6},{8,9},{9,8},{10,11... | collective-permute-start | bytes 1474568 | tf_op jit(solution)/shard_map/ppermute | solution.py:357
  4.7 3.7 %collective-permute-start.2 = (bf16[4,2,240,128]{3,2,1,0:T(8,128)(2,1)S(1)}, bf16[4,2,240,128]{3,2,1,0:T(8,128)(2,1)S(1)}, u32[]{:S(2)}, u32[]{:S(2)}) collective-permute-start(bf16[4,2,240,128]{3,2,1,0:T(8,128)(2,1)S(1)} %get-tuple-element.32), channel_id=1, source_target_pairs={{1,2},{3,4},{5,6},{7,8},{9,10},{11,12},{13,14},{15,16},{17,18},{19... | collective-permute-start | bytes 1474568 | tf_op jit(solution)/shard_map/ppermute | solution.py:358
  8.4 0.0 collective-permute-done.a_ref
  8.4 1.3 %collective-permute-start.3 = (bf16[2,2,240,128]{3,2,1,0:T(8,128)(2,1)S(1)}, bf16[2,2,240,128]{3,2,1,0:T(8,128)(2,1)S(1)}, u32[]{:S(2)}, u32[]{:S(2)}) collective-permute-start(bf16[2,2,240,128]{3,2,1,0:T(8,128)(2,1)S(1)} %get-tuple-element.42), channel_id=1, source_target_pairs={{1,66},{3,68},{5,70},{7,72},{9,74},{11,76},{13,78},{15,80},{17,82}... | collective-permute-start | bytes 737288 | tf_op jit(solution)/shard_map/ppermute | solution.py:366
  9.7 1.3 %collective-permute-start.1 = (bf16[2,4,240,128]{3,2,1,0:T(8,128)(2,1)S(1)}, bf16[2,4,240,128]{3,2,1,0:T(8,128)(2,1)S(1)}, u32[]{:S(2)}, u32[]{:S(2)}) collective-permute-start(bf16[2,4,240,128]{3,2,1,0:T(8,128)(2,1)S(1)} %get-tuple-element.31), channel_id=1, source_target_pairs={{0,64},{1,65},{2,66},{3,67},{4,68},{5,69},{6,70},{7,71},{8,72},{9,... | collective-permute-start | bytes 1474568 | tf_op jit(solution)/shard_map/ppermute | solution.py:360
  11.0 0.0 copy-done
  11.0 0.0 copy-done.1
  11.0 9.2 %early.1 = (bf16[2,4,160,192]{3,2,1,0:T(8,128)(2,1)S(1)}, f32[2,4,160,192]{3,2,1,0:T(8,128)S(1)}, f32[4,2,160,192]{3,2,1,0:T(8,128)S(1)}, bf16[2,2,240,128]{3,2,1,0:T(8,128)(2,1)S(1)}, f32[2,2,160,192]{3,2,1,0:T(8,128)S(1)}) custom-call(bf16[4,4,192,192]{3,2,1,0:T(8,128)(2,1)S(1)} %get-tuple-element.33.own_ref, ...), custom_call_target="tpu_custom_call" | custom-call | flops 10800000000 | bytes 3000000 | tf_op jit(solution)/shard_map/early/pallas_call | solution.py:330
  20.2 1.5 %collective-permute-done.2.bx_ref = bf16[4,2,240,128]{3,2,1,0:T(8,128)(2,1)S(1)} collective-permute-done((bf16[4,2,240,128]{3,2,1,0:T(8,128)(2,1)S(1)}, bf16[4,2,240,128]{3,2,1,0:T(8,128)(2,1)S(1)}, u32[]{:S(2)}, u32[]{:S(2)}) %collective-permute-start.2) | collective-permute-done | bytes 491552 | tf_op jit(solution)/shard_map/ppermute | solution.py:358
  21.7 0.0 copy-start.3
  21.7 1.4 %mid.1 = (bf16[2,2,160,192]{3,2,1,0:T(8,128)(2,1)S(1)}, bf16[2,4,240,128]{3,2,1,0:T(8,128)(2,1)S(1)}) custom-call(bf16[4,2,240,128]{3,2,1,0:T(8,128)(2,1)S(1)} %collective-permute-done.2.bx_ref, f32[4,2,160,192]{3,2,1,0:T(8,128)S(1)} %get-tuple-element.35.i_ref, bf16[2,2,240,128]{3,2,1,0:T(8,128)(2,1)S(1)} %get-tuple-element.37.pe_ref, ...), custom_call_target="tpu_custom_call" | custom-call | flops 1800000000 | bytes 3000000 | tf_op jit(solution)/shard_map/mid/pallas_call | solution.py:330
  23.1 1.3 %collective-permute-start.5 = (bf16[2,4,240,128]{3,2,1,0:T(8,128)(2,1)S(1)}, bf16[2,4,240,128]{3,2,1,0:T(8,128)(2,1)S(1)}, u32[]{:S(2)}, u32[]{:S(2)}) collective-permute-start(bf16[2,4,240,128]{3,2,1,0:T(8,128)(2,1)S(1)} %get-tuple-element.49), channel_id=1, source_target_pairs={{0,64},{1,65},{2,66},{3,67},{4,68},{5,69},{6,70},{7,71},{8,72},{9,... | collective-permute-start | bytes 1474568 | tf_op jit(solution)/shard_map/ppermute | solution.py:372
  24.4 0.0 copy-done.3
  24.4 3.7 %wait.1 = (f32[2,2,160,192]{3,2,1,0:T(8,128)S(1)}, f32[4,4,160,192]{3,2,1,0:T(8,128)S(1)}) custom-call(bf16[4,2,240,128]{3,2,1,0:T(8,128)(2,1)S(1)} %collective-permute-done.2.bx_ref, f32[4,2,160,192]{3,2,1,0:T(8,128)S(1)} %get-tuple-element.35.i_ref, bf16[2,4,160,192]{3,2,1,0:T(8,128)(2,1)S(1)} %get-tuple-element.36.re_ref, ...), custom_call_target="tpu_custom_call" | custom-call | flops 12000000000 | bytes 3000000 | tf_op jit(solution)/shard_map/wait/pallas_call | solution.py:330
  28.1 1.0 %collective-permute-done.1.t_ref = bf16[2,4,240,128]{3,2,1,0:T(8,128)(2,1)S(1)} collective-permute-done((bf16[2,4,240,128]{3,2,1,0:T(8,128)(2,1)S(1)}, bf16[2,4,240,128]{3,2,1,0:T(8,128)(2,1)S(1)}, u32[]{:S(2)}, u32[]{:S(2)}) %collective-permute-start.1) | collective-permute-done | bytes 491552 | tf_op jit(solution)/shard_map/ppermute | solution.py:360
  29.2 5.4 %collective-permute-start.4 = (bf16[2,2,240,128]{3,2,1,0:T(8,128)(2,1)S(1)}, bf16[2,2,240,128]{3,2,1,0:T(8,128)(2,1)S(1)}, u32[]{:S(2)}, u32[]{:S(2)}) collective-permute-start(bf16[2,2,240,128]{3,2,1,0:T(8,128)(2,1)S(1)} %pad_maximum_fusion), channel_id=1, source_target_pairs={{0,1},{1,0},{2,3},{3,2},{4,5},{5,4},{6,7},{7,6},{8,9},{9,8},{10,11... | collective-permute-start | bytes 737288 | tf_op jit(solution)/shard_map/ppermute | solution.py:379
  34.6 0.0 collective-permute-done.3.d_ref
  34.6 2.3 %late.1.r_ref = bf16[2,4,160,192]{3,2,1,0:T(8,128)(2,1)S(1)} custom-call(bf16[2,4,240,128]{3,2,1,0:T(8,128)(2,1)S(1)} %collective-permute-done.1.t_ref, bf16[2,2,240,128]{3,2,1,0:T(8,128)(2,1)S(1)} %collective-permute-done.3.d_ref, f32[2,4,160,192]{3,2,1,0:T(8,128)S(1)} %get-tuple-element.43.o_ref, f32[2,2,160,192]{3,2,1,0:T(8,128)S(1)} %get-tuple-element.44.j_ref, ...), custom_call_target="tpu_custom_call" | custom-call | flops 600000000 | bytes 3000000 | tf_op jit(solution)/shard_map/late/pallas_call | solution.py:330
  36.9 0.0 collective-permute-done.4.c_ref
  36.9 6.2 %last.1 = (bf16[4,4,160,192]{3,2,1,0:T(8,128)(2,1)}, f32[2,4,160,192]{3,2,1,0:T(8,128)S(1)}) custom-call(bf16[2,4,240,128]{3,2,1,0:T(8,128)(2,1)S(1)} %collective-permute-done.1.t_ref, bf16[2,2,240,128]{3,2,1,0:T(8,128)(2,1)S(1)} %collective-permute-done.4.c_ref, f32[2,4,160,192]{3,2,1,0:T(8,128)S(1)} %get-tuple-element.43.o_ref, ...), custom_call_target="tpu_custom_call" | custom-call | flops 600000000 | bytes 3000000 | tf_op jit(solution)/shard_map/last/pallas_call | solution.py:330
  43.1 0.0 collective-permute-done.5.p_ref
  43.1 1.2 %add.1 = bf16[4,4,160,192]{3,2,1,0:T(8,128)(2,1)} custom-call(f32[2,4,160,192]{3,2,1,0:T(8,128)S(1)} %get-tuple-element.48.acc_ref, bf16[2,4,240,128]{3,2,1,0:T(8,128)(2,1)S(1)} %collective-permute-done.5.p_ref, bf16[4,4,160,192]{3,2,1,0:T(8,128)(2,1)} %get-tuple-element.50.full_ref), custom_call_target="tpu_custom_call", output_to_operand_aliasing={{}: (2, {})} | custom-call | flops 600000000 | bytes 3000000 | tf_op jit(solution)/shard_map/add/pallas_call | solution.py:330
  (2 shorter events, 0.0 us)
Async XLA Ops:
  0.7 1.3 %copy-start.2 = (bf16[4,4,160,192]{3,2,1,0:T(8,128)(2,1)S(1)}, bf16[4,4,160,192]{3,2,1,0:T(8,128)(2,1)}, u32[]{:S(2)}) copy-start(bf16[4,4,160,192]{3,2,1,0:T(8,128)(2,1)} %in_ref.1) | copy-start | bytes 2949124
  2.1 8.9 %copy-start = (bf16[3,3,3,192,192]{4,3,2,1,0:T(8,128)(2,1)S(1)}, bf16[3,3,3,192,192]{4,3,2,1,0:T(8,128)(2,1)}, u32[]{:S(2)}) copy-start(bf16[3,3,3,192,192]{4,3,2,1,0:T(8,128)(2,1)} %w1_ref.9) | copy-start | bytes 5971972
  2.1 8.9 %copy-start.1 = (bf16[3,3,3,192,192]{4,3,2,1,0:T(8,128)(2,1)S(1)}, bf16[3,3,3,192,192]{4,3,2,1,0:T(8,128)(2,1)}, u32[]{:S(2)}) copy-start(bf16[3,3,3,192,192]{4,3,2,1,0:T(8,128)(2,1)} %w2_ref.7) | copy-start | bytes 5971972
  4.0 4.4 %collective-permute-start = (bf16[4,2,240,128]{3,2,1,0:T(8,128)(2,1)S(1)}, bf16[4,2,240,128]{3,2,1,0:T(8,128)(2,1)S(1)}, u32[]{:S(2)}, u32[]{:S(2)}) collective-permute-start(bf16[4,2,240,128]{3,2,1,0:T(8,128)(2,1)S(1)} %get-tuple-element.30), channel_id=1, source_target_pairs={{0,1},{1,0},{2,3},{3,2},{4,5},{5,4},{6,7},{7,6},{8,9},{9,8},{10,11... | collective-permute-start | bytes 1474568 | tf_op jit(solution)/shard_map/ppermute | solution.py:357
  4.7 17.0 %collective-permute-start.2 = (bf16[4,2,240,128]{3,2,1,0:T(8,128)(2,1)S(1)}, bf16[4,2,240,128]{3,2,1,0:T(8,128)(2,1)S(1)}, u32[]{:S(2)}, u32[]{:S(2)}) collective-permute-start(bf16[4,2,240,128]{3,2,1,0:T(8,128)(2,1)S(1)} %get-tuple-element.32), channel_id=1, source_target_pairs={{1,2},{3,4},{5,6},{7,8},{9,10},{11,12},{13,14},{15,16},{17,18},{19... | collective-permute-start | bytes 1474568 | tf_op jit(solution)/shard_map/ppermute | solution.py:358
  8.4 26.2 %collective-permute-start.3 = (bf16[2,2,240,128]{3,2,1,0:T(8,128)(2,1)S(1)}, bf16[2,2,240,128]{3,2,1,0:T(8,128)(2,1)S(1)}, u32[]{:S(2)}, u32[]{:S(2)}) collective-permute-start(bf16[2,2,240,128]{3,2,1,0:T(8,128)(2,1)S(1)} %get-tuple-element.42), channel_id=1, source_target_pairs={{1,66},{3,68},{5,70},{7,72},{9,74},{11,76},{13,78},{15,80},{17,82}... | collective-permute-start | bytes 737288 | tf_op jit(solution)/shard_map/ppermute | solution.py:366
  9.7 19.4 %collective-permute-start.1 = (bf16[2,4,240,128]{3,2,1,0:T(8,128)(2,1)S(1)}, bf16[2,4,240,128]{3,2,1,0:T(8,128)(2,1)S(1)}, u32[]{:S(2)}, u32[]{:S(2)}) collective-permute-start(bf16[2,4,240,128]{3,2,1,0:T(8,128)(2,1)S(1)} %get-tuple-element.31), channel_id=1, source_target_pairs={{0,64},{1,65},{2,66},{3,67},{4,68},{5,69},{6,70},{7,71},{8,72},{9,... | collective-permute-start | bytes 1474568 | tf_op jit(solution)/shard_map/ppermute | solution.py:360
  21.7 2.7 %copy-start.3 = (bf16[4,4,160,192]{3,2,1,0:T(8,128)(2,1)S(1)}, bf16[4,4,160,192]{3,2,1,0:T(8,128)(2,1)}, u32[]{:S(2)}) copy-start(bf16[4,4,160,192]{3,2,1,0:T(8,128)(2,1)} %in_ref.1) | copy-start | bytes 2949124
  23.1 20.0 %collective-permute-start.5 = (bf16[2,4,240,128]{3,2,1,0:T(8,128)(2,1)S(1)}, bf16[2,4,240,128]{3,2,1,0:T(8,128)(2,1)S(1)}, u32[]{:S(2)}, u32[]{:S(2)}) collective-permute-start(bf16[2,4,240,128]{3,2,1,0:T(8,128)(2,1)S(1)} %get-tuple-element.49), channel_id=1, source_target_pairs={{0,64},{1,65},{2,66},{3,67},{4,68},{5,69},{6,70},{7,71},{8,72},{9,... | collective-permute-start | bytes 1474568 | tf_op jit(solution)/shard_map/ppermute | solution.py:372
  29.2 7.7 %collective-permute-start.4 = (bf16[2,2,240,128]{3,2,1,0:T(8,128)(2,1)S(1)}, bf16[2,2,240,128]{3,2,1,0:T(8,128)(2,1)S(1)}, u32[]{:S(2)}, u32[]{:S(2)}) collective-permute-start(bf16[2,2,240,128]{3,2,1,0:T(8,128)(2,1)S(1)} %pad_maximum_fusion), channel_id=1, source_target_pairs={{0,1},{1,0},{2,3},{3,2},{4,5},{5,4},{6,7},{7,6},{8,9},{9,8},{10,11... | collective-permute-start | bytes 737288 | tf_op jit(solution)/shard_map/ppermute | solution.py:379

commit v5 on v4

--- a/solution.py
+++ b/solution.py
@@ -356,13 +356,15 @@
     )
     ar = lax.ppermute(as_, "rows", near)
     br = lax.ppermute(bs, "rows", far)
-    ts, ds, ar = lax.optimization_barrier((ts, ds, ar))
+    ts, ar = lax.optimization_barrier((ts, ar))
     tr = lax.ppermute(ts, "tm", [(0, 1)])
     se, oacc, iacc, pe, pf = call(
         early_kernel, "early", [own, ar, conv_one, conv_two, kv],
         [((2, 4, W, C), BF), ((2, 4, W, C), F32), ((4, 2, W, C), F32), ((2, 2, D, 128), BF), ((2, 2, W, C), F32)],
         [pltpu.VMEM((4, 6, 3, E, 128), BF), pltpu.VMEM((2, 5, 3, E, 128), BF)], 18,
     )
+    kv, ar = lax.optimization_barrier((kv + 0.0 * ar[0, 0, 0, 0].astype(F32), ar))
+    ds, kv = lax.optimization_barrier((ds, kv))
     dr = lax.ppermute(ds, ("tm", "rows"), diag)
     sm, ps = call(
         mid_kernel, "mid", [br, iacc, pe, pf, conv_one, conv_two, kv],

time: 44.6 us -> 44.3 us (level)
  the two profiles are of different devices: /device:TPU:35 before, /device:TPU:65 now
where the time goes in v5:
time: 44.3 us; the launch traced here: 44.1 us
  Pallas kernels  25.5 us (58%)
  starting transfers between devices  14.2 us (32%)
  local copies, waits for them, and re-layouts  1.88 us (4%)
  between operations  1.02 us (2%)
  other arithmetic  0.78 us (2%)
  waiting for transfers between devices  0.68 us (2%)
    pallas_call x7, Pallas kernels, call(): pl.pallas_call(kernel, in_specs=in_specs or [VMEM] * len(ins), out_specs=...  25.5 us
    ppermute x1, starting transfers between devices, local(): br = lax.ppermute(bs, 'rows', far)  4.55 us
    ppermute x1, starting transfers between devices, local(): dr = lax.ppermute(ds, ('tm', 'rows'), diag)  3.15 us
    ppermute x1, starting transfers between devices, local(): cr = lax.ppermute(jnp.stack([tr[:, 3], tr[:, 2]], axis=1), 'rows', near)  3.11 us
    unnamed x16, local copies, waits for them, and re-layouts  1.35 us
    ppermute x1, starting transfers between devices, local(): tr = lax.ppermute(ts, 'tm', [(0, 1)])  1.32 us
    ppermute x1, starting transfers between devices, local(): pr = lax.ppermute(ps, 'tm', [(0, 1)])  1.32 us
  transfers between devices with their start and end apart: 6, of which 1 were waited for; matrix products, arithmetic and copies ran while one was open for 1% of the time, Pallas kernels for 51%

profile of v5, /device:TPU:65, one launch (start us, length us, event | category | flops | bytes accessed | tf_op | source)
XLA Modules:
  0.0 44.1 jit_solution(21270393856553644)
XLA Ops:
  0.0 0.7 %pad_maximum_fusion.1.k_ref = f32[4,192]{1,0:T(4,128)S(1)} fusion(f32[1,192]{1,0:T(1,128)} %bitcast.5, f32[1,192]{1,0:T(1,128)} %bitcast.7, f32[1,192]{1,0:T(1,128)} %bitcast.9, f32[1,192]{1,0:T(1,128)} %bitcast.11), kind=kLoop, calls=%fused_computation.1 | loop fusion | flops 2304 | bytes 6144 | tf_op jit(solution)/shard_map/stack | solution.py:350
  0.7 0.0 copy-start.2
  0.8 1.3 %copy-done.2 = bf16[4,4,160,192]{3,2,1,0:T(8,128)(2,1)S(1)} copy-done((bf16[4,4,160,192]{3,2,1,0:T(8,128)(2,1)S(1)}, bf16[4,4,160,192]{3,2,1,0:T(8,128)(2,1)}, u32[]{:S(2)}) %copy-start.2) | copy-done | bytes 983064
  2.1 0.0 copy-start
  2.1 0.0 copy-start.1
  2.1 1.9 %prep.1 = (bf16[4,4,192,192]{3,2,1,0:T(8,128)(2,1)S(1)}, bf16[4,2,240,128]{3,2,1,0:T(8,128)(2,1)S(1)}, bf16[4,2,240,128]{3,2,1,0:T(8,128)(2,1)S(1)}, bf16[2,4,24...) custom-call(bf16[4,4,160,192]{3,2,1,0:T(8,128)(2,1)S(1)} %copy-done.2, f32[4,192]{1,0:T(4,128)S(1)} %pad_maximum_fusion.1.k_ref), custom_call_target="tpu_custom_call" | custom-call | flops 24000000000 | bytes 3000000 | tf_op jit(solution)/shard_map/prep/pallas_call | solution.py:330
  4.0 0.8 %collective-permute-start = (bf16[4,2,240,128]{3,2,1,0:T(8,128)(2,1)S(1)}, bf16[4,2,240,128]{3,2,1,0:T(8,128)(2,1)S(1)}, u32[]{:S(2)}, u32[]{:S(2)}) collective-permute-start(bf16[4,2,240,128]{3,2,1,0:T(8,128)(2,1)S(1)} %get-tuple-element.31), channel_id=1, source_target_pairs={{0,1},{1,0},{2,3},{3,2},{4,5},{5,4},{6,7},{7,6},{8,9},{9,8},{10,11... | collective-permute-start | bytes 1474568 | tf_op jit(solution)/shard_map/ppermute | solution.py:357
  4.8 4.5 %collective-permute-start.2 = (bf16[4,2,240,128]{3,2,1,0:T(8,128)(2,1)S(1)}, bf16[4,2,240,128]{3,2,1,0:T(8,128)(2,1)S(1)}, u32[]{:S(2)}, u32[]{:S(2)}) collective-permute-start(bf16[4,2,240,128]{3,2,1,0:T(8,128)(2,1)S(1)} %get-tuple-element.33), channel_id=1, source_target_pairs={{1,2},{3,4},{5,6},{7,8},{9,10},{11,12},{13,14},{15,16},{17,18},{19... | collective-permute-start | bytes 1474568 | tf_op jit(solution)/shard_map/ppermute | solution.py:358
  9.3 0.0 collective-permute-done.a_ref
  9.3 0.5 %slice.9 = bf16[1,1,1,1]{3,2,1,0:T(2,128)(2,1)} slice(bf16[4,2,240,128]{3,2,1,0:T(8,128)(2,1)S(1)} %collective-permute-done.a_ref), slice={[0:1], [0:1], [0:1], [0:1]} | slice | bytes 4 | tf_op jit(solution)/shard_map/slice | solution.py:366
  10.5 0.0 copy-done.4
  10.5 0.0 copy-done.5
  10.5 0.0 copy-done.6
  10.5 0.0 copy-done.7
  10.6 3.2 %collective-permute-start.3 = (bf16[2,2,240,128]{3,2,1,0:T(8,128)(2,1)S(1)}, bf16[2,2,240,128]{3,2,1,0:T(8,128)(2,1)S(1)}, u32[]{:S(2)}, u32[]{:S(2)}) collective-permute-start(bf16[2,2,240,128]{3,2,1,0:T(8,128)(2,1)S(1)} %get-tuple-element.46), channel_id=1, source_target_pairs={{1,66},{3,68},{5,70},{7,72},{9,74},{11,76},{13,78},{15,80},{17,82}... | collective-permute-start | bytes 737288 | tf_op jit(solution)/shard_map/ppermute | solution.py:368
  13.7 1.3 %collective-permute-start.1 = (bf16[2,4,240,128]{3,2,1,0:T(8,128)(2,1)S(1)}, bf16[2,4,240,128]{3,2,1,0:T(8,128)(2,1)S(1)}, u32[]{:S(2)}, u32[]{:S(2)}) collective-permute-start(bf16[2,4,240,128]{3,2,1,0:T(8,128)(2,1)S(1)} %get-tuple-element.32), channel_id=1, source_target_pairs={{0,64},{1,65},{2,66},{3,67},{4,68},{5,69},{6,70},{7,71},{8,72},{9,... | collective-permute-start | bytes 1474568 | tf_op jit(solution)/shard_map/ppermute | solution.py:360
  15.0 0.0 copy-done
  15.1 0.0 copy-done.1
  15.1 10.8 %early.1 = (bf16[2,4,160,192]{3,2,1,0:T(8,128)(2,1)S(1)}, f32[2,4,160,192]{3,2,1,0:T(8,128)S(1)}, f32[4,2,160,192]{3,2,1,0:T(8,128)S(1)}, bf16[2,2,240,128]{3,2,1,0:T(8,128)(2,1)S(1)}, f32[2,2,160,192]{3,2,1,0:T(8,128)S(1)}) custom-call(bf16[4,4,192,192]{3,2,1,0:T(8,128)(2,1)S(1)} %get-tuple-element.34.own_ref, ...), custom_call_target="tpu_custom_call" | custom-call | flops 10800000000 | bytes 3000000 | tf_op jit(solution)/shard_map/early/pallas_call | solution.py:330
  25.9 0.0 collective-permute-done.2.bx_ref
  25.9 0.0 copy-start.3
  25.9 2.2 %mid.1 = (bf16[2,2,160,192]{3,2,1,0:T(8,128)(2,1)S(1)}, bf16[2,4,240,128]{3,2,1,0:T(8,128)(2,1)S(1)}) custom-call(bf16[4,2,240,128]{3,2,1,0:T(8,128)(2,1)S(1)} %collective-permute-done.2.bx_ref, f32[4,2,160,192]{3,2,1,0:T(8,128)S(1)} %get-tuple-element.36.i_ref, bf16[2,2,240,128]{3,2,1,0:T(8,128)(2,1)S(1)} %get-tuple-element.38.pe_ref, ...), custom_call_target="tpu_custom_call" | custom-call | flops 1800000000 | bytes 3000000 | tf_op jit(solution)/shard_map/mid/pallas_call | solution.py:330
  28.1 1.3 %collective-permute-start.5 = (bf16[2,4,240,128]{3,2,1,0:T(8,128)(2,1)S(1)}, bf16[2,4,240,128]{3,2,1,0:T(8,128)(2,1)S(1)}, u32[]{:S(2)}, u32[]{:S(2)}) collective-permute-start(bf16[2,4,240,128]{3,2,1,0:T(8,128)(2,1)S(1)} %get-tuple-element.53), channel_id=1, source_target_pairs={{0,64},{1,65},{2,66},{3,67},{4,68},{5,69},{6,70},{7,71},{8,72},{9,... | collective-permute-start | bytes 1474568 | tf_op jit(solution)/shard_map/ppermute | solution.py:374
  29.4 3.7 %wait.1 = (f32[2,2,160,192]{3,2,1,0:T(8,128)S(1)}, f32[4,4,160,192]{3,2,1,0:T(8,128)S(1)}) custom-call(bf16[4,2,240,128]{3,2,1,0:T(8,128)(2,1)S(1)} %collective-permute-done.2.bx_ref, f32[4,2,160,192]{3,2,1,0:T(8,128)S(1)} %get-tuple-element.36.i_ref, bf16[2,4,160,192]{3,2,1,0:T(8,128)(2,1)S(1)} %get-tuple-element.37.re_ref, ...), custom_call_target="tpu_custom_call" | custom-call | flops 12000000000 | bytes 3000000 | tf_op jit(solution)/shard_map/wait/pallas_call | solution.py:330
  33.1 0.0 collective-permute-done.1.t_ref
  33.2 3.1 %collective-permute-start.4 = (bf16[2,2,240,128]{3,2,1,0:T(8,128)(2,1)S(1)}, bf16[2,2,240,128]{3,2,1,0:T(8,128)(2,1)S(1)}, u32[]{:S(2)}, u32[]{:S(2)}) collective-permute-start(bf16[2,2,240,128]{3,2,1,0:T(8,128)(2,1)S(1)} %pad_maximum_fusion), channel_id=1, source_target_pairs={{0,1},{1,0},{2,3},{3,2},{4,5},{5,4},{6,7},{7,6},{8,9},{9,8},{10,11... | collective-permute-start | bytes 737288 | tf_op jit(solution)/shard_map/ppermute | solution.py:381
  36.3 0.0 collective-permute-done.3.d_ref
  36.3 0.5 %late.1.r_ref = bf16[2,4,160,192]{3,2,1,0:T(8,128)(2,1)S(1)} custom-call(bf16[2,4,240,128]{3,2,1,0:T(8,128)(2,1)S(1)} %collective-permute-done.1.t_ref, bf16[2,2,240,128]{3,2,1,0:T(8,128)(2,1)S(1)} %collective-permute-done.3.d_ref, f32[2,4,160,192]{3,2,1,0:T(8,128)S(1)} %get-tuple-element.47.o_ref, f32[2,2,160,192]{3,2,1,0:T(8,128)S(1)} %get-tuple-element.48.j_ref, ...), custom_call_target="tpu_custom_call" | custom-call | flops 600000000 | bytes 3000000 | tf_op jit(solution)/shard_map/late/pallas_call | solution.py:330
  36.8 0.7 %collective-permute-done.4.c_ref = bf16[2,2,240,128]{3,2,1,0:T(8,128)(2,1)S(1)} collective-permute-done((bf16[2,2,240,128]{3,2,1,0:T(8,128)(2,1)S(1)}, bf16[2,2,240,128]{3,2,1,0:T(8,128)(2,1)S(1)}, u32[]{:S(2)}, u32[]{:S(2)}) %collective-permute-start.4) | collective-permute-done | bytes 245792 | tf_op jit(solution)/shard_map/ppermute | solution.py:381
  37.4 5.3 %last.1 = (bf16[4,4,160,192]{3,2,1,0:T(8,128)(2,1)}, f32[2,4,160,192]{3,2,1,0:T(8,128)S(1)}) custom-call(bf16[2,4,240,128]{3,2,1,0:T(8,128)(2,1)S(1)} %collective-permute-done.1.t_ref, bf16[2,2,240,128]{3,2,1,0:T(8,128)(2,1)S(1)} %collective-permute-done.4.c_ref, f32[2,4,160,192]{3,2,1,0:T(8,128)S(1)} %get-tuple-element.47.o_ref, ...), custom_call_target="tpu_custom_call" | custom-call | flops 600000000 | bytes 3000000 | tf_op jit(solution)/shard_map/last/pallas_call | solution.py:330
  42.7 0.0 collective-permute-done.5.p_ref
  42.7 1.2 %add.11 = bf16[4,4,160,192]{3,2,1,0:T(8,128)(2,1)} custom-call(f32[2,4,160,192]{3,2,1,0:T(8,128)S(1)} %get-tuple-element.52.acc_ref, bf16[2,4,240,128]{3,2,1,0:T(8,128)(2,1)S(1)} %collective-permute-done.5.p_ref, bf16[4,4,160,192]{3,2,1,0:T(8,128)(2,1)} %get-tuple-element.54.full_ref), custom_call_target="tpu_custom_call", output_to_operand_aliasing={{}: (2, {})} | custom-call | flops 600000000 | bytes 3000000 | tf_op jit(solution)/shard_map/add/pallas_call | solution.py:330
  (8 shorter events, 0.1 us)
Async XLA Ops:
  0.7 1.3 %copy-start.2 = (bf16[4,4,160,192]{3,2,1,0:T(8,128)(2,1)S(1)}, bf16[4,4,160,192]{3,2,1,0:T(8,128)(2,1)}, u32[]{:S(2)}) copy-start(bf16[4,4,160,192]{3,2,1,0:T(8,128)(2,1)} %in_ref.1) | copy-start | bytes 2949124
  2.1 8.4 %copy-start.4 = (f32[192]{0:T(256)S(1)}, f32[192]{0:T(256)}, u32[]{:S(2)}) copy-start(f32[192]{0:T(256)} %param.13) | copy-start | bytes 2308
  2.1 8.4 %copy-start.5 = (f32[192]{0:T(256)S(1)}, f32[192]{0:T(256)}, u32[]{:S(2)}) copy-start(f32[192]{0:T(256)} %param.11) | copy-start | bytes 2308
  2.1 8.5 %copy-start.6 = (f32[192]{0:T(256)S(1)}, f32[192]{0:T(256)}, u32[]{:S(2)}) copy-start(f32[192]{0:T(256)} %param.10) | copy-start | bytes 2308
  2.1 8.5 %copy-start.7 = (f32[192]{0:T(256)S(1)}, f32[192]{0:T(256)}, u32[]{:S(2)}) copy-start(f32[192]{0:T(256)} %param.8) | copy-start | bytes 2308
  2.1 13.0 %copy-start = (bf16[3,3,3,192,192]{4,3,2,1,0:T(8,128)(2,1)S(1)}, bf16[3,3,3,192,192]{4,3,2,1,0:T(8,128)(2,1)}, u32[]{:S(2)}) copy-start(bf16[3,3,3,192,192]{4,3,2,1,0:T(8,128)(2,1)} %w1_ref.9) | copy-start | bytes 5971972
  2.1 13.0 %copy-start.1 = (bf16[3,3,3,192,192]{4,3,2,1,0:T(8,128)(2,1)S(1)}, bf16[3,3,3,192,192]{4,3,2,1,0:T(8,128)(2,1)}, u32[]{:S(2)}) copy-start(bf16[3,3,3,192,192]{4,3,2,1,0:T(8,128)(2,1)} %w2_ref.7) | copy-start | bytes 5971972
  4.0 5.3 %collective-permute-start = (bf16[4,2,240,128]{3,2,1,0:T(8,128)(2,1)S(1)}, bf16[4,2,240,128]{3,2,1,0:T(8,128)(2,1)S(1)}, u32[]{:S(2)}, u32[]{:S(2)}) collective-permute-start(bf16[4,2,240,128]{3,2,1,0:T(8,128)(2,1)S(1)} %get-tuple-element.31), channel_id=1, source_target_pairs={{0,1},{1,0},{2,3},{3,2},{4,5},{5,4},{6,7},{7,6},{8,9},{9,8},{10,11... | collective-permute-start | bytes 1474568 | tf_op jit(solution)/shard_map/ppermute | solution.py:357
  4.8 21.1 %collective-permute-start.2 = (bf16[4,2,240,128]{3,2,1,0:T(8,128)(2,1)S(1)}, bf16[4,2,240,128]{3,2,1,0:T(8,128)(2,1)S(1)}, u32[]{:S(2)}, u32[]{:S(2)}) collective-permute-start(bf16[4,2,240,128]{3,2,1,0:T(8,128)(2,1)S(1)} %get-tuple-element.33), channel_id=1, source_target_pairs={{1,2},{3,4},{5,6},{7,8},{9,10},{11,12},{13,14},{15,16},{17,18},{19... | collective-permute-start | bytes 1474568 | tf_op jit(solution)/shard_map/ppermute | solution.py:358
  10.6 25.7 %collective-permute-start.3 = (bf16[2,2,240,128]{3,2,1,0:T(8,128)(2,1)S(1)}, bf16[2,2,240,128]{3,2,1,0:T(8,128)(2,1)S(1)}, u32[]{:S(2)}, u32[]{:S(2)}) collective-permute-start(bf16[2,2,240,128]{3,2,1,0:T(8,128)(2,1)S(1)} %get-tuple-element.46), channel_id=1, source_target_pairs={{1,66},{3,68},{5,70},{7,72},{9,74},{11,76},{13,78},{15,80},{17,82}... | collective-permute-start | bytes 737288 | tf_op jit(solution)/shard_map/ppermute | solution.py:368
  13.7 19.4 %collective-permute-start.1 = (bf16[2,4,240,128]{3,2,1,0:T(8,128)(2,1)S(1)}, bf16[2,4,240,128]{3,2,1,0:T(8,128)(2,1)S(1)}, u32[]{:S(2)}, u32[]{:S(2)}) collective-permute-start(bf16[2,4,240,128]{3,2,1,0:T(8,128)(2,1)S(1)} %get-tuple-element.32), channel_id=1, source_target_pairs={{0,64},{1,65},{2,66},{3,67},{4,68},{5,69},{6,70},{7,71},{8,72},{9,... | collective-permute-start | bytes 1474568 | tf_op jit(solution)/shard_map/ppermute | solution.py:360
  25.9 3.5 %copy-start.3 = (bf16[4,4,160,192]{3,2,1,0:T(8,128)(2,1)S(1)}, bf16[4,4,160,192]{3,2,1,0:T(8,128)(2,1)}, u32[]{:S(2)}) copy-start(bf16[4,4,160,192]{3,2,1,0:T(8,128)(2,1)} %in_ref.1) | copy-start | bytes 2949124
  28.1 14.7 %collective-permute-start.5 = (bf16[2,4,240,128]{3,2,1,0:T(8,128)(2,1)S(1)}, bf16[2,4,240,128]{3,2,1,0:T(8,128)(2,1)S(1)}, u32[]{:S(2)}, u32[]{:S(2)}) collective-permute-start(bf16[2,4,240,128]{3,2,1,0:T(8,128)(2,1)S(1)} %get-tuple-element.53), channel_id=1, source_target_pairs={{0,64},{1,65},{2,66},{3,67},{4,68},{5,69},{6,70},{7,71},{8,72},{9,... | collective-permute-start | bytes 1474568 | tf_op jit(solution)/shard_map/ppermute | solution.py:374
  33.2 4.3 %collective-permute-start.4 = (bf16[2,2,240,128]{3,2,1,0:T(8,128)(2,1)S(1)}, bf16[2,2,240,128]{3,2,1,0:T(8,128)(2,1)S(1)}, u32[]{:S(2)}, u32[]{:S(2)}) collective-permute-start(bf16[2,2,240,128]{3,2,1,0:T(8,128)(2,1)S(1)} %pad_maximum_fusion), channel_id=1, source_target_pairs={{0,1},{1,0},{2,3},{3,2},{4,5},{5,4},{6,7},{7,6},{8,9},{9,8},{10,11... | collective-permute-start | bytes 737288 | tf_op jit(solution)/shard_map/ppermute | solution.py:381

commit v6 on v5

--- a/solution.py
+++ b/solution.py
@@ -153,7 +153,8 @@
         o_ref[1, k] = taps(x_ref, [(a - 1, k, a, all3) for a in (1, 2)], w1_ref, par)
         return 0
 
-    lax.fori_loop(0, 4, row, 0)
+    for k in range(4):
+        row(k, 0)
     for tau in range(4):
         ok = [a for a in range(3) if tau + a >= 2]
         i_ref[tau, 0] = taps(x_ref, [(tau + a - 2, -2, a, (2,)) for a in ok], w1_ref, par)
@@ -223,7 +224,8 @@
             z_ref[tau, u] = start
         return 0
 
-    lax.fori_loop(0, 4, row, 0)
+    for k in range(4):
+        row(k, 0)
 
 
 def recent(x_ref, r_ref, o_ref, k_ref, w1_ref, par, rows, off, fetch, scale, also):

time: 44.3 us -> 45.3 us (1.023)
  the two profiles are of different devices: /device:TPU:65 before, /device:TPU:99 now
where the time goes in v6:
time: 45.3 us; the launch traced here: 45.1 us
  Pallas kernels  23.9 us (53%)
  starting transfers between devices  14.3 us (32%)
  waiting for transfers between devices  3.14 us (7%)
  local copies, waits for them, and re-layouts  1.87 us (4%)
  between operations  1.03 us (2%)
  other arithmetic  0.78 us (2%)
    pallas_call x7, Pallas kernels, call(): pl.pallas_call(kernel, in_specs=in_specs or [VMEM] * len(ins), out_specs=...  23.9 us
    ppermute x1, starting transfers between devices, local(): cr = lax.ppermute(jnp.stack([tr[:, 3], tr[:, 2]], axis=1), 'rows', near)  6.06 us
    ppermute x1, starting transfers between devices, local(): br = lax.ppermute(bs, 'rows', far)  3.65 us
    ppermute x1, waiting for transfers between devices, local(): br = lax.ppermute(bs, 'rows', far)  2.07 us
    unnamed x16, local copies, waits for them, and re-layouts  1.34 us
    ppermute x1, starting transfers between devices, local(): dr = lax.ppermute(ds, ('tm', 'rows'), diag)  1.29 us
    ppermute x1, starting transfers between devices, local(): tr = lax.ppermute(ts, 'tm', [(0, 1)])  1.29 us
    ppermute x1, starting transfers between devices, local(): pr = lax.ppermute(ps, 'tm', [(0, 1)])  1.29 us
  transfers between devices with their start and end apart: 6, of which 2 were waited for; matrix products, arithmetic and copies ran while one was open for 1% of the time, Pallas kernels for 46%

profile of v6, /device:TPU:99, one launch (start us, length us, event | category | flops | bytes accessed | tf_op | source)
XLA Modules:
  0.0 45.1 jit_solution(13819366754044075052)
XLA Ops:
  0.0 0.7 %pad_maximum_fusion.1.k_ref = f32[4,192]{1,0:T(4,128)S(1)} fusion(f32[1,192]{1,0:T(1,128)} %bitcast.5, f32[1,192]{1,0:T(1,128)} %bitcast.7, f32[1,192]{1,0:T(1,128)} %bitcast.9, f32[1,192]{1,0:T(1,128)} %bitcast.11), kind=kLoop, calls=%fused_computation.1 | loop fusion | flops 2304 | bytes 6144 | tf_op jit(solution)/shard_map/stack | solution.py:352
  0.7 0.0 copy-start.2
  0.8 1.3 %copy-done.2 = bf16[4,4,160,192]{3,2,1,0:T(8,128)(2,1)S(1)} copy-done((bf16[4,4,160,192]{3,2,1,0:T(8,128)(2,1)S(1)}, bf16[4,4,160,192]{3,2,1,0:T(8,128)(2,1)}, u32[]{:S(2)}) %copy-start.2) | copy-done | bytes 983064
  2.1 0.0 copy-start
  2.1 0.0 copy-start.1
  2.1 1.9 %prep.1 = (bf16[4,4,192,192]{3,2,1,0:T(8,128)(2,1)S(1)}, bf16[4,2,240,128]{3,2,1,0:T(8,128)(2,1)S(1)}, bf16[4,2,240,128]{3,2,1,0:T(8,128)(2,1)S(1)}, bf16[2,4,24...) custom-call(bf16[4,4,160,192]{3,2,1,0:T(8,128)(2,1)S(1)} %copy-done.2, f32[4,192]{1,0:T(4,128)S(1)} %pad_maximum_fusion.1.k_ref), custom_call_target="tpu_custom_call" | custom-call | flops 24000000000 | bytes 3000000 | tf_op jit(solution)/shard_map/prep/pallas_call | solution.py:332
  4.0 0.8 %collective-permute-start = (bf16[4,2,240,128]{3,2,1,0:T(8,128)(2,1)S(1)}, bf16[4,2,240,128]{3,2,1,0:T(8,128)(2,1)S(1)}, u32[]{:S(2)}, u32[]{:S(2)}) collective-permute-start(bf16[4,2,240,128]{3,2,1,0:T(8,128)(2,1)S(1)} %get-tuple-element.31), channel_id=1, source_target_pairs={{0,1},{1,0},{2,3},{3,2},{4,5},{5,4},{6,7},{7,6},{8,9},{9,8},{10,11... | collective-permute-start | bytes 1474568 | tf_op jit(solution)/shard_map/ppermute | solution.py:359
  4.8 3.7 %collective-permute-start.2 = (bf16[4,2,240,128]{3,2,1,0:T(8,128)(2,1)S(1)}, bf16[4,2,240,128]{3,2,1,0:T(8,128)(2,1)S(1)}, u32[]{:S(2)}, u32[]{:S(2)}) collective-permute-start(bf16[4,2,240,128]{3,2,1,0:T(8,128)(2,1)S(1)} %get-tuple-element.33), channel_id=1, source_target_pairs={{1,2},{3,4},{5,6},{7,8},{9,10},{11,12},{13,14},{15,16},{17,18},{19... | collective-permute-start | bytes 1474568 | tf_op jit(solution)/shard_map/ppermute | solution.py:360
  8.4 0.0 collective-permute-done.a_ref
  8.4 0.5 %slice.9 = bf16[1,1,1,1]{3,2,1,0:T(2,128)(2,1)} slice(bf16[4,2,240,128]{3,2,1,0:T(8,128)(2,1)S(1)} %collective-permute-done.a_ref), slice={[0:1], [0:1], [0:1], [0:1]} | slice | bytes 4 | tf_op jit(solution)/shard_map/slice | solution.py:368
  9.6 0.0 copy-done.4
  9.6 0.0 copy-done.5
  9.6 0.0 copy-done.6
  9.6 0.0 copy-done.7
  9.7 1.3 %collective-permute-start.3 = (bf16[2,2,240,128]{3,2,1,0:T(8,128)(2,1)S(1)}, bf16[2,2,240,128]{3,2,1,0:T(8,128)(2,1)S(1)}, u32[]{:S(2)}, u32[]{:S(2)}) collective-permute-start(bf16[2,2,240,128]{3,2,1,0:T(8,128)(2,1)S(1)} %get-tuple-element.46), channel_id=1, source_target_pairs={{1,66},{3,68},{5,70},{7,72},{9,74},{11,76},{13,78},{15,80},{17,82}... | collective-permute-start | bytes 737288 | tf_op jit(solution)/shard_map/ppermute | solution.py:370
  11.0 1.3 %collective-permute-start.1 = (bf16[2,4,240,128]{3,2,1,0:T(8,128)(2,1)S(1)}, bf16[2,4,240,128]{3,2,1,0:T(8,128)(2,1)S(1)}, u32[]{:S(2)}, u32[]{:S(2)}) collective-permute-start(bf16[2,4,240,128]{3,2,1,0:T(8,128)(2,1)S(1)} %get-tuple-element.32), channel_id=1, source_target_pairs={{0,64},{1,65},{2,66},{3,67},{4,68},{5,69},{6,70},{7,71},{8,72},{9,... | collective-permute-start | bytes 1474568 | tf_op jit(solution)/shard_map/ppermute | solution.py:362
  12.3 0.0 copy-done
  12.3 0.0 copy-done.1
  12.3 7.4 %early.1 = (bf16[2,4,160,192]{3,2,1,0:T(8,128)(2,1)S(1)}, f32[2,4,160,192]{3,2,1,0:T(8,128)S(1)}, f32[4,2,160,192]{3,2,1,0:T(8,128)S(1)}, bf16[2,2,240,128]{3,2,1,0:T(8,128)(2,1)S(1)}, f32[2,2,160,192]{3,2,1,0:T(8,128)S(1)}) custom-call(bf16[4,4,192,192]{3,2,1,0:T(8,128)(2,1)S(1)} %get-tuple-element.34.own_ref, ...), custom_call_target="tpu_custom_call" | custom-call | flops 10800000000 | bytes 3000000 | tf_op jit(solution)/shard_map/early/pallas_call | solution.py:332
  19.7 2.1 %collective-permute-done.2.bx_ref = bf16[4,2,240,128]{3,2,1,0:T(8,128)(2,1)S(1)} collective-permute-done((bf16[4,2,240,128]{3,2,1,0:T(8,128)(2,1)S(1)}, bf16[4,2,240,128]{3,2,1,0:T(8,128)(2,1)S(1)}, u32[]{:S(2)}, u32[]{:S(2)}) %collective-permute-start.2) | collective-permute-done | bytes 491552 | tf_op jit(solution)/shard_map/ppermute | solution.py:360
  21.8 1.6 %mid.1 = (bf16[2,2,160,192]{3,2,1,0:T(8,128)(2,1)S(1)}, bf16[2,4,240,128]{3,2,1,0:T(8,128)(2,1)S(1)}) custom-call(bf16[4,2,240,128]{3,2,1,0:T(8,128)(2,1)S(1)} %collective-permute-done.2.bx_ref, f32[4,2,160,192]{3,2,1,0:T(8,128)S(1)} %get-tuple-element.36.i_ref, bf16[2,2,240,128]{3,2,1,0:T(8,128)(2,1)S(1)} %get-tuple-element.38.pe_ref, ...), custom_call_target="tpu_custom_call" | custom-call | flops 1800000000 | bytes 3000000 | tf_op jit(solution)/shard_map/mid/pallas_call | solution.py:332
  23.3 1.3 %collective-permute-start.5 = (bf16[2,4,240,128]{3,2,1,0:T(8,128)(2,1)S(1)}, bf16[2,4,240,128]{3,2,1,0:T(8,128)(2,1)S(1)}, u32[]{:S(2)}, u32[]{:S(2)}) collective-permute-start(bf16[2,4,240,128]{3,2,1,0:T(8,128)(2,1)S(1)} %get-tuple-element.53), channel_id=1, source_target_pairs={{0,64},{1,65},{2,66},{3,67},{4,68},{5,69},{6,70},{7,71},{8,72},{9,... | collective-permute-start | bytes 1474568 | tf_op jit(solution)/shard_map/ppermute | solution.py:376
  24.6 0.0 copy-done.3
  24.6 3.1 %wait.1 = (f32[2,2,160,192]{3,2,1,0:T(8,128)S(1)}, f32[4,4,160,192]{3,2,1,0:T(8,128)S(1)}) custom-call(bf16[4,2,240,128]{3,2,1,0:T(8,128)(2,1)S(1)} %collective-permute-done.2.bx_ref, f32[4,2,160,192]{3,2,1,0:T(8,128)S(1)} %get-tuple-element.36.i_ref, bf16[2,4,160,192]{3,2,1,0:T(8,128)(2,1)S(1)} %get-tuple-element.37.re_ref, ...), custom_call_target="tpu_custom_call" | custom-call | flops 12000000000 | bytes 3000000 | tf_op jit(solution)/shard_map/wait/pallas_call | solution.py:332
  27.8 1.1 %collective-permute-done.1.t_ref = bf16[2,4,240,128]{3,2,1,0:T(8,128)(2,1)S(1)} collective-permute-done((bf16[2,4,240,128]{3,2,1,0:T(8,128)(2,1)S(1)}, bf16[2,4,240,128]{3,2,1,0:T(8,128)(2,1)S(1)}, u32[]{:S(2)}, u32[]{:S(2)}) %collective-permute-start.1) | collective-permute-done | bytes 491552 | tf_op jit(solution)/shard_map/ppermute | solution.py:362
  28.9 6.1 %collective-permute-start.4 = (bf16[2,2,240,128]{3,2,1,0:T(8,128)(2,1)S(1)}, bf16[2,2,240,128]{3,2,1,0:T(8,128)(2,1)S(1)}, u32[]{:S(2)}, u32[]{:S(2)}) collective-permute-start(bf16[2,2,240,128]{3,2,1,0:T(8,128)(2,1)S(1)} %pad_maximum_fusion), channel_id=1, source_target_pairs={{0,1},{1,0},{2,3},{3,2},{4,5},{5,4},{6,7},{7,6},{8,9},{9,8},{10,11... | collective-permute-start | bytes 737288 | tf_op jit(solution)/shard_map/ppermute | solution.py:383
  35.0 0.0 collective-permute-done.3.d_ref
  35.0 2.3 %late.1.r_ref = bf16[2,4,160,192]{3,2,1,0:T(8,128)(2,1)S(1)} custom-call(bf16[2,4,240,128]{3,2,1,0:T(8,128)(2,1)S(1)} %collective-permute-done.1.t_ref, bf16[2,2,240,128]{3,2,1,0:T(8,128)(2,1)S(1)} %collective-permute-done.3.d_ref, f32[2,4,160,192]{3,2,1,0:T(8,128)S(1)} %get-tuple-element.47.o_ref, f32[2,2,160,192]{3,2,1,0:T(8,128)S(1)} %get-tuple-element.48.j_ref, ...), custom_call_target="tpu_custom_call" | custom-call | flops 600000000 | bytes 3000000 | tf_op jit(solution)/shard_map/late/pallas_call | solution.py:332
  37.3 0.0 collective-permute-done.4.c_ref
  37.3 6.4 %last.1 = (bf16[4,4,160,192]{3,2,1,0:T(8,128)(2,1)}, f32[2,4,160,192]{3,2,1,0:T(8,128)S(1)}) custom-call(bf16[2,4,240,128]{3,2,1,0:T(8,128)(2,1)S(1)} %collective-permute-done.1.t_ref, bf16[2,2,240,128]{3,2,1,0:T(8,128)(2,1)S(1)} %collective-permute-done.4.c_ref, f32[2,4,160,192]{3,2,1,0:T(8,128)S(1)} %get-tuple-element.47.o_ref, ...), custom_call_target="tpu_custom_call" | custom-call | flops 600000000 | bytes 3000000 | tf_op jit(solution)/shard_map/last/pallas_call | solution.py:332
  43.7 0.0 collective-permute-done.5.p_ref
  43.7 1.2 %add.11 = bf16[4,4,160,192]{3,2,1,0:T(8,128)(2,1)} custom-call(f32[2,4,160,192]{3,2,1,0:T(8,128)S(1)} %get-tuple-element.52.acc_ref, bf16[2,4,240,128]{3,2,1,0:T(8,128)(2,1)S(1)} %collective-permute-done.5.p_ref, bf16[4,4,160,192]{3,2,1,0:T(8,128)(2,1)} %get-tuple-element.54.full_ref), custom_call_target="tpu_custom_call", output_to_operand_aliasing={{}: (2, {})} | custom-call | flops 600000000 | bytes 3000000 | tf_op jit(solution)/shard_map/add/pallas_call | solution.py:332
  (8 shorter events, 0.1 us)
Async XLA Ops:
  0.7 1.3 %copy-start.2 = (bf16[4,4,160,192]{3,2,1,0:T(8,128)(2,1)S(1)}, bf16[4,4,160,192]{3,2,1,0:T(8,128)(2,1)}, u32[]{:S(2)}) copy-start(bf16[4,4,160,192]{3,2,1,0:T(8,128)(2,1)} %in_ref.1) | copy-start | bytes 2949124
  2.1 7.5 %copy-start.4 = (f32[192]{0:T(256)S(1)}, f32[192]{0:T(256)}, u32[]{:S(2)}) copy-start(f32[192]{0:T(256)} %param.13) | copy-start | bytes 2308
  2.1 7.5 %copy-start.5 = (f32[192]{0:T(256)S(1)}, f32[192]{0:T(256)}, u32[]{:S(2)}) copy-start(f32[192]{0:T(256)} %param.11) | copy-start | bytes 2308
  2.1 7.6 %copy-start.6 = (f32[192]{0:T(256)S(1)}, f32[192]{0:T(256)}, u32[]{:S(2)}) copy-start(f32[192]{0:T(256)} %param.10) | copy-start | bytes 2308
  2.1 7.6 %copy-start.7 = (f32[192]{0:T(256)S(1)}, f32[192]{0:T(256)}, u32[]{:S(2)}) copy-start(f32[192]{0:T(256)} %param.8) | copy-start | bytes 2308
  2.1 10.2 %copy-start = (bf16[3,3,3,192,192]{4,3,2,1,0:T(8,128)(2,1)S(1)}, bf16[3,3,3,192,192]{4,3,2,1,0:T(8,128)(2,1)}, u32[]{:S(2)}) copy-start(bf16[3,3,3,192,192]{4,3,2,1,0:T(8,128)(2,1)} %w1_ref.9) | copy-start | bytes 5971972
  2.1 10.2 %copy-start.1 = (bf16[3,3,3,192,192]{4,3,2,1,0:T(8,128)(2,1)S(1)}, bf16[3,3,3,192,192]{4,3,2,1,0:T(8,128)(2,1)}, u32[]{:S(2)}) copy-start(bf16[3,3,3,192,192]{4,3,2,1,0:T(8,128)(2,1)} %w2_ref.7) | copy-start | bytes 5971972
  4.0 4.4 %collective-permute-start = (bf16[4,2,240,128]{3,2,1,0:T(8,128)(2,1)S(1)}, bf16[4,2,240,128]{3,2,1,0:T(8,128)(2,1)S(1)}, u32[]{:S(2)}, u32[]{:S(2)}) collective-permute-start(bf16[4,2,240,128]{3,2,1,0:T(8,128)(2,1)S(1)} %get-tuple-element.31), channel_id=1, source_target_pairs={{0,1},{1,0},{2,3},{3,2},{4,5},{5,4},{6,7},{7,6},{8,9},{9,8},{10,11... | collective-permute-start | bytes 1474568 | tf_op jit(solution)/shard_map/ppermute | solution.py:359
  4.8 17.0 %collective-permute-start.2 = (bf16[4,2,240,128]{3,2,1,0:T(8,128)(2,1)S(1)}, bf16[4,2,240,128]{3,2,1,0:T(8,128)(2,1)S(1)}, u32[]{:S(2)}, u32[]{:S(2)}) collective-permute-start(bf16[4,2,240,128]{3,2,1,0:T(8,128)(2,1)S(1)} %get-tuple-element.33), channel_id=1, source_target_pairs={{1,2},{3,4},{5,6},{7,8},{9,10},{11,12},{13,14},{15,16},{17,18},{19... | collective-permute-start | bytes 1474568 | tf_op jit(solution)/shard_map/ppermute | solution.py:360
  9.7 25.3 %collective-permute-start.3 = (bf16[2,2,240,128]{3,2,1,0:T(8,128)(2,1)S(1)}, bf16[2,2,240,128]{3,2,1,0:T(8,128)(2,1)S(1)}, u32[]{:S(2)}, u32[]{:S(2)}) collective-permute-start(bf16[2,2,240,128]{3,2,1,0:T(8,128)(2,1)S(1)} %get-tuple-element.46), channel_id=1, source_target_pairs={{1,66},{3,68},{5,70},{7,72},{9,74},{11,76},{13,78},{15,80},{17,82}... | collective-permute-start | bytes 737288 | tf_op jit(solution)/shard_map/ppermute | solution.py:370
  11.0 17.9 %collective-permute-start.1 = (bf16[2,4,240,128]{3,2,1,0:T(8,128)(2,1)S(1)}, bf16[2,4,240,128]{3,2,1,0:T(8,128)(2,1)S(1)}, u32[]{:S(2)}, u32[]{:S(2)}) collective-permute-start(bf16[2,4,240,128]{3,2,1,0:T(8,128)(2,1)S(1)} %get-tuple-element.32), channel_id=1, source_target_pairs={{0,64},{1,65},{2,66},{3,67},{4,68},{5,69},{6,70},{7,71},{8,72},{9,... | collective-permute-start | bytes 1474568 | tf_op jit(solution)/shard_map/ppermute | solution.py:362
  21.7 2.9 %copy-start.3 = (bf16[4,4,160,192]{3,2,1,0:T(8,128)(2,1)S(1)}, bf16[4,4,160,192]{3,2,1,0:T(8,128)(2,1)}, u32[]{:S(2)}) copy-start(bf16[4,4,160,192]{3,2,1,0:T(8,128)(2,1)} %in_ref.1) | copy-start | bytes 2949124
  23.3 20.4 %collective-permute-start.5 = (bf16[2,4,240,128]{3,2,1,0:T(8,128)(2,1)S(1)}, bf16[2,4,240,128]{3,2,1,0:T(8,128)(2,1)S(1)}, u32[]{:S(2)}, u32[]{:S(2)}) collective-permute-start(bf16[2,4,240,128]{3,2,1,0:T(8,128)(2,1)S(1)} %get-tuple-element.53), channel_id=1, source_target_pairs={{0,64},{1,65},{2,66},{3,67},{4,68},{5,69},{6,70},{7,71},{8,72},{9,... | collective-permute-start | bytes 1474568 | tf_op jit(solution)/shard_map/ppermute | solution.py:376
  28.9 8.4 %collective-permute-start.4 = (bf16[2,2,240,128]{3,2,1,0:T(8,128)(2,1)S(1)}, bf16[2,2,240,128]{3,2,1,0:T(8,128)(2,1)S(1)}, u32[]{:S(2)}, u32[]{:S(2)}) collective-permute-start(bf16[2,2,240,128]{3,2,1,0:T(8,128)(2,1)S(1)} %pad_maximum_fusion), channel_id=1, source_target_pairs={{0,1},{1,0},{2,3},{3,2},{4,5},{5,4},{6,7},{7,6},{8,9},{9,8},{10,11... | collective-permute-start | bytes 737288 | tf_op jit(solution)/shard_map/ppermute | solution.py:383
